TPU v7x, 32 devices: a whole 2x2x4 slice. The times are simulated.
32 devices in a mesh: grp: 4 (over y, x), wide: 8 (over z, core).
Axes of the slice: x: 2, y: 2, z: 4, core: 2. Of those that a mesh axis runs over, the one named last changes fastest.
Arguments:
- tiles: bfloat16 [1536, 256, 256], P(('grp', 'wide')), may hold values from -0.59765625 to 0.59765625
- contraction: int32 [1536], P(('grp', 'wide')), may hold values from 0 to 15
- row_tile: int32 [1536], P(('grp', 'wide')), may hold values from 0 to 31, as said below
- owner_map: int32 [32], replicated, may hold values from 0 to 31, as said below
- panel: bfloat16 [4096, 768], P('grp'), may hold values from -0.5390625 to 0.5390625
Outputs:
- column_block: float32 [8192, 768], P('wide')
Inputs may be any that keep to these rules, and one draw needn't show every extreme that they name: `row_tile`: every row tile's owner is owner_map // 4; among the 48 contributions of one device at most 16 have row tiles of one owner, and on every device some owner gets exactly 16. `owner_map`: A permutation of the row tiles.
All inputs are finite; a program needn't handle non-finite values.
Results may differ from a plain program's by a relative error of at most 0.0003.
Values may be sent and summed in bfloat16 or wider, within the bound.
No kernel may reach another device: no remote copies, remote signals or barrier semaphores. Data moves between devices by JAX's collectives and lax.ppermute only.
A program may use at most 192 MiB of HBM per device.

v0:
```python
import functools
import math

import jax
import jax.numpy as jnp
from jax import lax
from jax.experimental import pallas as pl
from jax.experimental.pallas import tpu as pltpu
from jax.sharding import PartitionSpec as P

MIB = 1024 * 1024
CODE_ROWS = 16
CODE_STEPS = 256.0
TOP = 32000.0
CHUNK = 256
UNROLL = 8
LOG2 = math.log(2.0)


def place_slots(row_ids, owner_map, out_dev):
    table_ids = jnp.arange(owner_map.shape[0], dtype=jnp.int32)
    position = jnp.sum(jnp.where(row_ids[..., None] == table_ids, owner_map, 0), axis=-1)
    target = position // out_dev
    serial = jnp.arange(row_ids.shape[-1], dtype=jnp.int32)
    earlier = (target[..., :, None] == target[..., None, :]) & (serial[:, None] > serial[None, :])
    ranking = jnp.sum(earlier.astype(jnp.int32), axis=-1)
    return (position % out_dev, target, ranking)


def add_products(summed, arrived, slot_labels, panel_tiles):
    slot_count = arrived.shape[0]
    block_rows = math.gcd(slot_count, 32)
    out_dev = summed.shape[0]
    local_ids = jnp.arange(out_dev, dtype=jnp.int32)

    def one_block(which_block, running, source_tiles, source_labels):
        part_tiles = lax.dynamic_slice_in_dim(source_tiles, which_block * block_rows, block_rows, 0)
        part_labels = lax.dynamic_slice_in_dim(
            source_labels, which_block * block_rows, block_rows, 0
        )
        chosen = jnp.take(panel_tiles, part_labels[:, 1], axis=0)
        products = jnp.einsum(
            "sab,sbc->sac", part_tiles, chosen, preferred_element_type=jnp.float32
        )
        row_hits = (part_labels[:, 0][:, None] == local_ids[None, :]).astype(jnp.float32)
        return running + jnp.einsum(
            "sr,sac->rac", row_hits, products, precision=lax.Precision.HIGHEST
        )

    return lax.fori_loop(
        0,
        slot_count // block_rows,
        lambda which_block, running: one_block(which_block, running, arrived, slot_labels),
        summed,
    )


def slots_plan(tiles, contraction, row_tile, owner_map, panel):
    wide_count = lax.axis_size("wide")
    tile_dev = tiles.shape[0]
    tile_side = tiles.shape[1]
    out_dev = owner_map.shape[0] // wide_count
    most_slots = tile_dev * 8 // (3 * wide_count)
    slot_total = wide_count * most_slots
    local_row, target, ranking = place_slots(row_tile, owner_map, out_dev)
    slot_index = target * most_slots + ranking
    outgoing = jnp.zeros((slot_total, tile_side, tile_side), tiles.dtype).at[slot_index].set(tiles)
    all_rows, all_contraction = (
        lax.all_gather(row_tile, "wide", axis=0, tiled=True),
        lax.all_gather(contraction, "wide", axis=0, tiled=True),
    )
    all_rows = all_rows.reshape(wide_count, tile_dev)
    all_contraction = all_contraction.reshape(wide_count, tile_dev)
    source_local, source_target, source_rank = place_slots(all_rows, owner_map, out_dev)
    source_ids = jnp.arange(wide_count, dtype=jnp.int32)
    mine = source_target == lax.axis_index("wide")
    arrive_index = jnp.where(mine, source_ids[:, None] * most_slots + source_rank, slot_total)
    label_pairs = jnp.stack([source_local, all_contraction], axis=-1).reshape(
        wide_count * tile_dev, 2
    )
    vacant_label = jnp.stack(
        [jnp.full((slot_total,), out_dev, jnp.int32), jnp.zeros((slot_total,), jnp.int32)], axis=1
    )
    arrived_labels = vacant_label.at[arrive_index.reshape(-1)].set(label_pairs, mode="drop")
    gathered = lax.all_gather(panel, "grp", axis=0, tiled=True)
    panel_tiles = gathered.reshape(gathered.shape[0] // tile_side, tile_side, gathered.shape[1])
    summed = jnp.zeros((out_dev, tile_side, gathered.shape[1]), jnp.float32)
    arrived = lax.all_to_all(outgoing, "wide", split_axis=0, concat_axis=0, tiled=True)
    summed = add_products(summed, arrived, arrived_labels, panel_tiles)
    summed = lax.psum(summed, "grp")
    return summed.reshape(out_dev * tile_side, gathered.shape[1])


def encode(value):
    largest = jnp.max(jnp.abs(value), axis=0, keepdims=True)
    code = jnp.ceil(jnp.log(jnp.maximum(largest, 1e-30)) * (CODE_STEPS / LOG2))
    scale = jnp.exp(code * (-LOG2 / CODE_STEPS)) * TOP
    whole = jnp.round(value * scale).astype(jnp.int32).astype(jnp.int16)
    return whole, code.astype(jnp.int32)


def put_encoded(ref, value):
    side = value.shape[0]
    whole, code = encode(value)
    ref[pl.ds(0, side), :] = whole
    ref[pl.ds(side, CODE_ROWS), :] = jnp.broadcast_to(
        code, (CODE_ROWS, code.shape[1])
    ).astype(jnp.int16)


def get_decoded(ref, side):
    code = ref[pl.ds(side, CODE_ROWS), :].astype(jnp.int32).astype(jnp.float32)[:1]
    scale = jnp.exp(code * (LOG2 / CODE_STEPS)) * (1.0 / TOP)
    return ref[pl.ds(0, side), :].astype(jnp.int32).astype(jnp.float32) * scale


def hold_kernel(order_ref, own_tiles, sib_tiles, out, sems):
    count = own_tiles.shape[0]
    copies = [
        pltpu.make_async_copy(tiles, out.at[pl.ds(i * count, count)], sems.at[i])
        for i, tiles in enumerate((own_tiles, sib_tiles))
    ]
    for copy in copies:
        copy.start()
    for copy in copies:
        copy.wait()


def join_kernel(order_ref, *refs):
    *parts, out = refs
    rows = parts[0].shape[0]
    for i, part in enumerate(parts):
        out[pl.ds(i * rows, rows), :] = part[...]


def products_kernel(
    fill, rounds_ref, source_ref, slot_ref, label_ref, tiles, own_panel, *refs
):
    parts = refs[: 1 + max(which for which, _, _ in fill)]
    *outs, stack, acc = refs[len(parts) :]
    side = tiles.shape[1]
    for t in range(own_panel.shape[0] // side):
        stack[t] = own_panel[pl.ds(t * side, side), :]
    for which, t, at in fill:
        stack[at] = parts[which][pl.ds(t * side, side), :]

    @pl.loop(0, acc.shape[0])
    def _(i):
        acc[i] = jnp.zeros(acc.shape[1:], jnp.float32)

    @pl.loop(0, rounds_ref[0])
    def _(i):
        found = [
            jnp.dot(
                tiles[source_ref[i * UNROLL + u]],
                stack[label_ref[i * UNROLL + u]],
                preferred_element_type=jnp.float32,
            )
            for u in range(UNROLL)
        ]
        for u in range(UNROLL):
            acc[slot_ref[i * UNROLL + u]] += found[u]

    sent = 0
    for out in outs:

        @pl.loop(0, out.shape[0])
        def _(i, out=out, sent=sent):
            if out.dtype == jnp.int16:
                put_encoded(out.at[i], acc[sent + i])
            else:
                out[i] = acc[sent + i]

        sent += out.shape[0]


def plane_kernel(bits_ref, recv_a, recv_b, kept, send_a, send_b, keep):
    side, half = kept.shape[1], send_a.shape[0]
    for first, bit, recv, send in ((0, bits_ref[1], recv_a, send_a), (1, bits_ref[0], recv_b, send_b)):

        @pl.loop(0, half)
        def _(i, first=first, bit=bit, recv=recv, send=send):
            other, mine = 2 * i + 1 - bit, 2 * i + bit
            base = first * 2 * half
            put_encoded(send.at[i], kept[base + other] + get_decoded(recv.at[other], side))
            keep[first * half + i] = kept[base + mine] + get_decoded(recv.at[mine], side)


def owner_kernel(bits_ref, recv_a, recv_b, kept, send, keep):
    side, half = kept.shape[1], send.shape[0]
    odd = bits_ref[2]

    @pl.loop(0, half)
    def _(i):
        value_a = kept[i] + get_decoded(recv_a.at[i], side)
        value_b = kept[half + i] + get_decoded(recv_b.at[i], side)
        put_encoded(send.at[i], jnp.where(odd == 1, value_a, value_b))
        keep[i] = jnp.where(odd == 1, value_b, value_a)


def line_kernel(bits_ref, recv, kept, send, keep):
    side, half = kept.shape[1], send.shape[0]
    bit = bits_ref[3]

    @pl.loop(0, half)
    def _(i):
        other, mine = (1 - bit) * half + i, bit * half + i
        put_encoded(send.at[i], kept[other] + get_decoded(recv.at[other], side))
        keep[i] = kept[mine] + get_decoded(recv.at[mine], side)


def rows_kernel(bits_ref, recv, kept, send_1, send_2, send_3, keep):
    side = kept.shape[1]
    row = bits_ref[1] * 2 + bits_ref[0]
    for d, send in enumerate((send_1, send_2, send_3), 1):
        put_encoded(send, kept[row ^ d] + get_decoded(recv.at[row ^ d], side))
    keep[...] = kept[row] + get_decoded(recv.at[row], side)


def finish_kernel(bits_ref, *refs):
    *recvs, kept, out = refs
    value = kept[...]
    for recv in recvs:
        value += get_decoded(recv, kept.shape[0])
    put_encoded(out, value)


def spread_kernel(bits_ref, *refs):
    blocks, out = refs[:4], refs[-1]
    side = blocks[0].shape[0] - CODE_ROWS
    row = bits_ref[1] * 2 + bits_ref[0]
    for d, block in enumerate(blocks):
        at = pl.multiple_of((row ^ d) * side, side)
        out[pl.ds(at, side), :] = get_decoded(block, side)


def in_vmem(count):
    return [pl.BlockSpec(memory_space=pltpu.VMEM)] * count


def in_smem(count):
    return [pl.BlockSpec(memory_space=pltpu.SMEM)] * count


def in_any(count):
    return [pl.BlockSpec(memory_space=pl.ANY)] * count


def shape(dims, kind):
    return jax.ShapeDtypeStruct(dims, kind)


def params(mib):
    return pltpu.CompilerParams(vmem_limit_bytes=mib * MIB)


def cost(flops, moved):
    return pl.CostEstimate(flops=flops, bytes_accessed=moved, transcendentals=0)


def compact(match, values):
    count = -(-match.shape[0] // UNROLL) * UNROLL
    rank = jnp.cumsum(match.astype(jnp.int32)) - 1
    hit = match & (rank == jnp.arange(count, dtype=jnp.int32)[:, None])
    return [jnp.sum(jnp.where(hit, v, 0), axis=-1) for v in values]


def sums_plan(tiles, contraction, row_tile, owner_map, panel):
    wide_count = lax.axis_size("wide")
    tile_dev, side = tiles.shape[0], tiles.shape[1]
    out_dev = owner_map.shape[0] // wide_count
    rows, columns = panel.shape
    shard = rows // side
    chunks = columns // CHUNK
    sums = owner_map.shape[0] // 2
    g, w = lax.axis_index("grp"), lax.axis_index("wide")
    core = w % 2

    def to_core(v):
        return lax.ppermute(v, "wide", [(i, i ^ 1) for i in range(wide_count)])

    def to_grp(v, d):
        return lax.ppermute(v, "grp", [(i, i ^ d) for i in range(4)])

    def to_line(v, b):
        return lax.ppermute(v, "wide", [(i, i ^ (2 << b)) for i in range(wide_count)])

    x, y, z = g % 2, g // 2, w // 2
    bits = jnp.stack([x, y, z % 2, z // 2]).astype(jnp.int32)

    labels = jnp.stack([row_tile, contraction])
    both = jnp.stack([labels, to_core(labels)])
    sib_tiles = to_core(tiles)

    def own_half(source, j):
        return lax.dynamic_slice(source, (core * (rows // 2), j * CHUNK), (rows // 2, CHUNK))

    mines = [own_half(panel, j) for j in range(chunks)]
    ways = [None, (1, 2), (2, 1)]
    firsts = [None] + [to_grp(mines[j], ways[j][0]) for j in range(1, chunks)]
    mine, both = lax.optimization_barrier((mines[0], both))
    near = [to_grp(mine, 1), to_grp(mine, 2), to_grp(mines[0], 3)]

    table_ids = jnp.arange(owner_map.shape[0], dtype=jnp.int32)
    position = jnp.sum(jnp.where(both[:, 0, :, None] == table_ids, owner_map, 0), axis=-1)
    owner, local = position // out_dev, position % out_dev
    to_z, odd = owner // 4, (owner // 2) % 2
    bit_x, bit_y = local % 2, local // 2
    first = jnp.where(odd == 1, bit_y == y, bit_x == x)
    second = jnp.where(odd == 1, bit_x, bit_y)
    in_plane = jnp.where(first, sums // 2, 0) + odd * (sums // 4) + 2 * to_z + second
    in_line = jnp.where(odd == z % 2, sums // 2, 0) + to_z * out_dev + local
    k = both[:, 1]
    apart, inner = (k // shard) ^ g, k % shard
    half = shard // 2
    crossed = jnp.where(inner // half == core, 0, half) + inner % half
    label = jnp.where(apart == 0, inner, apart * shard + crossed)
    match = (owner % 2 == core).reshape(-1)
    entries = [v.reshape(-1) for v in (in_plane, in_line, label)]
    serial = jnp.arange(match.shape[0], dtype=jnp.int32)
    source, in_plane, in_line, label = compact(match, [serial, *entries])
    found = jnp.sum(match.astype(jnp.int32))
    rounds = ((found + UNROLL - 1) // UNROLL)[None]
    beyond = jnp.arange(source.shape[0], dtype=jnp.int32) >= found
    in_plane = jnp.where(beyond, sums, in_plane)
    in_line = jnp.where(beyond, sums, in_line)

    half, quarter = sums // 2, sums // 4
    coded = shape((side + CODE_ROWS, CHUNK), jnp.int16)
    plain = shape((side, CHUNK), jnp.float32)

    def stack_of(count, one):
        return shape((count, *one.shape), one.dtype)

    last = None

    def in_order(small):
        return small if last is None else lax.optimization_barrier((small, last))[0]

    def call(body, name, outs, *args):
        nonlocal last
        done = pl.pallas_call(
            body,
            in_specs=in_smem(1) + in_vmem(len(args)),
            out_specs=in_vmem(len(outs)),
            out_shape=outs,
            compiler_params=params(16),
            cost_estimate=cost(0, sum(math.prod(a.shape) * a.dtype.itemsize for a in args)),
            name=name,
        )(in_order(bits), *args)
        last = done[0]
        return done

    first, *lists = lax.optimization_barrier((bits, rounds, source, in_plane, in_line, label))
    rounds, source, in_plane, in_line, label = lists
    held = None

    def hold():
        nonlocal held, last
        held = last = pl.pallas_call(
            hold_kernel,
            in_specs=in_smem(1) + in_any(2),
            out_specs=in_vmem(1)[0],
            out_shape=pltpu.VMEM((2 * tile_dev, side, side), tiles.dtype),
            scratch_shapes=[pltpu.SemaphoreType.DMA((2,))],
            compiler_params=params(8),
            cost_estimate=cost(0, 4 * tile_dev * side * side),
            name="hold",
        )(
            in_order(first),
            *[pltpu.with_memory_space_constraint(v, pltpu.HBM) for v in (tiles, sib_tiles)],
        )

    def places(operand, tiles_of, first):
        return [
            (operand, t, d * shard + first + i % part)
            for i, (t, d) in enumerate((t, d) for d, ts in tiles_of for t in ts)
        ]

    part = shard // 2

    def join(j):
        (joined,) = call(join_kernel, "join", [shape((3 * rows // 2, CHUNK), panel.dtype)], *near)
        tiles_of = [(d, range((d - 1) * part, d * part)) for d in (1, 2, 3)]
        fill = places(0, tiles_of, 0) + places(1, tiles_of, part)
        return fill, [joined, to_core(joined)]

    def pair(j):
        way, other = ways[j]
        (joined,) = call(
            join_kernel, "join", [shape((rows, CHUNK), panel.dtype)], mines[j], firsts[j]
        )
        second = to_grp(joined, other)
        in_first = [(way, range(part, 2 * part))]
        in_second = [(other, range(part)), (way ^ other, range(part, 2 * part))]
        fill = (
            places(0, in_first, 0)
            + places(1, in_first, part)
            + places(2, in_second, 0)
            + places(3, in_second, part)
        )
        return fill, [joined, to_core(joined), second, to_core(second)]

    def products(j, slot, outs, fill, parts):
        nonlocal last
        done = pl.pallas_call(
            functools.partial(products_kernel, tuple(fill)),
            grid=(1,),
            in_specs=in_smem(4)
            + in_vmem(1)
            + [pl.BlockSpec((rows, CHUNK), lambda i: (0, j))]
            + in_vmem(len(parts)),
            out_specs=in_vmem(len(outs)),
            out_shape=outs,
            scratch_shapes=[
                pltpu.VMEM((4 * shard, side, CHUNK), panel.dtype),
                pltpu.VMEM((sums + 1, side, CHUNK), jnp.float32),
            ],
            compiler_params=params(24),
            cost_estimate=cost(0, 4 * tile_dev * side * side),
            name="products",
        )(in_order(rounds), source, slot, label, held, panel, *parts)
        last = done[0]
        return done

    def spread(j, done, result):
        nonlocal last
        blocks = [done] + [to_grp(done, d) for d in (1, 2, 3)]
        earlier = [] if result is None else [result]
        last = pl.pallas_call(
            spread_kernel,
            grid=(1,),
            in_specs=in_smem(1) + in_vmem(4) + in_any(len(earlier)),
            out_specs=pl.BlockSpec((out_dev * side, CHUNK), lambda i: (0, j)),
            out_shape=shape((out_dev * side, columns), jnp.float32),
            input_output_aliases={5: 0} if earlier else {},
            compiler_params=params(16),
            cost_estimate=cost(0, 6 * out_dev * side * CHUNK),
            name="spread",
        )(in_order(bits), *blocks, *earlier)
        return last

    def line_first(j):
        panel_of = join(j)
        yield
        send, keep = products(
            j, in_line, [stack_of(half, coded), stack_of(half, plain)], *panel_of
        )
        yield
        recv = to_line(send, 0)
        send, keep = call(
            line_kernel, "line", [stack_of(quarter, coded), stack_of(quarter, plain)], recv, keep
        )
        yield
        *sends, keep = call(rows_kernel, "rows", [coded] * 3 + [plain], to_line(send, 1), keep)
        yield
        recvs = [to_grp(v, d) for d, v in enumerate(sends, 1)]
        (done,) = call(finish_kernel, "finish", [coded], *recvs, keep)
        yield
        yield done

    def plane_first(j):
        panel_of = pair(j)
        yield
        send_a, send_b, keep = products(
            j, in_plane, [stack_of(quarter, coded)] * 2 + [stack_of(half, plain)], *panel_of
        )
        yield
        send_a, send_b, keep = call(
            plane_kernel,
            "plane",
            [stack_of(quarter // 2, coded)] * 2 + [stack_of(quarter, plain)],
            to_grp(send_a, 1),
            to_grp(send_b, 2),
            keep,
        )
        yield
        send, keep = call(
            owner_kernel,
            "owner",
            [stack_of(quarter // 2, coded), stack_of(quarter // 2, plain)],
            to_grp(send_a, 2),
            to_grp(send_b, 1),
            keep,
        )
        yield
        send, keep = call(
            line_kernel,
            "line",
            [stack_of(quarter // 4, coded), stack_of(quarter // 4, plain)],
            to_line(send, 0),
            keep,
        )
        yield
        recv = to_line(send, 1)
        (done,) = call(finish_kernel, "finish", [coded], recv[0], keep[0])
        yield
        yield done

    steps, lengths = [0] * chunks, [5] + [6] * (chunks - 1)
    work = [(line_first if j == 0 else plane_first)(j) for j in range(chunks)]
    dones, result = {}, None
    for j in (1, 2, None, 0, 0, 1, 2, 0, 1, 2, 1, 0, 2, 1, 0, 2, 1, 0, 2, 1, 2):
        if j is None:
            hold()
        elif j in dones:
            result = spread(j, dones[j], result)
        else:
            next(work[j])
            steps[j] += 1
            if steps[j] == lengths[j]:
                dones[j] = next(work[j])
    return result


def per_device(tiles, contraction, row_tile, owner_map, panel):
    dense = owner_map.shape[0] <= tiles.shape[0]
    wide_count = lax.axis_size("wide")
    fits = lax.axis_size("grp") == 4 and wide_count >= 4 and wide_count & (wide_count - 1) == 0
    out_dev = owner_map.shape[0] // wide_count
    if dense and fits and wide_count == 8 and out_dev == 4 and panel.shape[1] == 3 * CHUNK:
        return sums_plan(tiles, contraction, row_tile, owner_map, panel)
    return slots_plan(tiles, contraction, row_tile, owner_map, panel)


def solution(mesh):
    return jax.shard_map(
        per_device,
        mesh=mesh,
        in_specs=(
            P(("grp", "wide"), None, None),
            P(("grp", "wide")),
            P(("grp", "wide")),
            P(),
            P("grp", None),
        ),
        out_specs=P("wide", None),
        check_vma=False,
    )
```

profile of v0, /device:TPU:0, one launch (start us, length us, event | category | flops | bytes accessed | tf_op | source)
XLA Modules:
  0.0 124.6 jit_solution(5977702983741519002)
XLA Ops:
  2.4 3.0 %collective-permute-start.2 = (bf16[512,256]{1,0:T(8,128)(2,1)S(1)}, bf16[512,256]{1,0:T(8,128)(2,1)S(1)}, u32[]{:S(2)}, u32[]{:S(2)}) collective-permute-start(bf16[512,256]{1,0:T(8,128)(2,1)S(1)} %get-tuple-element.125.refs_0_), channel_id=1, source_target_pairs={{0,16},{8,24},{16,0},{24,8},{1,17},{9,25},{17,1},{25,9},{2,18},{10... | collective-permute-start | bytes 786440 | tf_op jit(solution)/shard_map/ppermute | solution.py:283
  7.0 3.1 %collective-permute-done = s32[2,48]{1,0:T(2,128)S(1)} collective-permute-done((s32[2,48]{1,0:T(2,128)S(1)}, s32[2,48]{1,0:T(2,128)S(1)}, u32[]{:S(2)}, u32[]{:S(2)}) %collective-permute-start) | collective-permute-done | bytes 416 | tf_op jit(solution)/shard_map/ppermute | solution.py:280
  11.2 2.6 %collective-permute-start.5 = (bf16[512,256]{1,0:T(8,128)(2,1)S(1)}, bf16[512,256]{1,0:T(8,128)(2,1)S(1)}, u32[]{:S(2)}, u32[]{:S(2)}) collective-permute-start(bf16[512,256]{1,0:T(8,128)(2,1)S(1)} %get-tuple-element.67), channel_id=1, source_target_pairs={{0,16},{8,24},{16,0},{24,8},{1,17},{9,25},{17,1},{25,9},{2,18},{10... | collective-permute-start | bytes 786440 | tf_op jit(solution)/shard_map/ppermute | solution.py:283
  19.3 5.2 %hold.1.tiles = bf16[96,256,256]{2,1,0:T(8,128)(2,1)S(1)} custom-call(s32[4]{0:T(128)S(1)} %pad_add_fusion.2.order_ref.bits_ref, bf16[48,256,256]{2,1,0:T(8,128)(2,1)} %own_tiles.1, bf16[48,256,256]{2,1,0:T(8,128)(2,1)} %collective-permute-done.3.sib_tiles), custom_call_target="tpu_custom_call" | custom-call | bytes 12582912 | tf_op jit(solution)/shard_map/hold/pallas_call | solution.py:360
  28.3 4.5 %products.3 = (s16[8,272,256]{2,1,0:T(8,128)(2,1)S(1)}, f32[8,256,256]{2,1,0:T(8,128)S(1)}) custom-call(s32[1]{0:T(128)} %bitcast.9.rounds_ref, s32[96]{0:T(128)S(1)} %get-tuple-element.69.source_ref, s32[96]{0:T(128)S(1)} %get-tuple-element.70.slot_ref, s32[96]{0:T(128)S(1)} %get-tuple-element.71.label_ref, bf16[96,256,256]{2,1,0:T(8,128)(2,1)S(1)} %hold.1.tiles, ...), custom_call_target="tpu_custom_call" | custom-call | bytes 12582912 | tf_op jit(solution)/shard_map/products/pallas_call | solution.py:406
  35.0 4.6 %collective-permute-done.9.refs_2_ = bf16[1024,256]{1,0:T(8,128)(2,1)S(1)} collective-permute-done((bf16[1024,256]{1,0:T(8,128)(2,1)S(1)}, bf16[1024,256]{1,0:T(8,128)(2,1)S(1)}, u32[]{:S(2)}, u32[]{:S(2)}) %collective-permute-start.9) | collective-permute-done | bytes 524320 | tf_op jit(solution)/shard_map/ppermute | solution.py:283
  41.6 4.5 %products.4 = (s16[4,272,256]{2,1,0:T(8,128)(2,1)S(1)}, s16[4,272,256]{2,1,0:T(8,128)(2,1)S(1)}, f32[8,256,256]{2,1,0:T(8,128)S(1)}) custom-call(s32[1]{0:T(128)} %bitcast.9.rounds_ref, s32[96]{0:T(128)S(1)} %get-tuple-element.69.source_ref, s32[96]{0:T(128)S(1)} %get-tuple-element.74.slot_ref, s32[96]{0:T(128)S(1)} %get-tuple-element.71.label_ref, ...), custom_call_target="tpu_custom_call" | custom-call | bytes 12582912 | tf_op jit(solution)/shard_map/products/pallas_call | solution.py:406
  49.1 4.5 %products.5 = (s16[4,272,256]{2,1,0:T(8,128)(2,1)S(1)}, s16[4,272,256]{2,1,0:T(8,128)(2,1)S(1)}, f32[8,256,256]{2,1,0:T(8,128)S(1)}) custom-call(s32[1]{0:T(128)} %bitcast.9.rounds_ref, s32[96]{0:T(128)S(1)} %get-tuple-element.69.source_ref, s32[96]{0:T(128)S(1)} %get-tuple-element.74.slot_ref, s32[96]{0:T(128)S(1)} %get-tuple-element.71.label_ref, ...), custom_call_target="tpu_custom_call" | custom-call | bytes 12582912 | tf_op jit(solution)/shard_map/products/pallas_call | solution.py:406
  54.8 5.3 %collective-permute-done.14.recv = s16[8,272,256]{2,1,0:T(8,128)(2,1)S(1)} collective-permute-done((s16[8,272,256]{2,1,0:T(8,128)(2,1)S(1)}, s16[8,272,256]{2,1,0:T(8,128)(2,1)S(1)}, u32[]{:S(2)}, u32[]{:S(2)}) %collective-permute-start.14) | collective-permute-done | bytes 1114144 | tf_op jit(solution)/shard_map/ppermute | solution.py:286
  61.2 2.3 %collective-permute-start.21 = (s16[4,272,256]{2,1,0:T(8,128)(2,1)S(1)}, s16[4,272,256]{2,1,0:T(8,128)(2,1)S(1)}, u32[]{:S(2)}, u32[]{:S(2)}) collective-permute-start(s16[4,272,256]{2,1,0:T(8,128)(2,1)S(1)} %get-tuple-element.80), channel_id=1, source_target_pairs={{0,4},{1,5},{2,6},{3,7},{4,0},{5,1},{6,2},{7,3},{8,12},{9,13},{10,... | collective-permute-start | bytes 1671176 | tf_op jit(solution)/shard_map/ppermute | solution.py:286
  66.5 7.0 %collective-permute-done.18.recv_b = s16[4,272,256]{2,1,0:T(8,128)(2,1)S(1)} collective-permute-done((s16[4,272,256]{2,1,0:T(8,128)(2,1)S(1)}, s16[4,272,256]{2,1,0:T(8,128)(2,1)S(1)}, u32[]{:S(2)}, u32[]{:S(2)}) %collective-permute-start.18) | collective-permute-done | bytes 557088 | tf_op jit(solution)/shard_map/ppermute | solution.py:283
  77.6 3.3 %collective-permute-done.20.recv_b = s16[2,272,256]{2,1,0:T(8,128)(2,1)S(1)} collective-permute-done((s16[2,272,256]{2,1,0:T(8,128)(2,1)S(1)}, s16[2,272,256]{2,1,0:T(8,128)(2,1)S(1)}, u32[]{:S(2)}, u32[]{:S(2)}) %collective-permute-start.20) | collective-permute-done | bytes 278560 | tf_op jit(solution)/shard_map/ppermute | solution.py:283
  81.8 2.2 %collective-permute-start.24 = (s16[2,272,256]{2,1,0:T(8,128)(2,1)S(1)}, s16[2,272,256]{2,1,0:T(8,128)(2,1)S(1)}, u32[]{:S(2)}, u32[]{:S(2)}) collective-permute-start(s16[2,272,256]{2,1,0:T(8,128)(2,1)S(1)} %get-tuple-element.92), channel_id=1, source_target_pairs={{0,2},{1,3},{2,0},{3,1},{4,6},{5,7},{6,4},{7,5},{8,10},{9,11},{10,... | collective-permute-start | bytes 835592 | tf_op jit(solution)/shard_map/ppermute | solution.py:286
  84.0 4.5 %collective-permute-done.21.recv = s16[4,272,256]{2,1,0:T(8,128)(2,1)S(1)} collective-permute-done((s16[4,272,256]{2,1,0:T(8,128)(2,1)S(1)}, s16[4,272,256]{2,1,0:T(8,128)(2,1)S(1)}, u32[]{:S(2)}, u32[]{:S(2)}) %collective-permute-start.21) | collective-permute-done | bytes 557088 | tf_op jit(solution)/shard_map/ppermute | solution.py:286
  91.0 1.6 %collective-permute-start.27 = (s16[272,256]{1,0:T(8,128)(2,1)S(1)}, s16[272,256]{1,0:T(8,128)(2,1)S(1)}, u32[]{:S(2)}, u32[]{:S(2)}) collective-permute-start(s16[272,256]{1,0:T(8,128)(2,1)S(1)} %get-tuple-element.105), channel_id=1, source_target_pairs={{0,24},{8,16},{16,8},{24,0},{1,25},{9,17},{17,9},{25,1},{2,26},{10... | collective-permute-start | bytes 417800 | tf_op jit(solution)/shard_map/ppermute | solution.py:283
  95.2 2.2 %collective-permute-start.29 = (s16[1,272,256]{2,1,0:T(8,128)(2,1)S(1)}, s16[1,272,256]{2,1,0:T(8,128)(2,1)S(1)}, u32[]{:S(2)}, u32[]{:S(2)}) collective-permute-start(s16[1,272,256]{2,1,0:T(8,128)(2,1)S(1)} %get-tuple-element.102), channel_id=1, source_target_pairs={{0,4},{1,5},{2,6},{3,7},{4,0},{5,1},{6,2},{7,3},{8,12},{9,13},{10,... | collective-permute-start | bytes 417800 | tf_op jit(solution)/shard_map/ppermute | solution.py:286
  100.3 2.7 %collective-permute-start.32 = (s16[272,256]{1,0:T(8,128)(2,1)S(1)}, s16[272,256]{1,0:T(8,128)(2,1)S(1)}, u32[]{:S(2)}, u32[]{:S(2)}) collective-permute-start(s16[272,256]{1,0:T(8,128)(2,1)S(1)} %finish.3.refs_0_), channel_id=1, source_target_pairs={{0,24},{8,16},{16,8},{24,0},{1,25},{9,17},{17,9},{25,1},{2,26},{10... | collective-permute-start | bytes 417800 | tf_op jit(solution)/shard_map/ppermute | solution.py:283
  104.6 3.4 %collective-permute-start.33 = (s16[1,272,256]{2,1,0:T(8,128)(2,1)S(1)}, s16[1,272,256]{2,1,0:T(8,128)(2,1)S(1)}, u32[]{:S(2)}, u32[]{:S(2)}) collective-permute-start(s16[1,272,256]{2,1,0:T(8,128)(2,1)S(1)} %get-tuple-element.109), channel_id=1, source_target_pairs={{0,4},{1,5},{2,6},{3,7},{4,0},{5,1},{6,2},{7,3},{8,12},{9,13},{10,... | collective-permute-start | bytes 417800 | tf_op jit(solution)/shard_map/ppermute | solution.py:286
  108.7 2.7 %collective-permute-start.36 = (s16[272,256]{1,0:T(8,128)(2,1)S(1)}, s16[272,256]{1,0:T(8,128)(2,1)S(1)}, u32[]{:S(2)}, u32[]{:S(2)}) collective-permute-start(s16[272,256]{1,0:T(8,128)(2,1)S(1)} %finish.4.refs_0_), channel_id=1, source_target_pairs={{0,24},{8,16},{16,8},{24,0},{1,25},{9,17},{17,9},{25,1},{2,26},{10... | collective-permute-start | bytes 417800 | tf_op jit(solution)/shard_map/ppermute | solution.py:283
  112.2 1.6 %spread.3.refs_4_ = f32[1024,768]{1,0:T(8,128)} custom-call(s32[4]{0:T(128)S(1)} %pad_add_fusion.2.order_ref.bits_ref, s16[272,256]{1,0:T(8,128)(2,1)S(1)} %finish.3.refs_0_, s16[272,256]{1,0:T(8,128)(2,1)S(1)} %collective-permute-done.30.refs_1_, s16[272,256]{1,0:T(8,128)(2,1)S(1)} %collective-permute-done.31.refs_2_, ...), custom_call_target="tpu_custom_call" | custom-call | bytes 1572864 | tf_op jit(solution)/shard_map/spread/pallas_call | solution.py:430
  114.5 2.7 %collective-permute-start.39 = (s16[272,256]{1,0:T(8,128)(2,1)S(1)}, s16[272,256]{1,0:T(8,128)(2,1)S(1)}, u32[]{:S(2)}, u32[]{:S(2)}) collective-permute-start(s16[272,256]{1,0:T(8,128)(2,1)S(1)} %finish.5.refs_0_), channel_id=1, source_target_pairs={{0,24},{8,16},{16,8},{24,0},{1,25},{9,17},{17,9},{25,1},{2,26},{10... | collective-permute-start | bytes 417800 | tf_op jit(solution)/shard_map/ppermute | solution.py:283
  118.7 1.6 %spread.4.refs_4_ = f32[1024,768]{1,0:T(8,128)} custom-call(s32[4]{0:T(128)S(1)} %pad_add_fusion.2.order_ref.bits_ref, s16[272,256]{1,0:T(8,128)(2,1)S(1)} %finish.4.refs_0_, s16[272,256]{1,0:T(8,128)(2,1)S(1)} %collective-permute-done.34.refs_1_, s16[272,256]{1,0:T(8,128)(2,1)S(1)} %collective-permute-done.35.refs_2_, ...), custom_call_target="tpu_custom_call", output_to_operand_aliasing={{}: (5, {})} | custom-call | bytes 1572864 | tf_op jit(solution)/shard_map/spread/pallas_call | solution.py:430
  120.3 1.8 %collective-permute-done.39.refs_3_ = s16[272,256]{1,0:T(8,128)(2,1)S(1)} collective-permute-done((s16[272,256]{1,0:T(8,128)(2,1)S(1)}, s16[272,256]{1,0:T(8,128)(2,1)S(1)}, u32[]{:S(2)}, u32[]{:S(2)}) %collective-permute-start.39) | collective-permute-done | bytes 139296 | tf_op jit(solution)/shard_map/ppermute | solution.py:283
  123.0 1.6 %spread.5 = f32[1024,768]{1,0:T(8,128)} custom-call(s32[4]{0:T(128)S(1)} %pad_add_fusion.2.order_ref.bits_ref, s16[272,256]{1,0:T(8,128)(2,1)S(1)} %finish.5.refs_0_, s16[272,256]{1,0:T(8,128)(2,1)S(1)} %collective-permute-done.37.refs_1_, s16[272,256]{1,0:T(8,128)(2,1)S(1)} %collective-permute-done.38.refs_2_, ...), custom_call_target="tpu_custom_call", output_to_operand_aliasing={{}: (5, {})} | custom-call | bytes 1572864 | tf_op jit(solution)/shard_map/spread/pallas_call | solution.py:430
  (98 shorter events, 44.9 us)
Async XLA Ops:
  0.0 19.2 %collective-permute-start.3 = (bf16[48,256,256]{2,1,0:T(8,128)(2,1)}, bf16[48,256,256]{2,1,0:T(8,128)(2,1)}, u32[]{:S(2)}, u32[]{:S(2)}) collective-permute-start(bf16[48,256,256]{2,1,0:T(8,128)(2,1)} %own_tiles.1), channel_id=1, source_target_pairs={{0,1},{1,0},{2,3},{3,2},{4,5},{5,4},{6,7},{7,6},{8,9},{9,8},{10,11... | collective-permute-start | bytes 18874376 | tf_op jit(solution)/shard_map/ppermute | solution.py:280
  2.4 16.3 %collective-permute-start.2 = (bf16[512,256]{1,0:T(8,128)(2,1)S(1)}, bf16[512,256]{1,0:T(8,128)(2,1)S(1)}, u32[]{:S(2)}, u32[]{:S(2)}) collective-permute-start(bf16[512,256]{1,0:T(8,128)(2,1)S(1)} %get-tuple-element.125.refs_0_), channel_id=1, source_target_pairs={{0,16},{8,24},{16,0},{24,8},{1,17},{9,25},{17,1},{25,9},{2,18},{10... | collective-permute-start | bytes 786440 | tf_op jit(solution)/shard_map/ppermute | solution.py:283
  5.4 9.2 %collective-permute-start.1 = (bf16[512,256]{1,0:T(8,128)(2,1)S(1)}, bf16[512,256]{1,0:T(8,128)(2,1)S(1)}, u32[]{:S(2)}, u32[]{:S(2)}) collective-permute-start(bf16[512,256]{1,0:T(8,128)(2,1)S(1)} %get-tuple-element.126.refs_0_), channel_id=1, source_target_pairs={{0,8},{8,0},{16,24},{24,16},{1,9},{9,1},{17,25},{25,17},{2,10},{10... | collective-permute-start | bytes 786440 | tf_op jit(solution)/shard_map/ppermute | solution.py:283
  6.9 17.6 %collective-permute-start.6 = (bf16[512,256]{1,0:T(8,128)(2,1)S(1)}, bf16[512,256]{1,0:T(8,128)(2,1)S(1)}, u32[]{:S(2)}, u32[]{:S(2)}) collective-permute-start(bf16[512,256]{1,0:T(8,128)(2,1)S(1)} %get-tuple-element.67), channel_id=1, source_target_pairs={{0,24},{8,16},{16,8},{24,0},{1,25},{9,17},{17,9},{25,1},{2,26},{10... | collective-permute-start | bytes 786440 | tf_op jit(solution)/shard_map/ppermute | solution.py:283
  11.2 13.3 %collective-permute-start.5 = (bf16[512,256]{1,0:T(8,128)(2,1)S(1)}, bf16[512,256]{1,0:T(8,128)(2,1)S(1)}, u32[]{:S(2)}, u32[]{:S(2)}) collective-permute-start(bf16[512,256]{1,0:T(8,128)(2,1)S(1)} %get-tuple-element.67), channel_id=1, source_target_pairs={{0,16},{8,24},{16,0},{24,8},{1,17},{9,25},{17,1},{25,9},{2,18},{10... | collective-permute-start | bytes 786440 | tf_op jit(solution)/shard_map/ppermute | solution.py:283
  14.6 10.0 %collective-permute-start.4 = (bf16[512,256]{1,0:T(8,128)(2,1)S(1)}, bf16[512,256]{1,0:T(8,128)(2,1)S(1)}, u32[]{:S(2)}, u32[]{:S(2)}) collective-permute-start(bf16[512,256]{1,0:T(8,128)(2,1)S(1)} %get-tuple-element.67), channel_id=1, source_target_pairs={{0,8},{8,0},{16,24},{24,16},{1,9},{9,1},{17,25},{25,17},{2,10},{10... | collective-permute-start | bytes 786440 | tf_op jit(solution)/shard_map/ppermute | solution.py:283
  25.3 14.3 %collective-permute-start.9 = (bf16[1024,256]{1,0:T(8,128)(2,1)S(1)}, bf16[1024,256]{1,0:T(8,128)(2,1)S(1)}, u32[]{:S(2)}, u32[]{:S(2)}) collective-permute-start(bf16[1024,256]{1,0:T(8,128)(2,1)S(1)} %join.3.refs_0_), channel_id=1, source_target_pairs={{0,16},{8,24},{16,0},{24,8},{1,17},{9,25},{17,1},{25,9},{2,18},{10... | collective-permute-start | bytes 1572872 | tf_op jit(solution)/shard_map/ppermute | solution.py:283
  26.8 14.0 %collective-permute-start.12 = (bf16[1024,256]{1,0:T(8,128)(2,1)S(1)}, bf16[1024,256]{1,0:T(8,128)(2,1)S(1)}, u32[]{:S(2)}, u32[]{:S(2)}) collective-permute-start(bf16[1024,256]{1,0:T(8,128)(2,1)S(1)} %join.4.refs_0_), channel_id=1, source_target_pairs={{0,8},{8,0},{16,24},{24,16},{1,9},{9,1},{17,25},{25,17},{2,10},{10... | collective-permute-start | bytes 1572872 | tf_op jit(solution)/shard_map/ppermute | solution.py:283
  32.8 27.2 %collective-permute-start.14 = (s16[8,272,256]{2,1,0:T(8,128)(2,1)S(1)}, s16[8,272,256]{2,1,0:T(8,128)(2,1)S(1)}, u32[]{:S(2)}, u32[]{:S(2)}) collective-permute-start(s16[8,272,256]{2,1,0:T(8,128)(2,1)S(1)} %get-tuple-element.72), channel_id=1, source_target_pairs={{0,2},{1,3},{2,0},{3,1},{4,6},{5,7},{6,4},{7,5},{8,10},{9,11},{10,... | collective-permute-start | bytes 3342344 | tf_op jit(solution)/shard_map/ppermute | solution.py:286
  39.7 9.4 %collective-permute-start.11 = (bf16[1024,256]{1,0:T(8,128)(2,1)S(1)}, bf16[1024,256]{1,0:T(8,128)(2,1)S(1)}, u32[]{:S(2)}, u32[]{:S(2)}) collective-permute-start(bf16[1024,256]{1,0:T(8,128)(2,1)S(1)} %join.4.refs_0_), channel_id=1, source_target_pairs={{0,1},{1,0},{2,3},{3,2},{4,5},{5,4},{6,7},{7,6},{8,9},{9,8},{10,11... | collective-permute-start | bytes 1572872 | tf_op jit(solution)/shard_map/ppermute | solution.py:280
  46.1 17.4 %collective-permute-start.16 = (s16[4,272,256]{2,1,0:T(8,128)(2,1)S(1)}, s16[4,272,256]{2,1,0:T(8,128)(2,1)S(1)}, u32[]{:S(2)}, u32[]{:S(2)}) collective-permute-start(s16[4,272,256]{2,1,0:T(8,128)(2,1)S(1)} %get-tuple-element.82), channel_id=1, source_target_pairs={{0,16},{8,24},{16,0},{24,8},{1,17},{9,25},{17,1},{25,9},{2,18},{10... | collective-permute-start | bytes 1671176 | tf_op jit(solution)/shard_map/ppermute | solution.py:283
  47.6 15.9 %collective-permute-start.15 = (s16[4,272,256]{2,1,0:T(8,128)(2,1)S(1)}, s16[4,272,256]{2,1,0:T(8,128)(2,1)S(1)}, u32[]{:S(2)}, u32[]{:S(2)}) collective-permute-start(s16[4,272,256]{2,1,0:T(8,128)(2,1)S(1)} %get-tuple-element.75), channel_id=1, source_target_pairs={{0,8},{8,0},{16,24},{24,16},{1,9},{9,1},{17,25},{25,17},{2,10},{10... | collective-permute-start | bytes 1671176 | tf_op jit(solution)/shard_map/ppermute | solution.py:283
  53.6 20.0 %collective-permute-start.18 = (s16[4,272,256]{2,1,0:T(8,128)(2,1)S(1)}, s16[4,272,256]{2,1,0:T(8,128)(2,1)S(1)}, u32[]{:S(2)}, u32[]{:S(2)}) collective-permute-start(s16[4,272,256]{2,1,0:T(8,128)(2,1)S(1)} %get-tuple-element.86), channel_id=1, source_target_pairs={{0,16},{8,24},{16,0},{24,8},{1,17},{9,25},{17,1},{25,9},{2,18},{10... | collective-permute-start | bytes 1671176 | tf_op jit(solution)/shard_map/ppermute | solution.py:283
  53.8 21.2 %collective-permute-start.17 = (s16[4,272,256]{2,1,0:T(8,128)(2,1)S(1)}, s16[4,272,256]{2,1,0:T(8,128)(2,1)S(1)}, u32[]{:S(2)}, u32[]{:S(2)}) collective-permute-start(s16[4,272,256]{2,1,0:T(8,128)(2,1)S(1)} %get-tuple-element.77), channel_id=1, source_target_pairs={{0,8},{8,0},{16,24},{24,16},{1,9},{9,1},{17,25},{25,17},{2,10},{10... | collective-permute-start | bytes 1671176 | tf_op jit(solution)/shard_map/ppermute | solution.py:283
  61.2 27.4 %collective-permute-start.21 = (s16[4,272,256]{2,1,0:T(8,128)(2,1)S(1)}, s16[4,272,256]{2,1,0:T(8,128)(2,1)S(1)}, u32[]{:S(2)}, u32[]{:S(2)}) collective-permute-start(s16[4,272,256]{2,1,0:T(8,128)(2,1)S(1)} %get-tuple-element.80), channel_id=1, source_target_pairs={{0,4},{1,5},{2,6},{3,7},{4,0},{5,1},{6,2},{7,3},{8,12},{9,13},{10,... | collective-permute-start | bytes 1671176 | tf_op jit(solution)/shard_map/ppermute | solution.py:286
  64.7 16.3 %collective-permute-start.20 = (s16[2,272,256]{2,1,0:T(8,128)(2,1)S(1)}, s16[2,272,256]{2,1,0:T(8,128)(2,1)S(1)}, u32[]{:S(2)}, u32[]{:S(2)}) collective-permute-start(s16[2,272,256]{2,1,0:T(8,128)(2,1)S(1)} %get-tuple-element.90), channel_id=1, source_target_pairs={{0,8},{8,0},{16,24},{24,16},{1,9},{9,1},{17,25},{25,17},{2,10},{10... | collective-permute-start | bytes 835592 | tf_op jit(solution)/shard_map/ppermute | solution.py:283
  65.7 15.2 %collective-permute-start.19 = (s16[2,272,256]{2,1,0:T(8,128)(2,1)S(1)}, s16[2,272,256]{2,1,0:T(8,128)(2,1)S(1)}, u32[]{:S(2)}, u32[]{:S(2)}) collective-permute-start(s16[2,272,256]{2,1,0:T(8,128)(2,1)S(1)} %get-tuple-element.84), channel_id=1, source_target_pairs={{0,16},{8,24},{16,0},{24,8},{1,17},{9,25},{17,1},{25,9},{2,18},{10... | collective-permute-start | bytes 835592 | tf_op jit(solution)/shard_map/ppermute | solution.py:283
  76.1 13.3 %collective-permute-start.23 = (s16[2,272,256]{2,1,0:T(8,128)(2,1)S(1)}, s16[2,272,256]{2,1,0:T(8,128)(2,1)S(1)}, u32[]{:S(2)}, u32[]{:S(2)}) collective-permute-start(s16[2,272,256]{2,1,0:T(8,128)(2,1)S(1)} %get-tuple-element.97), channel_id=1, source_target_pairs={{0,8},{8,0},{16,24},{24,16},{1,9},{9,1},{17,25},{25,17},{2,10},{10... | collective-permute-start | bytes 835592 | tf_op jit(solution)/shard_map/ppermute | solution.py:283
  77.6 11.7 %collective-permute-start.22 = (s16[2,272,256]{2,1,0:T(8,128)(2,1)S(1)}, s16[2,272,256]{2,1,0:T(8,128)(2,1)S(1)}, u32[]{:S(2)}, u32[]{:S(2)}) collective-permute-start(s16[2,272,256]{2,1,0:T(8,128)(2,1)S(1)} %get-tuple-element.88), channel_id=1, source_target_pairs={{0,16},{8,24},{16,0},{24,8},{1,17},{9,25},{17,1},{25,9},{2,18},{10... | collective-permute-start | bytes 835592 | tf_op jit(solution)/shard_map/ppermute | solution.py:283
  81.8 12.7 %collective-permute-start.24 = (s16[2,272,256]{2,1,0:T(8,128)(2,1)S(1)}, s16[2,272,256]{2,1,0:T(8,128)(2,1)S(1)}, u32[]{:S(2)}, u32[]{:S(2)}) collective-permute-start(s16[2,272,256]{2,1,0:T(8,128)(2,1)S(1)} %get-tuple-element.92), channel_id=1, source_target_pairs={{0,2},{1,3},{2,0},{3,1},{4,6},{5,7},{6,4},{7,5},{8,10},{9,11},{10,... | collective-permute-start | bytes 835592 | tf_op jit(solution)/shard_map/ppermute | solution.py:286
  90.2 13.6 %collective-permute-start.28 = (s16[2,272,256]{2,1,0:T(8,128)(2,1)S(1)}, s16[2,272,256]{2,1,0:T(8,128)(2,1)S(1)}, u32[]{:S(2)}, u32[]{:S(2)}) collective-permute-start(s16[2,272,256]{2,1,0:T(8,128)(2,1)S(1)} %get-tuple-element.99), channel_id=1, source_target_pairs={{0,2},{1,3},{2,0},{3,1},{4,6},{5,7},{6,4},{7,5},{8,10},{9,11},{10,... | collective-permute-start | bytes 835592 | tf_op jit(solution)/shard_map/ppermute | solution.py:286
  95.2 12.8 %collective-permute-start.29 = (s16[1,272,256]{2,1,0:T(8,128)(2,1)S(1)}, s16[1,272,256]{2,1,0:T(8,128)(2,1)S(1)}, u32[]{:S(2)}, u32[]{:S(2)}) collective-permute-start(s16[1,272,256]{2,1,0:T(8,128)(2,1)S(1)} %get-tuple-element.102), channel_id=1, source_target_pairs={{0,4},{1,5},{2,6},{3,7},{4,0},{5,1},{6,2},{7,3},{8,12},{9,13},{10,... | collective-permute-start | bytes 417800 | tf_op jit(solution)/shard_map/ppermute | solution.py:286
  100.3 11.1 %collective-permute-start.32 = (s16[272,256]{1,0:T(8,128)(2,1)S(1)}, s16[272,256]{1,0:T(8,128)(2,1)S(1)}, u32[]{:S(2)}, u32[]{:S(2)}) collective-permute-start(s16[272,256]{1,0:T(8,128)(2,1)S(1)} %finish.3.refs_0_), channel_id=1, source_target_pairs={{0,24},{8,16},{16,8},{24,0},{1,25},{9,17},{17,9},{25,1},{2,26},{10... | collective-permute-start | bytes 417800 | tf_op jit(solution)/shard_map/ppermute | solution.py:283
  104.6 9.3 %collective-permute-start.33 = (s16[1,272,256]{2,1,0:T(8,128)(2,1)S(1)}, s16[1,272,256]{2,1,0:T(8,128)(2,1)S(1)}, u32[]{:S(2)}, u32[]{:S(2)}) collective-permute-start(s16[1,272,256]{2,1,0:T(8,128)(2,1)S(1)} %get-tuple-element.109), channel_id=1, source_target_pairs={{0,4},{1,5},{2,6},{3,7},{4,0},{5,1},{6,2},{7,3},{8,12},{9,13},{10,... | collective-permute-start | bytes 417800 | tf_op jit(solution)/shard_map/ppermute | solution.py:286
  (17 other events, 114.4 us)
where the time goes:
time: 124 us; the launch traced here: 125 us
  starting transfers between devices  47.1 us (38%)
  waiting for transfers between devices  37.3 us (30%)
  Pallas kernels  34.5 us (28%)
  other arithmetic  3.33 us (3%)
  local copies, waits for them, and re-layouts  1.47 us (1%)
    ppermute x27, starting transfers between devices, to_grp(): return lax.ppermute(v, 'grp', [(i, i ^ d) for i in range(4)])  33.5 us
    ppermute x27, waiting for transfers between devices, to_grp(): return lax.ppermute(v, 'grp', [(i, i ^ d) for i in range(4)])  22.9 us
    pallas_call x3, Pallas kernels, products(): pl.pallas_call(functools.partial(products_kernel, tuple(fill)), grid=(1,)...  13.5 us
    ppermute x6, starting transfers between devices, to_line(): return lax.ppermute(v, 'wide', [(i, i ^ 2 << b) for i in range(wide_count)])  11.5 us
    pallas_call x14, Pallas kernels, call(): pl.pallas_call(body, in_specs=in_smem(1) + in_vmem(len(args)), out_specs=...  11 us
    ppermute x6, waiting for transfers between devices, to_line(): return lax.ppermute(v, 'wide', [(i, i ^ 2 << b) for i in range(wide_count)])  10.4 us
    pallas_call x1, Pallas kernels, hold(): pl.pallas_call(hold_kernel, in_specs=in_smem(1) + in_any(2), out_specs=in...  5.16 us
    pallas_call x3, Pallas kernels, spread(): pl.pallas_call(spread_kernel, grid=(1,), in_specs=in_smem(1) + in_vmem(4)...  4.87 us
  transfers between devices with their start and end apart: 40, of which 17 were waited for; matrix products, arithmetic and copies ran while one was open for 4% of the time, Pallas kernels for 26%

commit v1 on v0

--- a/solution.py
+++ b/solution.py
@@ -114,81 +114,89 @@
     return ref[pl.ds(0, side), :].astype(jnp.int32).astype(jnp.float32) * scale
 
 
-def hold_kernel(order_ref, own_tiles, sib_tiles, out, sems):
-    count = own_tiles.shape[0]
-    copies = [
-        pltpu.make_async_copy(tiles, out.at[pl.ds(i * count, count)], sems.at[i])
-        for i, tiles in enumerate((own_tiles, sib_tiles))
-    ]
-    for copy in copies:
-        copy.start()
-    for copy in copies:
-        copy.wait()
-
-
-def join_kernel(order_ref, *refs):
+def here():
+    g, w = lax.axis_index("grp"), lax.axis_index("wide")
+    return g % 2, g // 2, (w // 2) % 2, w // 4
+
+
+def hold_kernel(order, count_ref, source_ref, own_tiles, sib_tiles, out, sems):
+    own = own_tiles.shape[0]
+
+    def copy(tiles, which, i):
+        return pltpu.make_async_copy(tiles.at[which], out.at[i], sems.at[i])
+
+    @pl.loop(0, count_ref[0])
+    def _(i):
+        copy(own_tiles, source_ref[i], i).start()
+
+    @pl.loop(count_ref[0], count_ref[1])
+    def _(i):
+        copy(sib_tiles, source_ref[i] - own, i).start()
+
+    @pl.loop(0, count_ref[1])
+    def _(i):
+        copy(own_tiles, 0, i).wait()
+
+
+def join_kernel(order, *refs):
     *parts, out = refs
     rows = parts[0].shape[0]
     for i, part in enumerate(parts):
         out[pl.ds(i * rows, rows), :] = part[...]
 
 
-def products_kernel(
-    fill, rounds_ref, source_ref, slot_ref, label_ref, tiles, own_panel, *refs
-):
+def products_kernel(fill, order, count_ref, slot_ref, label_ref, tiles, own_panel, *refs):
     parts = refs[: 1 + max(which for which, _, _ in fill)]
-    *outs, stack, acc = refs[len(parts) :]
+    *sends, sums, stack = refs[len(parts) :]
     side = tiles.shape[1]
     for t in range(own_panel.shape[0] // side):
         stack[t] = own_panel[pl.ds(t * side, side), :]
     for which, t, at in fill:
         stack[at] = parts[which][pl.ds(t * side, side), :]
 
-    @pl.loop(0, acc.shape[0])
-    def _(i):
-        acc[i] = jnp.zeros(acc.shape[1:], jnp.float32)
-
-    @pl.loop(0, rounds_ref[0])
+    @pl.loop(0, sums.shape[0])
+    def _(i):
+        sums[i] = jnp.zeros(sums.shape[1:], jnp.float32)
+
+    @pl.loop(0, (count_ref[1] + UNROLL - 1) // UNROLL)
     def _(i):
         found = [
             jnp.dot(
-                tiles[source_ref[i * UNROLL + u]],
+                tiles[i * UNROLL + u],
                 stack[label_ref[i * UNROLL + u]],
                 preferred_element_type=jnp.float32,
             )
             for u in range(UNROLL)
         ]
         for u in range(UNROLL):
-            acc[slot_ref[i * UNROLL + u]] += found[u]
-
-    sent = 0
-    for out in outs:
-
-        @pl.loop(0, out.shape[0])
-        def _(i, out=out, sent=sent):
-            if out.dtype == jnp.int16:
-                put_encoded(out.at[i], acc[sent + i])
-            else:
-                out[i] = acc[sent + i]
-
-        sent += out.shape[0]
-
-
-def plane_kernel(bits_ref, recv_a, recv_b, kept, send_a, send_b, keep):
+            sums[slot_ref[i * UNROLL + u]] += found[u]
+
+    sent = sums.shape[0] // 2
+    for send in sends:
+
+        @pl.loop(0, send.shape[0])
+        def _(i, send=send, sent=sent):
+            put_encoded(send.at[i], sums[sent + i])
+
+        sent += send.shape[0]
+
+
+def plane_kernel(order, recv_a, recv_b, kept, send_a, send_b, keep):
     side, half = kept.shape[1], send_a.shape[0]
-    for first, bit, recv, send in ((0, bits_ref[1], recv_a, send_a), (1, bits_ref[0], recv_b, send_b)):
+    x, y, _, _ = here()
+    for base, bit, recv, send in ((0, y, recv_a, send_a), (1, x, recv_b, send_b)):
 
         @pl.loop(0, half)
-        def _(i, first=first, bit=bit, recv=recv, send=send):
+        def _(i, base=base, bit=bit, recv=recv, send=send):
             other, mine = 2 * i + 1 - bit, 2 * i + bit
-            base = first * 2 * half
-            put_encoded(send.at[i], kept[base + other] + get_decoded(recv.at[other], side))
-            keep[first * half + i] = kept[base + mine] + get_decoded(recv.at[mine], side)
-
-
-def owner_kernel(bits_ref, recv_a, recv_b, kept, send, keep):
+            at = base * 2 * half
+            put_encoded(send.at[i], kept[at + other] + get_decoded(recv.at[other], side))
+            keep[base * half + i] = kept[at + mine] + get_decoded(recv.at[mine], side)
+
+
+def owner_kernel(order, recv_a, recv_b, kept, send, keep):
     side, half = kept.shape[1], send.shape[0]
-    odd = bits_ref[2]
+    odd = here()[2]
 
     @pl.loop(0, half)
     def _(i):
@@ -198,26 +206,16 @@
         keep[i] = jnp.where(odd == 1, value_b, value_a)
 
 
-def line_kernel(bits_ref, recv, kept, send, keep):
-    side, half = kept.shape[1], send.shape[0]
-    bit = bits_ref[3]
-
-    @pl.loop(0, half)
-    def _(i):
-        other, mine = (1 - bit) * half + i, bit * half + i
-        put_encoded(send.at[i], kept[other] + get_decoded(recv.at[other], side))
-        keep[i] = kept[mine] + get_decoded(recv.at[mine], side)
-
-
-def rows_kernel(bits_ref, recv, kept, send_1, send_2, send_3, keep):
+def rows_kernel(order, recv, kept, send_1, send_2, send_3, keep):
     side = kept.shape[1]
-    row = bits_ref[1] * 2 + bits_ref[0]
+    x, y, _, _ = here()
+    row = 2 * y + x
     for d, send in enumerate((send_1, send_2, send_3), 1):
         put_encoded(send, kept[row ^ d] + get_decoded(recv.at[row ^ d], side))
     keep[...] = kept[row] + get_decoded(recv.at[row], side)
 
 
-def finish_kernel(bits_ref, *refs):
+def finish_rows_kernel(order, *refs):
     *recvs, kept, out = refs
     value = kept[...]
     for recv in recvs:
@@ -225,13 +223,37 @@
     put_encoded(out, value)
 
 
-def spread_kernel(bits_ref, *refs):
-    blocks, out = refs[:4], refs[-1]
-    side = blocks[0].shape[0] - CODE_ROWS
-    row = bits_ref[1] * 2 + bits_ref[0]
+def line_kernel(order, recv, kept, send, keep):
+    side, half = kept.shape[1], send.shape[0]
+    bit = here()[3]
+
+    @pl.loop(0, half)
+    def _(i):
+        other, mine = (1 - bit) * half + i, bit * half + i
+        put_encoded(send.at[i], kept[other] + get_decoded(recv.at[other], side))
+        keep[i] = kept[mine] + get_decoded(recv.at[mine], side)
+
+
+def finish_kernel(order, recv, kept, out):
+    put_encoded(out, kept[0] + get_decoded(recv.at[0], kept.shape[1]))
+
+
+def spread_kernel(chunk, order, *refs):
+    blocks, (out, rows, sems) = refs[:4], refs[-3:]
+    side, width = rows.shape[1:]
+    x, y, _, _ = here()
+    copies = []
     for d, block in enumerate(blocks):
-        at = pl.multiple_of((row ^ d) * side, side)
-        out[pl.ds(at, side), :] = get_decoded(block, side)
+        rows[d] = get_decoded(block, side)
+        at = pl.multiple_of(((2 * y + x) ^ d) * side, side)
+        copies.append(
+            pltpu.make_async_copy(
+                rows.at[d], out.at[pl.ds(at, side), pl.ds(chunk * width, width)], sems.at[d]
+            )
+        )
+        copies[-1].start()
+    for copy in copies:
+        copy.wait()
 
 
 def in_vmem(count):
@@ -286,7 +308,6 @@
         return lax.ppermute(v, "wide", [(i, i ^ (2 << b)) for i in range(wide_count)])
 
     x, y, z = g % 2, g // 2, w // 2
-    bits = jnp.stack([x, y, z % 2, z // 2]).astype(jnp.int32)
 
     labels = jnp.stack([row_tile, contraction])
     both = jnp.stack([labels, to_core(labels)])
@@ -308,8 +329,8 @@
     bit_x, bit_y = local % 2, local // 2
     first = jnp.where(odd == 1, bit_y == y, bit_x == x)
     second = jnp.where(odd == 1, bit_x, bit_y)
-    in_plane = jnp.where(first, sums // 2, 0) + odd * (sums // 4) + 2 * to_z + second
-    in_line = jnp.where(odd == z % 2, sums // 2, 0) + to_z * out_dev + local
+    in_plane = jnp.where(first, 0, sums // 2) + odd * (sums // 4) + 2 * to_z + second
+    in_line = jnp.where(odd == z % 2, 0, sums // 2) + to_z * out_dev + local
     k = both[:, 1]
     apart, inner = (k // shard) ^ g, k % shard
     half = shard // 2
@@ -319,9 +340,8 @@
     entries = [v.reshape(-1) for v in (in_plane, in_line, label)]
     serial = jnp.arange(match.shape[0], dtype=jnp.int32)
     source, in_plane, in_line, label = compact(match, [serial, *entries])
-    found = jnp.sum(match.astype(jnp.int32))
-    rounds = ((found + UNROLL - 1) // UNROLL)[None]
-    beyond = jnp.arange(source.shape[0], dtype=jnp.int32) >= found
+    counts = jnp.stack([jnp.sum(match[:tile_dev]), jnp.sum(match)]).astype(jnp.int32)
+    beyond = jnp.arange(source.shape[0], dtype=jnp.int32) >= counts[1]
     in_plane = jnp.where(beyond, sums, in_plane)
     in_line = jnp.where(beyond, sums, in_line)
 
@@ -332,44 +352,31 @@
     def stack_of(count, one):
         return shape((count, *one.shape), one.dtype)
 
+    order = jnp.zeros((1,), jnp.int32)
     last = None
 
-    def in_order(small):
-        return small if last is None else lax.optimization_barrier((small, last))[0]
-
-    def call(body, name, outs, *args):
+    def in_order():
+        return order if last is None else lax.optimization_barrier((order, last))[0]
+
+    def call(body, name, outs, *args, smem=0, mib=16, extra=(), **more):
         nonlocal last
         done = pl.pallas_call(
             body,
-            in_specs=in_smem(1) + in_vmem(len(args)),
-            out_specs=in_vmem(len(outs)),
+            in_specs=more.pop("in_specs", in_any(1) + in_smem(smem) + in_vmem(len(args) - smem)),
+            out_specs=more.pop("out_specs", in_vmem(len(outs))),
             out_shape=outs,
-            compiler_params=params(16),
+            scratch_shapes=list(extra),
+            compiler_params=params(mib),
             cost_estimate=cost(0, sum(math.prod(a.shape) * a.dtype.itemsize for a in args)),
             name=name,
-        )(in_order(bits), *args)
+            **more,
+        )(in_order(), *args)
         last = done[0]
         return done
 
-    first, *lists = lax.optimization_barrier((bits, rounds, source, in_plane, in_line, label))
-    rounds, source, in_plane, in_line, label = lists
-    held = None
-
-    def hold():
-        nonlocal held, last
-        held = last = pl.pallas_call(
-            hold_kernel,
-            in_specs=in_smem(1) + in_any(2),
-            out_specs=in_vmem(1)[0],
-            out_shape=pltpu.VMEM((2 * tile_dev, side, side), tiles.dtype),
-            scratch_shapes=[pltpu.SemaphoreType.DMA((2,))],
-            compiler_params=params(8),
-            cost_estimate=cost(0, 4 * tile_dev * side * side),
-            name="hold",
-        )(
-            in_order(first),
-            *[pltpu.with_memory_space_constraint(v, pltpu.HBM) for v in (tiles, sib_tiles)],
-        )
+    counts, source, in_plane, in_line, label = lax.optimization_barrier(
+        (counts, source, in_plane, in_line, label)
+    )
 
     def places(operand, tiles_of, first):
         return [
@@ -401,116 +408,122 @@
         )
         return fill, [joined, to_core(joined), second, to_core(second)]
 
-    def products(j, slot, outs, fill, parts):
-        nonlocal last
-        done = pl.pallas_call(
+    def products(j, slot, sends, fill, parts):
+        *sends, kept = call(
             functools.partial(products_kernel, tuple(fill)),
+            "products",
+            [*sends, stack_of(sums + 1, plain)],
+            counts,
+            slot,
+            label,
+            held,
+            panel,
+            *parts,
             grid=(1,),
-            in_specs=in_smem(4)
+            in_specs=in_any(1)
+            + in_smem(3)
             + in_vmem(1)
             + [pl.BlockSpec((rows, CHUNK), lambda i: (0, j))]
             + in_vmem(len(parts)),
-            out_specs=in_vmem(len(outs)),
-            out_shape=outs,
-            scratch_shapes=[
-                pltpu.VMEM((4 * shard, side, CHUNK), panel.dtype),
-                pltpu.VMEM((sums + 1, side, CHUNK), jnp.float32),
-            ],
-            compiler_params=params(24),
-            cost_estimate=cost(0, 4 * tile_dev * side * side),
-            name="products",
-        )(in_order(rounds), source, slot, label, held, panel, *parts)
-        last = done[0]
-        return done
-
-    def spread(j, done, result):
-        nonlocal last
-        blocks = [done] + [to_grp(done, d) for d in (1, 2, 3)]
+            extra=[pltpu.VMEM((4 * shard, side, CHUNK), panel.dtype)],
+            mib=24,
+        )
+        return *sends, kept
+
+    def gathered(done):
+        return [done] + [to_grp(done, d) for d in (1, 2, 3)]
+
+    def spread(j, blocks, result):
         earlier = [] if result is None else [result]
-        last = pl.pallas_call(
-            spread_kernel,
-            grid=(1,),
-            in_specs=in_smem(1) + in_vmem(4) + in_any(len(earlier)),
-            out_specs=pl.BlockSpec((out_dev * side, CHUNK), lambda i: (0, j)),
-            out_shape=shape((out_dev * side, columns), jnp.float32),
+        return call(
+            functools.partial(spread_kernel, j),
+            "spread",
+            [shape((out_dev * side, columns), jnp.float32)],
+            *blocks,
+            *earlier,
+            in_specs=in_any(1) + in_vmem(4) + in_any(len(earlier)),
+            out_specs=in_any(1),
             input_output_aliases={5: 0} if earlier else {},
-            compiler_params=params(16),
-            cost_estimate=cost(0, 6 * out_dev * side * CHUNK),
-            name="spread",
-        )(in_order(bits), *blocks, *earlier)
-        return last
-
-    def line_first(j):
-        panel_of = join(j)
-        yield
-        send, keep = products(
-            j, in_line, [stack_of(half, coded), stack_of(half, plain)], *panel_of
-        )
-        yield
-        recv = to_line(send, 0)
-        send, keep = call(
-            line_kernel, "line", [stack_of(quarter, coded), stack_of(quarter, plain)], recv, keep
-        )
-        yield
-        *sends, keep = call(rows_kernel, "rows", [coded] * 3 + [plain], to_line(send, 1), keep)
-        yield
-        recvs = [to_grp(v, d) for d, v in enumerate(sends, 1)]
-        (done,) = call(finish_kernel, "finish", [coded], *recvs, keep)
-        yield
-        yield done
-
-    def plane_first(j):
-        panel_of = pair(j)
-        yield
-        send_a, send_b, keep = products(
-            j, in_plane, [stack_of(quarter, coded)] * 2 + [stack_of(half, plain)], *panel_of
-        )
-        yield
-        send_a, send_b, keep = call(
+            extra=[pltpu.VMEM((4, side, CHUNK), jnp.float32), pltpu.SemaphoreType.DMA((4,))],
+        )[0]
+
+    eighth = quarter // 2
+    pairs = {j: pair(j) for j in (1, 2)}
+    (held,) = call(
+        hold_kernel,
+        "hold",
+        [pltpu.VMEM((2 * tile_dev, side, side), tiles.dtype)],
+        counts,
+        source,
+        *[pltpu.with_memory_space_constraint(v, pltpu.HBM) for v in (tiles, sib_tiles)],
+        in_specs=in_any(1) + in_smem(2) + in_any(2),
+        extra=[pltpu.SemaphoreType.DMA((2 * tile_dev,))],
+        mib=8,
+    )
+
+    send, keep_0 = products(0, in_line, [stack_of(half, coded)], *join(0))
+    sent_0 = send
+    sent, keep = {}, {}
+    for j in (1, 2):
+        send_a, send_b, keep[j] = products(j, in_plane, [stack_of(quarter, coded)] * 2, *pairs[j])
+        sent[j] = send_a, send_b
+
+    sent_0, keep_0 = call(
+        line_kernel,
+        "line",
+        [stack_of(quarter, coded), stack_of(quarter, plain)],
+        to_line(sent_0, 0),
+        keep_0,
+    )
+
+    def plane(j):
+        return call(
             plane_kernel,
             "plane",
-            [stack_of(quarter // 2, coded)] * 2 + [stack_of(quarter, plain)],
-            to_grp(send_a, 1),
-            to_grp(send_b, 2),
-            keep,
-        )
-        yield
-        send, keep = call(
+            [stack_of(eighth, coded)] * 2 + [stack_of(quarter, plain)],
+            to_grp(sent[j][0], 1),
+            to_grp(sent[j][1], 2),
+            keep[j],
+        )
+
+    def owner(j):
+        return call(
             owner_kernel,
             "owner",
-            [stack_of(quarter // 2, coded), stack_of(quarter // 2, plain)],
-            to_grp(send_a, 2),
-            to_grp(send_b, 1),
-            keep,
-        )
-        yield
-        send, keep = call(
+            [stack_of(eighth, coded), stack_of(eighth, plain)],
+            to_grp(sent[j][0], 2),
+            to_grp(sent[j][1], 1),
+            keep[j],
+        )
+
+    *sent[1], keep[1] = plane(1)
+    *sent[2], keep[2] = plane(2)
+    sent[1], keep[1] = owner(1)
+    *sends, keep_0 = call(
+        rows_kernel, "rows", [coded] * 3 + [plain], to_line(sent_0, 1), keep_0
+    )
+    sent[2], keep[2] = owner(2)
+    (done_0,) = call(
+        finish_rows_kernel,
+        "finish_rows",
+        [coded],
+        *[to_grp(v, d) for d, v in enumerate(sends, 1)],
+        keep_0,
+    )
+
+    for j in (1, 2):
+        sent[j], keep[j] = call(
             line_kernel,
             "line",
-            [stack_of(quarter // 4, coded), stack_of(quarter // 4, plain)],
-            to_line(send, 0),
-            keep,
-        )
-        yield
-        recv = to_line(send, 1)
-        (done,) = call(finish_kernel, "finish", [coded], recv[0], keep[0])
-        yield
-        yield done
-
-    steps, lengths = [0] * chunks, [5] + [6] * (chunks - 1)
-    work = [(line_first if j == 0 else plane_first)(j) for j in range(chunks)]
-    dones, result = {}, None
-    for j in (1, 2, None, 0, 0, 1, 2, 0, 1, 2, 1, 0, 2, 1, 0, 2, 1, 0, 2, 1, 2):
-        if j is None:
-            hold()
-        elif j in dones:
-            result = spread(j, dones[j], result)
-        else:
-            next(work[j])
-            steps[j] += 1
-            if steps[j] == lengths[j]:
-                dones[j] = next(work[j])
-    return result
+            [stack_of(1, coded), stack_of(1, plain)],
+            to_line(sent[j], 0),
+            keep[j],
+        )
+    (done_1,) = call(finish_kernel, "finish", [coded], to_line(sent[1], 1), keep[1])
+    result = spread(0, gathered(done_0), None)
+    (done_2,) = call(finish_kernel, "finish", [coded], to_line(sent[2], 1), keep[2])
+    result = spread(1, gathered(done_1), result)
+    return spread(2, gathered(done_2), result)
 
 
 def per_device(tiles, contraction, row_tile, owner_map, panel):

time: 124 us -> 126 us (1.016)
  Pallas kernels: 34.5 us -> 15.2 us
  starting transfers between devices: 47.1 us -> 59.4 us
  waiting for transfers between devices: 37.3 us -> 44 us
  other arithmetic: 3.33 us -> 5.26 us
    pallas_call x21, Pallas kernels: 34.5 us -> 15.2 us  [call(): pl.pallas_call(body, in_specs=more.pop('in_specs', in_any(1) + in_smem(sm...]
    ppermute x27, starting transfers between devices: 33.5 us -> 41.7 us  [to_grp(): return lax.ppermute(v, 'grp', [(i, i ^ d) for i in range(4)])]
    ppermute x27, waiting for transfers between devices: 22.9 us -> 29.8 us  [to_grp(): return lax.ppermute(v, 'grp', [(i, i ^ d) for i in range(4)])]
    ppermute x7, starting transfers between devices: 2.13 us -> 5.78 us  [to_core(): return lax.ppermute(v, 'wide', [(i, i ^ 1) for i in range(wide_count)])]
    ppermute x6, waiting for transfers between devices: 10.4 us -> 9.09 us  [to_line(): return lax.ppermute(v, 'wide', [(i, i ^ 2 << b) for i in range(wide_count)])]
    another operation x2, other arithmetic: 0.21 us -> 1.48 us  [the longest x1 1.35 us: sums_plan(): jnp.stack([jnp.sum(match[:tile_dev]), jnp.sum(match)]).astype(jnp.int32)]
  transfers between devices with their start and end apart: 40 -> 40, of which waited for: 17 -> 17; matrix products, arithmetic and copies ran while one was open for 4% -> 5% of each run, Pallas kernels for 26% -> 11%
where the time goes in v1:
time: 126 us
  starting transfers between devices  59.4 us (47%)
  waiting for transfers between devices  44 us (35%)
  Pallas kernels  15.2 us (12%)
  other arithmetic  5.26 us (4%)
  local copies, waits for them, and re-layouts  1.47 us (1%)
    ppermute x27, starting transfers between devices, to_grp(): return lax.ppermute(v, 'grp', [(i, i ^ d) for i in range(4)])  41.7 us
    ppermute x27, waiting for transfers between devices, to_grp(): return lax.ppermute(v, 'grp', [(i, i ^ d) for i in range(4)])  29.8 us
    pallas_call x21, Pallas kernels, call(): pl.pallas_call(body, in_specs=more.pop('in_specs', in_any(1) + in_smem(sm...  15.2 us
    ppermute x6, starting transfers between devices, to_line(): return lax.ppermute(v, 'wide', [(i, i ^ 2 << b) for i in range(wide_count)])  11.9 us
    ppermute x6, waiting for transfers between devices, to_line(): return lax.ppermute(v, 'wide', [(i, i ^ 2 << b) for i in range(wide_count)])  9.09 us
    ppermute x7, starting transfers between devices, to_core(): return lax.ppermute(v, 'wide', [(i, i ^ 1) for i in range(wide_count)])  5.78 us
    ppermute x7, waiting for transfers between devices, to_core(): return lax.ppermute(v, 'wide', [(i, i ^ 1) for i in range(wide_count)])  5.09 us
  transfers between devices with their start and end apart: 40, of which 17 were waited for; matrix products, arithmetic and copies ran while one was open for 5% of the time, Pallas kernels for 11%

profile of v1, /device:TPU:0, one launch (start us, length us, event | category | flops | bytes accessed | tf_op | source)
XLA Modules:
  0.0 125.7 jit_solution(12320638357890656726)
XLA Ops:
  2.4 4.0 %collective-permute-start.6 = (bf16[512,256]{1,0:T(8,128)(2,1)S(1)}, bf16[512,256]{1,0:T(8,128)(2,1)S(1)}, u32[]{:S(2)}, u32[]{:S(2)}) collective-permute-start(bf16[512,256]{1,0:T(8,128)(2,1)S(1)} %get-tuple-element.66), channel_id=1, source_target_pairs={{0,24},{8,16},{16,8},{24,0},{1,25},{9,17},{17,9},{25,1},{2,26},{10... | collective-permute-start | bytes 786440 | tf_op jit(solution)/shard_map/ppermute | solution.py:305
  7.0 3.2 %collective-permute-done.2 = s32[2,48]{1,0:T(2,128)S(1)} collective-permute-done((s32[2,48]{1,0:T(2,128)S(1)}, s32[2,48]{1,0:T(2,128)S(1)}, u32[]{:S(2)}, u32[]{:S(2)}) %collective-permute-start.2) | collective-permute-done | bytes 416 | tf_op jit(solution)/shard_map/ppermute | solution.py:302
  11.2 2.6 %collective-permute-start.5 = (bf16[512,256]{1,0:T(8,128)(2,1)S(1)}, bf16[512,256]{1,0:T(8,128)(2,1)S(1)}, u32[]{:S(2)}, u32[]{:S(2)}) collective-permute-start(bf16[512,256]{1,0:T(8,128)(2,1)S(1)} %get-tuple-element.66), channel_id=1, source_target_pairs={{0,16},{8,24},{16,0},{24,8},{1,17},{9,25},{17,1},{25,9},{2,18},{10... | collective-permute-start | bytes 786440 | tf_op jit(solution)/shard_map/ppermute | solution.py:305
  15.7 3.0 %collective-permute-done.refs_1_ = bf16[512,256]{1,0:T(8,128)(2,1)S(1)} collective-permute-done((bf16[512,256]{1,0:T(8,128)(2,1)S(1)}, bf16[512,256]{1,0:T(8,128)(2,1)S(1)}, u32[]{:S(2)}, u32[]{:S(2)}) %collective-permute-start) | collective-permute-done | bytes 262176 | tf_op jit(solution)/shard_map/ppermute | solution.py:305
  22.4 2.7 %hold.1.tiles = bf16[96,256,256]{2,1,0:T(8,128)(2,1)S(1)} custom-call(s32[1]{0:T(128)} %constant.143.clone.1.order, s32[2]{0:T(128)S(1)} %pad_add_fusion.2.count_ref, s32[96]{0:T(128)S(1)} %get-tuple-element.64.source_ref, bf16[48,256,256]{2,1,0:T(8,128)(2,1)} %own_tiles.1, bf16[48,256,256]{2,1,0:T(8,128)(2,1)} %collective-permute-done.3.sib_tiles), custom_call_target="tpu_custom_call" | custom-call | bytes 12583304 | tf_op jit(solution)/shard_map/hold/pallas_call | solution.py:363
  29.2 2.0 %products.3 = (s16[8,272,256]{2,1,0:T(8,128)(2,1)S(1)}, f32[17,256,256]{2,1,0:T(8,128)S(1)}) custom-call(s32[1]{0:T(128)} %constant.143.clone.1.order, s32[2]{0:T(128)S(1)} %pad_add_fusion.2.count_ref, s32[96]{0:T(128)S(1)} %get-tuple-element.68.slot_ref, s32[96]{0:T(128)S(1)} %get-tuple-element.69.label_ref, bf16[96,256,256]{2,1,0:T(8,128)(2,1)S(1)} %hold.1.tiles, ...), custom_call_target="tpu_custom_call" | custom-call | bytes 15729416 | tf_op jit(solution)/shard_map/products/pallas_call | solution.py:363
  31.2 2.1 %collective-permute-start.14 = (s16[8,272,256]{2,1,0:T(8,128)(2,1)S(1)}, s16[8,272,256]{2,1,0:T(8,128)(2,1)S(1)}, u32[]{:S(2)}, u32[]{:S(2)}) collective-permute-start(s16[8,272,256]{2,1,0:T(8,128)(2,1)S(1)} %get-tuple-element.70), channel_id=1, source_target_pairs={{0,2},{1,3},{2,0},{3,1},{4,6},{5,7},{6,4},{7,5},{8,10},{9,11},{10,... | collective-permute-start | bytes 3342344 | tf_op jit(solution)/shard_map/ppermute | solution.py:308
  33.3 3.7 %collective-permute-start.8 = (bf16[1024,256]{1,0:T(8,128)(2,1)S(1)}, bf16[1024,256]{1,0:T(8,128)(2,1)S(1)}, u32[]{:S(2)}, u32[]{:S(2)}) collective-permute-start(bf16[1024,256]{1,0:T(8,128)(2,1)S(1)} %join.3.refs_0_), channel_id=1, source_target_pairs={{0,1},{1,0},{2,3},{3,2},{4,5},{5,4},{6,7},{7,6},{8,9},{9,8},{10,11... | collective-permute-start | bytes 1572872 | tf_op jit(solution)/shard_map/ppermute | solution.py:302
  37.0 4.2 %collective-permute-done.9.refs_2_ = bf16[1024,256]{1,0:T(8,128)(2,1)S(1)} collective-permute-done((bf16[1024,256]{1,0:T(8,128)(2,1)S(1)}, bf16[1024,256]{1,0:T(8,128)(2,1)S(1)}, u32[]{:S(2)}, u32[]{:S(2)}) %collective-permute-start.9) | collective-permute-done | bytes 524320 | tf_op jit(solution)/shard_map/ppermute | solution.py:305
  43.1 2.0 %products.4 = (s16[4,272,256]{2,1,0:T(8,128)(2,1)S(1)}, s16[4,272,256]{2,1,0:T(8,128)(2,1)S(1)}, f32[17,256,256]{2,1,0:T(8,128)S(1)}) custom-call(s32[1]{0:T(128)} %constant.143.clone.1.order, s32[2]{0:T(128)S(1)} %pad_add_fusion.2.count_ref, s32[96]{0:T(128)S(1)} %get-tuple-element.72.slot_ref, s32[96]{0:T(128)S(1)} %get-tuple-element.69.label_ref, ...), custom_call_target="tpu_custom_call" | custom-call | bytes 16253704 | tf_op jit(solution)/shard_map/products/pallas_call | solution.py:363
  49.7 3.0 %collective-permute-start.18 = (s16[4,272,256]{2,1,0:T(8,128)(2,1)S(1)}, s16[4,272,256]{2,1,0:T(8,128)(2,1)S(1)}, u32[]{:S(2)}, u32[]{:S(2)}) collective-permute-start(s16[4,272,256]{2,1,0:T(8,128)(2,1)S(1)} %get-tuple-element.84), channel_id=1, source_target_pairs={{0,16},{8,24},{16,0},{24,8},{1,17},{9,25},{17,1},{25,9},{2,18},{10... | collective-permute-start | bytes 1671176 | tf_op jit(solution)/shard_map/ppermute | solution.py:305
  52.7 2.5 %collective-permute-done.14.recv = s16[8,272,256]{2,1,0:T(8,128)(2,1)S(1)} collective-permute-done((s16[8,272,256]{2,1,0:T(8,128)(2,1)S(1)}, s16[8,272,256]{2,1,0:T(8,128)(2,1)S(1)}, u32[]{:S(2)}, u32[]{:S(2)}) %collective-permute-start.14) | collective-permute-done | bytes 1114144 | tf_op jit(solution)/shard_map/ppermute | solution.py:308
  55.8 3.1 %collective-permute-start.21 = (s16[4,272,256]{2,1,0:T(8,128)(2,1)S(1)}, s16[4,272,256]{2,1,0:T(8,128)(2,1)S(1)}, u32[]{:S(2)}, u32[]{:S(2)}) collective-permute-start(s16[4,272,256]{2,1,0:T(8,128)(2,1)S(1)} %get-tuple-element.78), channel_id=1, source_target_pairs={{0,4},{1,5},{2,6},{3,7},{4,0},{5,1},{6,2},{7,3},{8,12},{9,13},{10,... | collective-permute-start | bytes 1671176 | tf_op jit(solution)/shard_map/ppermute | solution.py:308
  59.5 3.9 %collective-permute-start.20 = (s16[2,272,256]{2,1,0:T(8,128)(2,1)S(1)}, s16[2,272,256]{2,1,0:T(8,128)(2,1)S(1)}, u32[]{:S(2)}, u32[]{:S(2)}) collective-permute-start(s16[2,272,256]{2,1,0:T(8,128)(2,1)S(1)} %get-tuple-element.88), channel_id=1, source_target_pairs={{0,8},{8,0},{16,24},{24,16},{1,9},{9,1},{17,25},{25,17},{2,10},{10... | collective-permute-start | bytes 835592 | tf_op jit(solution)/shard_map/ppermute | solution.py:305
  64.1 4.2 %collective-permute-done.18.recv_b = s16[4,272,256]{2,1,0:T(8,128)(2,1)S(1)} collective-permute-done((s16[4,272,256]{2,1,0:T(8,128)(2,1)S(1)}, s16[4,272,256]{2,1,0:T(8,128)(2,1)S(1)}, u32[]{:S(2)}, u32[]{:S(2)}) %collective-permute-start.18) | collective-permute-done | bytes 557088 | tf_op jit(solution)/shard_map/ppermute | solution.py:305
  68.3 2.5 %collective-permute-done.17.recv_a = s16[4,272,256]{2,1,0:T(8,128)(2,1)S(1)} collective-permute-done((s16[4,272,256]{2,1,0:T(8,128)(2,1)S(1)}, s16[4,272,256]{2,1,0:T(8,128)(2,1)S(1)}, u32[]{:S(2)}, u32[]{:S(2)}) %collective-permute-start.17) | collective-permute-done | bytes 557088 | tf_op jit(solution)/shard_map/ppermute | solution.py:305
  71.4 2.3 %collective-permute-start.23 = (s16[2,272,256]{2,1,0:T(8,128)(2,1)S(1)}, s16[2,272,256]{2,1,0:T(8,128)(2,1)S(1)}, u32[]{:S(2)}, u32[]{:S(2)}) collective-permute-start(s16[2,272,256]{2,1,0:T(8,128)(2,1)S(1)} %get-tuple-element.95), channel_id=1, source_target_pairs={{0,8},{8,0},{16,24},{24,16},{1,9},{9,1},{17,25},{25,17},{2,10},{10... | collective-permute-start | bytes 835592 | tf_op jit(solution)/shard_map/ppermute | solution.py:305
  73.7 2.2 %collective-permute-start.22 = (s16[2,272,256]{2,1,0:T(8,128)(2,1)S(1)}, s16[2,272,256]{2,1,0:T(8,128)(2,1)S(1)}, u32[]{:S(2)}, u32[]{:S(2)}) collective-permute-start(s16[2,272,256]{2,1,0:T(8,128)(2,1)S(1)} %get-tuple-element.86), channel_id=1, source_target_pairs={{0,16},{8,24},{16,0},{24,8},{1,17},{9,25},{17,1},{25,9},{2,18},{10... | collective-permute-start | bytes 835592 | tf_op jit(solution)/shard_map/ppermute | solution.py:305
  77.1 3.7 %collective-permute-start.27 = (s16[2,272,256]{2,1,0:T(8,128)(2,1)S(1)}, s16[2,272,256]{2,1,0:T(8,128)(2,1)S(1)}, u32[]{:S(2)}, u32[]{:S(2)}) collective-permute-start(s16[2,272,256]{2,1,0:T(8,128)(2,1)S(1)} %get-tuple-element.90), channel_id=1, source_target_pairs={{0,2},{1,3},{2,0},{3,1},{4,6},{5,7},{6,4},{7,5},{8,10},{9,11},{10,... | collective-permute-start | bytes 835592 | tf_op jit(solution)/shard_map/ppermute | solution.py:308
  82.6 5.4 %collective-permute-start.24 = (s16[272,256]{1,0:T(8,128)(2,1)S(1)}, s16[272,256]{1,0:T(8,128)(2,1)S(1)}, u32[]{:S(2)}, u32[]{:S(2)}) collective-permute-start(s16[272,256]{1,0:T(8,128)(2,1)S(1)} %get-tuple-element.93), channel_id=1, source_target_pairs={{0,8},{8,0},{16,24},{24,16},{1,9},{9,1},{17,25},{25,17},{2,10},{10... | collective-permute-start | bytes 417800 | tf_op jit(solution)/shard_map/ppermute | solution.py:305
  90.1 7.0 %collective-permute-done.25.refs_1_ = s16[272,256]{1,0:T(8,128)(2,1)S(1)} collective-permute-done((s16[272,256]{1,0:T(8,128)(2,1)S(1)}, s16[272,256]{1,0:T(8,128)(2,1)S(1)}, u32[]{:S(2)}, u32[]{:S(2)}) %collective-permute-start.25) | collective-permute-done | bytes 139296 | tf_op jit(solution)/shard_map/ppermute | solution.py:305
  101.2 2.9 %collective-permute-start.33 = (s16[1,272,256]{2,1,0:T(8,128)(2,1)S(1)}, s16[1,272,256]{2,1,0:T(8,128)(2,1)S(1)}, u32[]{:S(2)}, u32[]{:S(2)}) collective-permute-start(s16[1,272,256]{2,1,0:T(8,128)(2,1)S(1)} %get-tuple-element.107), channel_id=1, source_target_pairs={{0,4},{1,5},{2,6},{3,7},{4,0},{5,1},{6,2},{7,3},{8,12},{9,13},{10,... | collective-permute-start | bytes 417800 | tf_op jit(solution)/shard_map/ppermute | solution.py:308
  104.1 5.0 %collective-permute-done.29.recv = s16[1,272,256]{2,1,0:T(8,128)(2,1)S(1)} collective-permute-done((s16[1,272,256]{2,1,0:T(8,128)(2,1)S(1)}, s16[1,272,256]{2,1,0:T(8,128)(2,1)S(1)}, u32[]{:S(2)}, u32[]{:S(2)}) %collective-permute-start.29) | collective-permute-done | bytes 139296 | tf_op jit(solution)/shard_map/ppermute | solution.py:308
  117.5 2.3 %collective-permute-done.35.refs_2_ = s16[272,256]{1,0:T(8,128)(2,1)S(1)} collective-permute-done((s16[272,256]{1,0:T(8,128)(2,1)S(1)}, s16[272,256]{1,0:T(8,128)(2,1)S(1)}, u32[]{:S(2)}, u32[]{:S(2)}) %collective-permute-start.35) | collective-permute-done | bytes 139296 | tf_op jit(solution)/shard_map/ppermute | solution.py:305
  (99 shorter events, 45.9 us)
Async XLA Ops:
  0.0 22.3 %collective-permute-start.3 = (bf16[48,256,256]{2,1,0:T(8,128)(2,1)}, bf16[48,256,256]{2,1,0:T(8,128)(2,1)}, u32[]{:S(2)}, u32[]{:S(2)}) collective-permute-start(bf16[48,256,256]{2,1,0:T(8,128)(2,1)} %own_tiles.1), channel_id=1, source_target_pairs={{0,1},{1,0},{2,3},{3,2},{4,5},{5,4},{6,7},{7,6},{8,9},{9,8},{10,11... | collective-permute-start | bytes 18874376 | tf_op jit(solution)/shard_map/ppermute | solution.py:302
  2.4 22.7 %collective-permute-start.6 = (bf16[512,256]{1,0:T(8,128)(2,1)S(1)}, bf16[512,256]{1,0:T(8,128)(2,1)S(1)}, u32[]{:S(2)}, u32[]{:S(2)}) collective-permute-start(bf16[512,256]{1,0:T(8,128)(2,1)S(1)} %get-tuple-element.66), channel_id=1, source_target_pairs={{0,24},{8,16},{16,8},{24,0},{1,25},{9,17},{17,9},{25,1},{2,26},{10... | collective-permute-start | bytes 786440 | tf_op jit(solution)/shard_map/ppermute | solution.py:305
  6.3 16.0 %collective-permute-start.1 = (bf16[512,256]{1,0:T(8,128)(2,1)S(1)}, bf16[512,256]{1,0:T(8,128)(2,1)S(1)}, u32[]{:S(2)}, u32[]{:S(2)}) collective-permute-start(bf16[512,256]{1,0:T(8,128)(2,1)S(1)} %get-tuple-element.126.refs_0_), channel_id=1, source_target_pairs={{0,16},{8,24},{16,0},{24,8},{1,17},{9,25},{17,1},{25,9},{2,18},{10... | collective-permute-start | bytes 786440 | tf_op jit(solution)/shard_map/ppermute | solution.py:305
  6.8 11.9 %collective-permute-start = (bf16[512,256]{1,0:T(8,128)(2,1)S(1)}, bf16[512,256]{1,0:T(8,128)(2,1)S(1)}, u32[]{:S(2)}, u32[]{:S(2)}) collective-permute-start(bf16[512,256]{1,0:T(8,128)(2,1)S(1)} %get-tuple-element.127.refs_0_), channel_id=1, source_target_pairs={{0,8},{8,0},{16,24},{24,16},{1,9},{9,1},{17,25},{25,17},{2,10},{10... | collective-permute-start | bytes 786440 | tf_op jit(solution)/shard_map/ppermute | solution.py:305
  11.2 13.9 %collective-permute-start.5 = (bf16[512,256]{1,0:T(8,128)(2,1)S(1)}, bf16[512,256]{1,0:T(8,128)(2,1)S(1)}, u32[]{:S(2)}, u32[]{:S(2)}) collective-permute-start(bf16[512,256]{1,0:T(8,128)(2,1)S(1)} %get-tuple-element.66), channel_id=1, source_target_pairs={{0,16},{8,24},{16,0},{24,8},{1,17},{9,25},{17,1},{25,9},{2,18},{10... | collective-permute-start | bytes 786440 | tf_op jit(solution)/shard_map/ppermute | solution.py:305
  27.3 13.9 %collective-permute-start.9 = (bf16[1024,256]{1,0:T(8,128)(2,1)S(1)}, bf16[1024,256]{1,0:T(8,128)(2,1)S(1)}, u32[]{:S(2)}, u32[]{:S(2)}) collective-permute-start(bf16[1024,256]{1,0:T(8,128)(2,1)S(1)} %join.3.refs_0_), channel_id=1, source_target_pairs={{0,16},{8,24},{16,0},{24,8},{1,17},{9,25},{17,1},{25,9},{2,18},{10... | collective-permute-start | bytes 1572872 | tf_op jit(solution)/shard_map/ppermute | solution.py:305
  27.3 14.4 %collective-permute-start.12 = (bf16[1024,256]{1,0:T(8,128)(2,1)S(1)}, bf16[1024,256]{1,0:T(8,128)(2,1)S(1)}, u32[]{:S(2)}, u32[]{:S(2)}) collective-permute-start(bf16[1024,256]{1,0:T(8,128)(2,1)S(1)} %join.4.refs_0_), channel_id=1, source_target_pairs={{0,8},{8,0},{16,24},{24,16},{1,9},{9,1},{17,25},{25,17},{2,10},{10... | collective-permute-start | bytes 1572872 | tf_op jit(solution)/shard_map/ppermute | solution.py:305
  31.2 24.0 %collective-permute-start.14 = (s16[8,272,256]{2,1,0:T(8,128)(2,1)S(1)}, s16[8,272,256]{2,1,0:T(8,128)(2,1)S(1)}, u32[]{:S(2)}, u32[]{:S(2)}) collective-permute-start(s16[8,272,256]{2,1,0:T(8,128)(2,1)S(1)} %get-tuple-element.70), channel_id=1, source_target_pairs={{0,2},{1,3},{2,0},{3,1},{4,6},{5,7},{6,4},{7,5},{8,10},{9,11},{10,... | collective-permute-start | bytes 3342344 | tf_op jit(solution)/shard_map/ppermute | solution.py:308
  45.1 13.8 %collective-permute-start.16 = (s16[4,272,256]{2,1,0:T(8,128)(2,1)S(1)}, s16[4,272,256]{2,1,0:T(8,128)(2,1)S(1)}, u32[]{:S(2)}, u32[]{:S(2)}) collective-permute-start(s16[4,272,256]{2,1,0:T(8,128)(2,1)S(1)} %get-tuple-element.80), channel_id=1, source_target_pairs={{0,16},{8,24},{16,0},{24,8},{1,17},{9,25},{17,1},{25,9},{2,18},{10... | collective-permute-start | bytes 1671176 | tf_op jit(solution)/shard_map/ppermute | solution.py:305
  46.5 12.4 %collective-permute-start.15 = (s16[4,272,256]{2,1,0:T(8,128)(2,1)S(1)}, s16[4,272,256]{2,1,0:T(8,128)(2,1)S(1)}, u32[]{:S(2)}, u32[]{:S(2)}) collective-permute-start(s16[4,272,256]{2,1,0:T(8,128)(2,1)S(1)} %get-tuple-element.73), channel_id=1, source_target_pairs={{0,8},{8,0},{16,24},{24,16},{1,9},{9,1},{17,25},{25,17},{2,10},{10... | collective-permute-start | bytes 1671176 | tf_op jit(solution)/shard_map/ppermute | solution.py:305
  49.7 18.6 %collective-permute-start.18 = (s16[4,272,256]{2,1,0:T(8,128)(2,1)S(1)}, s16[4,272,256]{2,1,0:T(8,128)(2,1)S(1)}, u32[]{:S(2)}, u32[]{:S(2)}) collective-permute-start(s16[4,272,256]{2,1,0:T(8,128)(2,1)S(1)} %get-tuple-element.84), channel_id=1, source_target_pairs={{0,16},{8,24},{16,0},{24,8},{1,17},{9,25},{17,1},{25,9},{2,18},{10... | collective-permute-start | bytes 1671176 | tf_op jit(solution)/shard_map/ppermute | solution.py:305
  52.7 18.1 %collective-permute-start.17 = (s16[4,272,256]{2,1,0:T(8,128)(2,1)S(1)}, s16[4,272,256]{2,1,0:T(8,128)(2,1)S(1)}, u32[]{:S(2)}, u32[]{:S(2)}) collective-permute-start(s16[4,272,256]{2,1,0:T(8,128)(2,1)S(1)} %get-tuple-element.75), channel_id=1, source_target_pairs={{0,8},{8,0},{16,24},{24,16},{1,9},{9,1},{17,25},{25,17},{2,10},{10... | collective-permute-start | bytes 1671176 | tf_op jit(solution)/shard_map/ppermute | solution.py:305
  55.8 26.5 %collective-permute-start.21 = (s16[4,272,256]{2,1,0:T(8,128)(2,1)S(1)}, s16[4,272,256]{2,1,0:T(8,128)(2,1)S(1)}, u32[]{:S(2)}, u32[]{:S(2)}) collective-permute-start(s16[4,272,256]{2,1,0:T(8,128)(2,1)S(1)} %get-tuple-element.78), channel_id=1, source_target_pairs={{0,4},{1,5},{2,6},{3,7},{4,0},{5,1},{6,2},{7,3},{8,12},{9,13},{10,... | collective-permute-start | bytes 1671176 | tf_op jit(solution)/shard_map/ppermute | solution.py:308
  59.5 17.3 %collective-permute-start.20 = (s16[2,272,256]{2,1,0:T(8,128)(2,1)S(1)}, s16[2,272,256]{2,1,0:T(8,128)(2,1)S(1)}, u32[]{:S(2)}, u32[]{:S(2)}) collective-permute-start(s16[2,272,256]{2,1,0:T(8,128)(2,1)S(1)} %get-tuple-element.88), channel_id=1, source_target_pairs={{0,8},{8,0},{16,24},{24,16},{1,9},{9,1},{17,25},{25,17},{2,10},{10... | collective-permute-start | bytes 835592 | tf_op jit(solution)/shard_map/ppermute | solution.py:305
  63.4 13.4 %collective-permute-start.19 = (s16[2,272,256]{2,1,0:T(8,128)(2,1)S(1)}, s16[2,272,256]{2,1,0:T(8,128)(2,1)S(1)}, u32[]{:S(2)}, u32[]{:S(2)}) collective-permute-start(s16[2,272,256]{2,1,0:T(8,128)(2,1)S(1)} %get-tuple-element.82), channel_id=1, source_target_pairs={{0,16},{8,24},{16,0},{24,8},{1,17},{9,25},{17,1},{25,9},{2,18},{10... | collective-permute-start | bytes 835592 | tf_op jit(solution)/shard_map/ppermute | solution.py:305
  71.4 16.9 %collective-permute-start.23 = (s16[2,272,256]{2,1,0:T(8,128)(2,1)S(1)}, s16[2,272,256]{2,1,0:T(8,128)(2,1)S(1)}, u32[]{:S(2)}, u32[]{:S(2)}) collective-permute-start(s16[2,272,256]{2,1,0:T(8,128)(2,1)S(1)} %get-tuple-element.95), channel_id=1, source_target_pairs={{0,8},{8,0},{16,24},{24,16},{1,9},{9,1},{17,25},{25,17},{2,10},{10... | collective-permute-start | bytes 835592 | tf_op jit(solution)/shard_map/ppermute | solution.py:305
  73.7 16.0 %collective-permute-start.22 = (s16[2,272,256]{2,1,0:T(8,128)(2,1)S(1)}, s16[2,272,256]{2,1,0:T(8,128)(2,1)S(1)}, u32[]{:S(2)}, u32[]{:S(2)}) collective-permute-start(s16[2,272,256]{2,1,0:T(8,128)(2,1)S(1)} %get-tuple-element.86), channel_id=1, source_target_pairs={{0,16},{8,24},{16,0},{24,8},{1,17},{9,25},{17,1},{25,9},{2,18},{10... | collective-permute-start | bytes 835592 | tf_op jit(solution)/shard_map/ppermute | solution.py:305
  77.1 20.2 %collective-permute-start.27 = (s16[2,272,256]{2,1,0:T(8,128)(2,1)S(1)}, s16[2,272,256]{2,1,0:T(8,128)(2,1)S(1)}, u32[]{:S(2)}, u32[]{:S(2)}) collective-permute-start(s16[2,272,256]{2,1,0:T(8,128)(2,1)S(1)} %get-tuple-element.90), channel_id=1, source_target_pairs={{0,2},{1,3},{2,0},{3,1},{4,6},{5,7},{6,4},{7,5},{8,10},{9,11},{10,... | collective-permute-start | bytes 835592 | tf_op jit(solution)/shard_map/ppermute | solution.py:308
  82.6 14.5 %collective-permute-start.24 = (s16[272,256]{1,0:T(8,128)(2,1)S(1)}, s16[272,256]{1,0:T(8,128)(2,1)S(1)}, u32[]{:S(2)}, u32[]{:S(2)}) collective-permute-start(s16[272,256]{1,0:T(8,128)(2,1)S(1)} %get-tuple-element.93), channel_id=1, source_target_pairs={{0,8},{8,0},{16,24},{24,16},{1,9},{9,1},{17,25},{25,17},{2,10},{10... | collective-permute-start | bytes 417800 | tf_op jit(solution)/shard_map/ppermute | solution.py:305
  97.4 11.7 %collective-permute-start.29 = (s16[1,272,256]{2,1,0:T(8,128)(2,1)S(1)}, s16[1,272,256]{2,1,0:T(8,128)(2,1)S(1)}, u32[]{:S(2)}, u32[]{:S(2)}) collective-permute-start(s16[1,272,256]{2,1,0:T(8,128)(2,1)S(1)} %get-tuple-element.104), channel_id=1, source_target_pairs={{0,4},{1,5},{2,6},{3,7},{4,0},{5,1},{6,2},{7,3},{8,12},{9,13},{10,... | collective-permute-start | bytes 417800 | tf_op jit(solution)/shard_map/ppermute | solution.py:308
  97.5 13.7 %collective-permute-start.32 = (s16[272,256]{1,0:T(8,128)(2,1)S(1)}, s16[272,256]{1,0:T(8,128)(2,1)S(1)}, u32[]{:S(2)}, u32[]{:S(2)}) collective-permute-start(s16[272,256]{1,0:T(8,128)(2,1)S(1)} %finish_rows.1.refs_0_), channel_id=1, source_target_pairs={{0,24},{8,16},{16,8},{24,0},{1,25},{9,17},{17,9},{25,1},{2,26},{10... | collective-permute-start | bytes 417800 | tf_op jit(solution)/shard_map/ppermute | solution.py:305
  98.9 12.2 %collective-permute-start.31 = (s16[272,256]{1,0:T(8,128)(2,1)S(1)}, s16[272,256]{1,0:T(8,128)(2,1)S(1)}, u32[]{:S(2)}, u32[]{:S(2)}) collective-permute-start(s16[272,256]{1,0:T(8,128)(2,1)S(1)} %finish_rows.1.refs_0_), channel_id=1, source_target_pairs={{0,16},{8,24},{16,0},{24,8},{1,17},{9,25},{17,1},{25,9},{2,18},{10... | collective-permute-start | bytes 417800 | tf_op jit(solution)/shard_map/ppermute | solution.py:305
  99.4 13.4 %collective-permute-start.30 = (s16[272,256]{1,0:T(8,128)(2,1)S(1)}, s16[272,256]{1,0:T(8,128)(2,1)S(1)}, u32[]{:S(2)}, u32[]{:S(2)}) collective-permute-start(s16[272,256]{1,0:T(8,128)(2,1)S(1)} %finish_rows.1.refs_0_), channel_id=1, source_target_pairs={{0,8},{8,0},{16,24},{24,16},{1,9},{9,1},{17,25},{25,17},{2,10},{10... | collective-permute-start | bytes 417800 | tf_op jit(solution)/shard_map/ppermute | solution.py:305
  101.2 12.6 %collective-permute-start.33 = (s16[1,272,256]{2,1,0:T(8,128)(2,1)S(1)}, s16[1,272,256]{2,1,0:T(8,128)(2,1)S(1)}, u32[]{:S(2)}, u32[]{:S(2)}) collective-permute-start(s16[1,272,256]{2,1,0:T(8,128)(2,1)S(1)} %get-tuple-element.107), channel_id=1, source_target_pairs={{0,4},{1,5},{2,6},{3,7},{4,0},{5,1},{6,2},{7,3},{8,12},{9,13},{10,... | collective-permute-start | bytes 417800 | tf_op jit(solution)/shard_map/ppermute | solution.py:308
  (17 other events, 128.4 us)

commit v2 on v1

--- a/solution.py
+++ b/solution.py
@@ -119,21 +119,56 @@
     return g % 2, g // 2, (w // 2) % 2, w // 4
 
 
-def hold_kernel(order, count_ref, source_ref, own_tiles, sib_tiles, out, sems):
-    own = own_tiles.shape[0]
-
-    def copy(tiles, which, i):
-        return pltpu.make_async_copy(tiles.at[which], out.at[i], sems.at[i])
-
-    @pl.loop(0, count_ref[0])
-    def _(i):
-        copy(own_tiles, source_ref[i], i).start()
-
-    @pl.loop(count_ref[0], count_ref[1])
-    def _(i):
-        copy(sib_tiles, source_ref[i] - own, i).start()
-
-    @pl.loop(0, count_ref[1])
+def hold_kernel(
+    order, row_ref, k_ref, sib_ref, owner_ref, own_tiles, sib_tiles,
+    count_ref, plane_ref, line_ref, label_ref, out, sems,
+):
+    tile_dev = own_tiles.shape[0]
+    sums = owner_ref.shape[0] // 2
+    shard, out_dev = 4, 4
+    x, y, z_low, _ = here()
+    g, core = lax.axis_index("grp"), lax.axis_index("wide") % 2
+
+    def copy(tiles, which, at):
+        return pltpu.make_async_copy(tiles.at[which], out.at[at], sems.at[at])
+
+    def scan(tiles, row, k, count):
+        def one(i, count):
+            position = owner_ref[row(i)]
+            owner, local = lax.div(position, out_dev), lax.rem(position, out_dev)
+            match = lax.rem(owner, 2) == core
+
+            @pl.when(match)
+            def _():
+                copy(tiles, i, count).start()
+                odd, to_z = lax.rem(lax.div(owner, 2), 2), lax.div(owner, 4)
+                bit_x, bit_y = lax.rem(local, 2), lax.div(local, 2)
+                first = jnp.where(odd == 1, bit_y == y, bit_x == x)
+                second = jnp.where(odd == 1, bit_x, bit_y)
+                plane_ref[count] = (
+                    jnp.where(first, 0, sums // 2) + odd * (sums // 4) + 2 * to_z + second
+                )
+                line_ref[count] = (
+                    jnp.where(odd == z_low, 0, sums // 2) + to_z * out_dev + local
+                )
+                apart, inner = lax.div(k(i), shard) ^ g, lax.rem(k(i), shard)
+                half = shard // 2
+                crossed = jnp.where(lax.div(inner, half) == core, 0, half) + lax.rem(inner, half)
+                label_ref[count] = jnp.where(apart == 0, inner, apart * shard + crossed)
+
+            return count + match.astype(jnp.int32)
+
+        return lax.fori_loop(0, tile_dev, one, count)
+
+    count = scan(own_tiles, lambda i: row_ref[i], lambda i: k_ref[i], 0)
+    count = scan(sib_tiles, lambda i: sib_ref[0, i], lambda i: sib_ref[1, i], count)
+    count_ref[0] = count
+    for i in range(UNROLL):
+        plane_ref[count + i] = sums
+        line_ref[count + i] = sums
+        label_ref[count + i] = 0
+
+    @pl.loop(0, count)
     def _(i):
         copy(own_tiles, 0, i).wait()
 
@@ -158,7 +193,7 @@
     def _(i):
         sums[i] = jnp.zeros(sums.shape[1:], jnp.float32)
 
-    @pl.loop(0, (count_ref[1] + UNROLL - 1) // UNROLL)
+    @pl.loop(0, lax.div(count_ref[0] + UNROLL - 1, UNROLL))
     def _(i):
         found = [
             jnp.dot(
@@ -280,13 +315,6 @@
     return pl.CostEstimate(flops=flops, bytes_accessed=moved, transcendentals=0)
 
 
-def compact(match, values):
-    count = -(-match.shape[0] // UNROLL) * UNROLL
-    rank = jnp.cumsum(match.astype(jnp.int32)) - 1
-    hit = match & (rank == jnp.arange(count, dtype=jnp.int32)[:, None])
-    return [jnp.sum(jnp.where(hit, v, 0), axis=-1) for v in values]
-
-
 def sums_plan(tiles, contraction, row_tile, owner_map, panel):
     wide_count = lax.axis_size("wide")
     tile_dev, side = tiles.shape[0], tiles.shape[1]
@@ -295,8 +323,7 @@
     shard = rows // side
     chunks = columns // CHUNK
     sums = owner_map.shape[0] // 2
-    g, w = lax.axis_index("grp"), lax.axis_index("wide")
-    core = w % 2
+    core = lax.axis_index("wide") % 2
 
     def to_core(v):
         return lax.ppermute(v, "wide", [(i, i ^ 1) for i in range(wide_count)])
@@ -307,10 +334,8 @@
     def to_line(v, b):
         return lax.ppermute(v, "wide", [(i, i ^ (2 << b)) for i in range(wide_count)])
 
-    x, y, z = g % 2, g // 2, w // 2
-
-    labels = jnp.stack([row_tile, contraction])
-    both = jnp.stack([labels, to_core(labels)])
+
+    sib_labels = to_core(jnp.stack([row_tile, contraction]))
     sib_tiles = to_core(tiles)
 
     def own_half(source, j):
@@ -319,31 +344,8 @@
     mines = [own_half(panel, j) for j in range(chunks)]
     ways = [None, (1, 2), (2, 1)]
     firsts = [None] + [to_grp(mines[j], ways[j][0]) for j in range(1, chunks)]
-    mine, both = lax.optimization_barrier((mines[0], both))
+    mine, sib_labels = lax.optimization_barrier((mines[0], sib_labels))
     near = [to_grp(mine, 1), to_grp(mine, 2), to_grp(mines[0], 3)]
-
-    table_ids = jnp.arange(owner_map.shape[0], dtype=jnp.int32)
-    position = jnp.sum(jnp.where(both[:, 0, :, None] == table_ids, owner_map, 0), axis=-1)
-    owner, local = position // out_dev, position % out_dev
-    to_z, odd = owner // 4, (owner // 2) % 2
-    bit_x, bit_y = local % 2, local // 2
-    first = jnp.where(odd == 1, bit_y == y, bit_x == x)
-    second = jnp.where(odd == 1, bit_x, bit_y)
-    in_plane = jnp.where(first, 0, sums // 2) + odd * (sums // 4) + 2 * to_z + second
-    in_line = jnp.where(odd == z % 2, 0, sums // 2) + to_z * out_dev + local
-    k = both[:, 1]
-    apart, inner = (k // shard) ^ g, k % shard
-    half = shard // 2
-    crossed = jnp.where(inner // half == core, 0, half) + inner % half
-    label = jnp.where(apart == 0, inner, apart * shard + crossed)
-    match = (owner % 2 == core).reshape(-1)
-    entries = [v.reshape(-1) for v in (in_plane, in_line, label)]
-    serial = jnp.arange(match.shape[0], dtype=jnp.int32)
-    source, in_plane, in_line, label = compact(match, [serial, *entries])
-    counts = jnp.stack([jnp.sum(match[:tile_dev]), jnp.sum(match)]).astype(jnp.int32)
-    beyond = jnp.arange(source.shape[0], dtype=jnp.int32) >= counts[1]
-    in_plane = jnp.where(beyond, sums, in_plane)
-    in_line = jnp.where(beyond, sums, in_line)
 
     half, quarter = sums // 2, sums // 4
     coded = shape((side + CODE_ROWS, CHUNK), jnp.int16)
@@ -373,10 +375,6 @@
         )(in_order(), *args)
         last = done[0]
         return done
-
-    counts, source, in_plane, in_line, label = lax.optimization_barrier(
-        (counts, source, in_plane, in_line, label)
-    )
 
     def places(operand, tiles_of, first):
         return [
@@ -448,18 +446,25 @@
         )[0]
 
     eighth = quarter // 2
-    pairs = {j: pair(j) for j in (1, 2)}
-    (held,) = call(
+    entries = shape((2 * tile_dev + UNROLL,), jnp.int32)
+    counts, in_plane, in_line, label, held = call(
         hold_kernel,
         "hold",
-        [pltpu.VMEM((2 * tile_dev, side, side), tiles.dtype)],
-        counts,
-        source,
+        [shape((1,), jnp.int32)]
+        + [entries] * 3
+        + [pltpu.VMEM((2 * tile_dev + UNROLL, side, side), tiles.dtype)],
+        row_tile,
+        contraction,
+        sib_labels,
+        owner_map,
         *[pltpu.with_memory_space_constraint(v, pltpu.HBM) for v in (tiles, sib_tiles)],
-        in_specs=in_any(1) + in_smem(2) + in_any(2),
+        in_specs=in_any(1) + in_smem(4) + in_any(2),
+        out_specs=in_smem(4) + in_vmem(1),
         extra=[pltpu.SemaphoreType.DMA((2 * tile_dev,))],
         mib=8,
     )
+    last = held
+    pairs = {j: pair(j) for j in (1, 2)}
 
     send, keep_0 = products(0, in_line, [stack_of(half, coded)], *join(0))
     sent_0 = send
@@ -499,10 +504,10 @@
     *sent[1], keep[1] = plane(1)
     *sent[2], keep[2] = plane(2)
     sent[1], keep[1] = owner(1)
+    sent[2], keep[2] = owner(2)
     *sends, keep_0 = call(
         rows_kernel, "rows", [coded] * 3 + [plain], to_line(sent_0, 1), keep_0
     )
-    sent[2], keep[2] = owner(2)
     (done_0,) = call(
         finish_rows_kernel,
         "finish_rows",

time: 126 us -> 122 us (0.968); the launches traced: 126 us -> 120 us
  starting transfers between devices: 59.4 us -> 44.6 us
  Pallas kernels: 15.2 us -> 29.7 us
  other arithmetic: 5.26 us -> 0.68 us
  waiting for transfers between devices: 44 us -> 41.5 us
  local copies, waits for them, and re-layouts: 1.47 us -> 3.14 us
    pallas_call x21, Pallas kernels: 15.2 us -> 29.7 us  [call(): pl.pallas_call(body, in_specs=more.pop('in_specs', in_any(1) + in_smem(sm...]
    ppermute x27, starting transfers between devices: 41.7 us -> 33.6 us  [to_grp(): return lax.ppermute(v, 'grp', [(i, i ^ d) for i in range(4)])]
    ppermute x7, starting transfers between devices: 5.78 us -> 1.42 us  [to_core(): return lax.ppermute(v, 'wide', [(i, i ^ 1) for i in range(wide_count)])]
    ppermute x6, waiting for transfers between devices: 9.09 us -> 6.43 us  [to_line(): return lax.ppermute(v, 'wide', [(i, i ^ 2 << b) for i in range(wide_count)])]
    ppermute x6, starting transfers between devices: 11.9 us -> 9.58 us  [to_line(): return lax.ppermute(v, 'wide', [(i, i ^ 2 << b) for i in range(wide_count)])]
    reduce_sum x4 -> x0, other arithmetic: 2.21 us -> none  [the longest x1 0.74 us: sums_plan(): jnp.sum(jnp.where(both[:, 0, :, None] == table_ids, owner_map, 0), axis=-1)]
    unnamed x2 -> x8, local copies, waits for them, and re-layouts: 0.01 us -> 1.97 us
    another operation x4 -> x1, other arithmetic: 2.17 us -> 0.68 us  [sums_plan(): sib_labels = to_core(jnp.stack([row_tile, contraction]))]
  transfers between devices with their start and end apart: 40 -> 40, of which waited for: 17 -> 21; matrix products, arithmetic and copies ran while one was open for 5% -> 2% of each run, Pallas kernels for 11% -> 24%
where the time goes in v2:
time: 122 us; the launch traced here: 120 us
  starting transfers between devices  44.6 us (37%)
  waiting for transfers between devices  41.5 us (34%)
  Pallas kernels  29.7 us (24%)
  local copies, waits for them, and re-layouts  3.14 us (3%)
    ppermute x27, starting transfers between devices, to_grp(): return lax.ppermute(v, 'grp', [(i, i ^ d) for i in range(4)])  33.6 us
    ppermute x27, waiting for transfers between devices, to_grp(): return lax.ppermute(v, 'grp', [(i, i ^ d) for i in range(4)])  31 us
    pallas_call x21, Pallas kernels, call(): pl.pallas_call(body, in_specs=more.pop('in_specs', in_any(1) + in_smem(sm...  29.7 us
    ppermute x6, starting transfers between devices, to_line(): return lax.ppermute(v, 'wide', [(i, i ^ 2 << b) for i in range(wide_count)])  9.58 us
    ppermute x6, waiting for transfers between devices, to_line(): return lax.ppermute(v, 'wide', [(i, i ^ 2 << b) for i in range(wide_count)])  6.43 us
    ppermute x7, waiting for transfers between devices, to_core(): return lax.ppermute(v, 'wide', [(i, i ^ 1) for i in range(wide_count)])  4.06 us
  transfers between devices with their start and end apart: 40, of which 21 were waited for; matrix products, arithmetic and copies ran while one was open for 2% of the time, Pallas kernels for 24%

profile of v2, /device:TPU:0, one launch (start us, length us, event | category | flops | bytes accessed | tf_op | source)
XLA Modules:
  0.0 119.9 jit_solution(1661741814792986933)
XLA Ops:
  2.4 3.0 %collective-permute-start.2 = (bf16[512,256]{1,0:T(8,128)(2,1)S(1)}, bf16[512,256]{1,0:T(8,128)(2,1)S(1)}, u32[]{:S(2)}, u32[]{:S(2)}) collective-permute-start(bf16[512,256]{1,0:T(8,128)(2,1)S(1)} %get-tuple-element.116.refs_0_), channel_id=1, source_target_pairs={{0,8},{8,0},{16,24},{24,16},{1,9},{9,1},{17,25},{25,17},{2,10},{10... | collective-permute-start | bytes 786440 | tf_op jit(solution)/shard_map/ppermute | solution.py:332
  6.9 3.2 %collective-permute-done.sib_ref = s32[2,48]{1,0:T(2,128)S(1)} collective-permute-done((s32[2,48]{1,0:T(2,128)S(1)}, s32[2,48]{1,0:T(2,128)S(1)}, u32[]{:S(2)}, u32[]{:S(2)}) %collective-permute-start) | collective-permute-done | bytes 416 | tf_op jit(solution)/shard_map/ppermute | solution.py:329
  10.1 2.6 %collective-permute-start.5 = (bf16[512,256]{1,0:T(8,128)(2,1)S(1)}, bf16[512,256]{1,0:T(8,128)(2,1)S(1)}, u32[]{:S(2)}, u32[]{:S(2)}) collective-permute-start(bf16[512,256]{1,0:T(8,128)(2,1)S(1)} %get-tuple-element.65), channel_id=1, source_target_pairs={{0,16},{8,24},{16,0},{24,8},{1,17},{9,25},{17,1},{25,9},{2,18},{10... | collective-permute-start | bytes 786440 | tf_op jit(solution)/shard_map/ppermute | solution.py:332
  16.2 6.9 %hold.1 = (s32[1]{0:T(128)}, s32[104]{0:T(128)S(1)}, s32[104]{0:T(128)S(1)}, s32[104]{0:T(128)S(1)}, bf16[104,256,256]{2,1,0:T(8,128)(2,1)S(1)}) custom-call(s32[1]{0:T(128)} %constant.8.clone.1.order, s32[48]{0:T(128)S(1)} %copy-done.1, s32[48]{0:T(128)S(1)} %copy-done.2, s32[2,48]{1,0:T(2,128)S(1)} %collective-permute-done.sib_ref, s32[32]{0:T(128)S(1)} %copy-done.3, ...), custom_call_target="tpu_custom_call" | custom-call | bytes 12583808 | tf_op jit(solution)/shard_map/hold/pallas_call | solution.py:365
  27.0 5.4 %products.3 = (s16[8,272,256]{2,1,0:T(8,128)(2,1)S(1)}, f32[17,256,256]{2,1,0:T(8,128)S(1)}) custom-call(s32[1]{0:T(128)} %constant.8.clone.1.order, s32[1]{0:T(128)} %get-tuple-element.67.count_ref, s32[104]{0:T(128)S(1)} %get-tuple-element.68.slot_ref, s32[104]{0:T(128)S(1)} %get-tuple-element.69.label_ref, ...), custom_call_target="tpu_custom_call" | custom-call | bytes 16778052 | tf_op jit(solution)/shard_map/products/pallas_call | solution.py:365
  33.9 5.1 %collective-permute-done.9.refs_2_ = bf16[1024,256]{1,0:T(8,128)(2,1)S(1)} collective-permute-done((bf16[1024,256]{1,0:T(8,128)(2,1)S(1)}, bf16[1024,256]{1,0:T(8,128)(2,1)S(1)}, u32[]{:S(2)}, u32[]{:S(2)}) %collective-permute-start.9) | collective-permute-done | bytes 524320 | tf_op jit(solution)/shard_map/ppermute | solution.py:332
  41.0 5.4 %products.4 = (s16[4,272,256]{2,1,0:T(8,128)(2,1)S(1)}, s16[4,272,256]{2,1,0:T(8,128)(2,1)S(1)}, f32[17,256,256]{2,1,0:T(8,128)S(1)}) custom-call(s32[1]{0:T(128)} %constant.8.clone.1.order, s32[1]{0:T(128)} %get-tuple-element.67.count_ref, s32[104]{0:T(128)S(1)} %get-tuple-element.72.slot_ref, s32[104]{0:T(128)S(1)} %get-tuple-element.69.label_ref, ...), custom_call_target="tpu_custom_call" | custom-call | bytes 17302340 | tf_op jit(solution)/shard_map/products/pallas_call | solution.py:365
  46.4 2.1 %collective-permute-start.16 = (s16[4,272,256]{2,1,0:T(8,128)(2,1)S(1)}, s16[4,272,256]{2,1,0:T(8,128)(2,1)S(1)}, u32[]{:S(2)}, u32[]{:S(2)}) collective-permute-start(s16[4,272,256]{2,1,0:T(8,128)(2,1)S(1)} %get-tuple-element.80), channel_id=1, source_target_pairs={{0,16},{8,24},{16,0},{24,8},{1,17},{9,25},{17,1},{25,9},{2,18},{10... | collective-permute-start | bytes 1671176 | tf_op jit(solution)/shard_map/ppermute | solution.py:332
  48.5 5.4 %products.5 = (s16[4,272,256]{2,1,0:T(8,128)(2,1)S(1)}, s16[4,272,256]{2,1,0:T(8,128)(2,1)S(1)}, f32[17,256,256]{2,1,0:T(8,128)S(1)}) custom-call(s32[1]{0:T(128)} %constant.8.clone.1.order, s32[1]{0:T(128)} %get-tuple-element.67.count_ref, s32[104]{0:T(128)S(1)} %get-tuple-element.72.slot_ref, s32[104]{0:T(128)S(1)} %get-tuple-element.69.label_ref, ...), custom_call_target="tpu_custom_call" | custom-call | bytes 17302340 | tf_op jit(solution)/shard_map/products/pallas_call | solution.py:365
  54.0 1.7 %collective-permute-start.18 = (s16[4,272,256]{2,1,0:T(8,128)(2,1)S(1)}, s16[4,272,256]{2,1,0:T(8,128)(2,1)S(1)}, u32[]{:S(2)}, u32[]{:S(2)}) collective-permute-start(s16[4,272,256]{2,1,0:T(8,128)(2,1)S(1)} %get-tuple-element.84), channel_id=1, source_target_pairs={{0,16},{8,24},{16,0},{24,8},{1,17},{9,25},{17,1},{25,9},{2,18},{10... | collective-permute-start | bytes 1671176 | tf_op jit(solution)/shard_map/ppermute | solution.py:332
  56.1 2.9 %collective-permute-done.14.recv = s16[8,272,256]{2,1,0:T(8,128)(2,1)S(1)} collective-permute-done((s16[8,272,256]{2,1,0:T(8,128)(2,1)S(1)}, s16[8,272,256]{2,1,0:T(8,128)(2,1)S(1)}, u32[]{:S(2)}, u32[]{:S(2)}) %collective-permute-start.14) | collective-permute-done | bytes 1114144 | tf_op jit(solution)/shard_map/ppermute | solution.py:335
  59.5 2.3 %collective-permute-start.23 = (s16[4,272,256]{2,1,0:T(8,128)(2,1)S(1)}, s16[4,272,256]{2,1,0:T(8,128)(2,1)S(1)}, u32[]{:S(2)}, u32[]{:S(2)}) collective-permute-start(s16[4,272,256]{2,1,0:T(8,128)(2,1)S(1)} %get-tuple-element.78), channel_id=1, source_target_pairs={{0,4},{1,5},{2,6},{3,7},{4,0},{5,1},{6,2},{7,3},{8,12},{9,13},{10,... | collective-permute-start | bytes 1671176 | tf_op jit(solution)/shard_map/ppermute | solution.py:335
  62.0 2.0 %collective-permute-done.15.recv_a = s16[4,272,256]{2,1,0:T(8,128)(2,1)S(1)} collective-permute-done((s16[4,272,256]{2,1,0:T(8,128)(2,1)S(1)}, s16[4,272,256]{2,1,0:T(8,128)(2,1)S(1)}, u32[]{:S(2)}, u32[]{:S(2)}) %collective-permute-start.15) | collective-permute-done | bytes 557088 | tf_op jit(solution)/shard_map/ppermute | solution.py:332
  65.9 8.0 %collective-permute-done.18.recv_b = s16[4,272,256]{2,1,0:T(8,128)(2,1)S(1)} collective-permute-done((s16[4,272,256]{2,1,0:T(8,128)(2,1)S(1)}, s16[4,272,256]{2,1,0:T(8,128)(2,1)S(1)}, u32[]{:S(2)}, u32[]{:S(2)}) %collective-permute-start.18) | collective-permute-done | bytes 557088 | tf_op jit(solution)/shard_map/ppermute | solution.py:332
  73.9 2.0 %collective-permute-done.17.recv_a = s16[4,272,256]{2,1,0:T(8,128)(2,1)S(1)} collective-permute-done((s16[4,272,256]{2,1,0:T(8,128)(2,1)S(1)}, s16[4,272,256]{2,1,0:T(8,128)(2,1)S(1)}, u32[]{:S(2)}, u32[]{:S(2)}) %collective-permute-start.17) | collective-permute-done | bytes 557088 | tf_op jit(solution)/shard_map/ppermute | solution.py:332
  77.9 4.0 %collective-permute-done.20.recv_b = s16[2,272,256]{2,1,0:T(8,128)(2,1)S(1)} collective-permute-done((s16[2,272,256]{2,1,0:T(8,128)(2,1)S(1)}, s16[2,272,256]{2,1,0:T(8,128)(2,1)S(1)}, u32[]{:S(2)}, u32[]{:S(2)}) %collective-permute-start.20) | collective-permute-done | bytes 278560 | tf_op jit(solution)/shard_map/ppermute | solution.py:332
  83.3 2.0 %collective-permute-done.22.recv_b = s16[2,272,256]{2,1,0:T(8,128)(2,1)S(1)} collective-permute-done((s16[2,272,256]{2,1,0:T(8,128)(2,1)S(1)}, s16[2,272,256]{2,1,0:T(8,128)(2,1)S(1)}, u32[]{:S(2)}, u32[]{:S(2)}) %collective-permute-start.22) | collective-permute-done | bytes 278560 | tf_op jit(solution)/shard_map/ppermute | solution.py:332
  88.1 2.0 %collective-permute-start.24 = (s16[272,256]{1,0:T(8,128)(2,1)S(1)}, s16[272,256]{1,0:T(8,128)(2,1)S(1)}, u32[]{:S(2)}, u32[]{:S(2)}) collective-permute-start(s16[272,256]{1,0:T(8,128)(2,1)S(1)} %get-tuple-element.97), channel_id=1, source_target_pairs={{0,8},{8,0},{16,24},{24,16},{1,9},{9,1},{17,25},{25,17},{2,10},{10... | collective-permute-start | bytes 417800 | tf_op jit(solution)/shard_map/ppermute | solution.py:332
  90.0 2.0 %collective-permute-start.28 = (s16[2,272,256]{2,1,0:T(8,128)(2,1)S(1)}, s16[2,272,256]{2,1,0:T(8,128)(2,1)S(1)}, u32[]{:S(2)}, u32[]{:S(2)}) collective-permute-start(s16[2,272,256]{2,1,0:T(8,128)(2,1)S(1)} %get-tuple-element.94), channel_id=1, source_target_pairs={{0,2},{1,3},{2,0},{3,1},{4,6},{5,7},{6,4},{7,5},{8,10},{9,11},{10,... | collective-permute-start | bytes 835592 | tf_op jit(solution)/shard_map/ppermute | solution.py:335
  92.4 1.6 %collective-permute-done.26.refs_2_ = s16[272,256]{1,0:T(8,128)(2,1)S(1)} collective-permute-done((s16[272,256]{1,0:T(8,128)(2,1)S(1)}, s16[272,256]{1,0:T(8,128)(2,1)S(1)}, u32[]{:S(2)}, u32[]{:S(2)}) %collective-permute-start.26) | collective-permute-done | bytes 139296 | tf_op jit(solution)/shard_map/ppermute | solution.py:332
  95.0 2.1 %collective-permute-start.29 = (s16[1,272,256]{2,1,0:T(8,128)(2,1)S(1)}, s16[1,272,256]{2,1,0:T(8,128)(2,1)S(1)}, u32[]{:S(2)}, u32[]{:S(2)}) collective-permute-start(s16[1,272,256]{2,1,0:T(8,128)(2,1)S(1)} %get-tuple-element.104), channel_id=1, source_target_pairs={{0,4},{1,5},{2,6},{3,7},{4,0},{5,1},{6,2},{7,3},{8,12},{9,13},{10,... | collective-permute-start | bytes 417800 | tf_op jit(solution)/shard_map/ppermute | solution.py:335
  101.7 3.0 %collective-permute-done.29.recv = s16[1,272,256]{2,1,0:T(8,128)(2,1)S(1)} collective-permute-done((s16[1,272,256]{2,1,0:T(8,128)(2,1)S(1)}, s16[1,272,256]{2,1,0:T(8,128)(2,1)S(1)}, u32[]{:S(2)}, u32[]{:S(2)}) %collective-permute-start.29) | collective-permute-done | bytes 139296 | tf_op jit(solution)/shard_map/ppermute | solution.py:335
  104.7 3.5 %collective-permute-start.36 = (s16[272,256]{1,0:T(8,128)(2,1)S(1)}, s16[272,256]{1,0:T(8,128)(2,1)S(1)}, u32[]{:S(2)}, u32[]{:S(2)}) collective-permute-start(s16[272,256]{1,0:T(8,128)(2,1)S(1)} %finish.2.refs_0_), channel_id=1, source_target_pairs={{0,24},{8,16},{16,8},{24,0},{1,25},{9,17},{17,9},{25,1},{2,26},{10... | collective-permute-start | bytes 417800 | tf_op jit(solution)/shard_map/ppermute | solution.py:332
  110.1 2.9 %collective-permute-start.39 = (s16[272,256]{1,0:T(8,128)(2,1)S(1)}, s16[272,256]{1,0:T(8,128)(2,1)S(1)}, u32[]{:S(2)}, u32[]{:S(2)}) collective-permute-start(s16[272,256]{1,0:T(8,128)(2,1)S(1)} %finish.3.refs_0_), channel_id=1, source_target_pairs={{0,24},{8,16},{16,8},{24,0},{1,25},{9,17},{17,9},{25,1},{2,26},{10... | collective-permute-start | bytes 417800 | tf_op jit(solution)/shard_map/ppermute | solution.py:332
  (87 shorter events, 38.3 us)
Async XLA Ops:
  0.0 12.8 %collective-permute-start.1 = (bf16[48,256,256]{2,1,0:T(8,128)(2,1)}, bf16[48,256,256]{2,1,0:T(8,128)(2,1)}, u32[]{:S(2)}, u32[]{:S(2)}) collective-permute-start(bf16[48,256,256]{2,1,0:T(8,128)(2,1)} %own_tiles.1), channel_id=1, source_target_pairs={{0,1},{1,0},{2,3},{3,2},{4,5},{5,4},{6,7},{7,6},{8,9},{9,8},{10,11... | collective-permute-start | bytes 18874376 | tf_op jit(solution)/shard_map/ppermute | solution.py:329
  2.4 20.7 %collective-permute-start.2 = (bf16[512,256]{1,0:T(8,128)(2,1)S(1)}, bf16[512,256]{1,0:T(8,128)(2,1)S(1)}, u32[]{:S(2)}, u32[]{:S(2)}) collective-permute-start(bf16[512,256]{1,0:T(8,128)(2,1)S(1)} %get-tuple-element.116.refs_0_), channel_id=1, source_target_pairs={{0,8},{8,0},{16,24},{24,16},{1,9},{9,1},{17,25},{25,17},{2,10},{10... | collective-permute-start | bytes 786440 | tf_op jit(solution)/shard_map/ppermute | solution.py:332
  5.4 17.8 %collective-permute-start.3 = (bf16[512,256]{1,0:T(8,128)(2,1)S(1)}, bf16[512,256]{1,0:T(8,128)(2,1)S(1)}, u32[]{:S(2)}, u32[]{:S(2)}) collective-permute-start(bf16[512,256]{1,0:T(8,128)(2,1)S(1)} %get-tuple-element.115.refs_0_), channel_id=1, source_target_pairs={{0,16},{8,24},{16,0},{24,8},{1,17},{9,25},{17,1},{25,9},{2,18},{10... | collective-permute-start | bytes 786440 | tf_op jit(solution)/shard_map/ppermute | solution.py:332
  6.9 16.3 %collective-permute-start.6 = (bf16[512,256]{1,0:T(8,128)(2,1)S(1)}, bf16[512,256]{1,0:T(8,128)(2,1)S(1)}, u32[]{:S(2)}, u32[]{:S(2)}) collective-permute-start(bf16[512,256]{1,0:T(8,128)(2,1)S(1)} %get-tuple-element.65), channel_id=1, source_target_pairs={{0,24},{8,16},{16,8},{24,0},{1,25},{9,17},{17,9},{25,1},{2,26},{10... | collective-permute-start | bytes 786440 | tf_op jit(solution)/shard_map/ppermute | solution.py:332
  10.1 14.4 %collective-permute-start.5 = (bf16[512,256]{1,0:T(8,128)(2,1)S(1)}, bf16[512,256]{1,0:T(8,128)(2,1)S(1)}, u32[]{:S(2)}, u32[]{:S(2)}) collective-permute-start(bf16[512,256]{1,0:T(8,128)(2,1)S(1)} %get-tuple-element.65), channel_id=1, source_target_pairs={{0,16},{8,24},{16,0},{24,8},{1,17},{9,25},{17,1},{25,9},{2,18},{10... | collective-permute-start | bytes 786440 | tf_op jit(solution)/shard_map/ppermute | solution.py:332
  12.8 11.8 %collective-permute-start.4 = (bf16[512,256]{1,0:T(8,128)(2,1)S(1)}, bf16[512,256]{1,0:T(8,128)(2,1)S(1)}, u32[]{:S(2)}, u32[]{:S(2)}) collective-permute-start(bf16[512,256]{1,0:T(8,128)(2,1)S(1)} %get-tuple-element.65), channel_id=1, source_target_pairs={{0,8},{8,0},{16,24},{24,16},{1,9},{9,1},{17,25},{25,17},{2,10},{10... | collective-permute-start | bytes 786440 | tf_op jit(solution)/shard_map/ppermute | solution.py:332
  24.7 14.3 %collective-permute-start.9 = (bf16[1024,256]{1,0:T(8,128)(2,1)S(1)}, bf16[1024,256]{1,0:T(8,128)(2,1)S(1)}, u32[]{:S(2)}, u32[]{:S(2)}) collective-permute-start(bf16[1024,256]{1,0:T(8,128)(2,1)S(1)} %join.3.refs_0_), channel_id=1, source_target_pairs={{0,16},{8,24},{16,0},{24,8},{1,17},{9,25},{17,1},{25,9},{2,18},{10... | collective-permute-start | bytes 1572872 | tf_op jit(solution)/shard_map/ppermute | solution.py:332
  26.3 14.0 %collective-permute-start.12 = (bf16[1024,256]{1,0:T(8,128)(2,1)S(1)}, bf16[1024,256]{1,0:T(8,128)(2,1)S(1)}, u32[]{:S(2)}, u32[]{:S(2)}) collective-permute-start(bf16[1024,256]{1,0:T(8,128)(2,1)S(1)} %join.4.refs_0_), channel_id=1, source_target_pairs={{0,8},{8,0},{16,24},{24,16},{1,9},{9,1},{17,25},{25,17},{2,10},{10... | collective-permute-start | bytes 1572872 | tf_op jit(solution)/shard_map/ppermute | solution.py:332
  32.4 26.5 %collective-permute-start.14 = (s16[8,272,256]{2,1,0:T(8,128)(2,1)S(1)}, s16[8,272,256]{2,1,0:T(8,128)(2,1)S(1)}, u32[]{:S(2)}, u32[]{:S(2)}) collective-permute-start(s16[8,272,256]{2,1,0:T(8,128)(2,1)S(1)} %get-tuple-element.70), channel_id=1, source_target_pairs={{0,2},{1,3},{2,0},{3,1},{4,6},{5,7},{6,4},{7,5},{8,10},{9,11},{10,... | collective-permute-start | bytes 3342344 | tf_op jit(solution)/shard_map/ppermute | solution.py:335
  39.0 9.5 %collective-permute-start.11 = (bf16[1024,256]{1,0:T(8,128)(2,1)S(1)}, bf16[1024,256]{1,0:T(8,128)(2,1)S(1)}, u32[]{:S(2)}, u32[]{:S(2)}) collective-permute-start(bf16[1024,256]{1,0:T(8,128)(2,1)S(1)} %join.4.refs_0_), channel_id=1, source_target_pairs={{0,1},{1,0},{2,3},{3,2},{4,5},{5,4},{6,7},{7,6},{8,9},{9,8},{10,11... | collective-permute-start | bytes 1572872 | tf_op jit(solution)/shard_map/ppermute | solution.py:329
  46.4 15.6 %collective-permute-start.16 = (s16[4,272,256]{2,1,0:T(8,128)(2,1)S(1)}, s16[4,272,256]{2,1,0:T(8,128)(2,1)S(1)}, u32[]{:S(2)}, u32[]{:S(2)}) collective-permute-start(s16[4,272,256]{2,1,0:T(8,128)(2,1)S(1)} %get-tuple-element.80), channel_id=1, source_target_pairs={{0,16},{8,24},{16,0},{24,8},{1,17},{9,25},{17,1},{25,9},{2,18},{10... | collective-permute-start | bytes 1671176 | tf_op jit(solution)/shard_map/ppermute | solution.py:332
  48.5 15.6 %collective-permute-start.15 = (s16[4,272,256]{2,1,0:T(8,128)(2,1)S(1)}, s16[4,272,256]{2,1,0:T(8,128)(2,1)S(1)}, u32[]{:S(2)}, u32[]{:S(2)}) collective-permute-start(s16[4,272,256]{2,1,0:T(8,128)(2,1)S(1)} %get-tuple-element.73), channel_id=1, source_target_pairs={{0,8},{8,0},{16,24},{24,16},{1,9},{9,1},{17,25},{25,17},{2,10},{10... | collective-permute-start | bytes 1671176 | tf_op jit(solution)/shard_map/ppermute | solution.py:332
  54.0 20.0 %collective-permute-start.18 = (s16[4,272,256]{2,1,0:T(8,128)(2,1)S(1)}, s16[4,272,256]{2,1,0:T(8,128)(2,1)S(1)}, u32[]{:S(2)}, u32[]{:S(2)}) collective-permute-start(s16[4,272,256]{2,1,0:T(8,128)(2,1)S(1)} %get-tuple-element.84), channel_id=1, source_target_pairs={{0,16},{8,24},{16,0},{24,8},{1,17},{9,25},{17,1},{25,9},{2,18},{10... | collective-permute-start | bytes 1671176 | tf_op jit(solution)/shard_map/ppermute | solution.py:332
  55.7 20.2 %collective-permute-start.17 = (s16[4,272,256]{2,1,0:T(8,128)(2,1)S(1)}, s16[4,272,256]{2,1,0:T(8,128)(2,1)S(1)}, u32[]{:S(2)}, u32[]{:S(2)}) collective-permute-start(s16[4,272,256]{2,1,0:T(8,128)(2,1)S(1)} %get-tuple-element.75), channel_id=1, source_target_pairs={{0,8},{8,0},{16,24},{24,16},{1,9},{9,1},{17,25},{25,17},{2,10},{10... | collective-permute-start | bytes 1671176 | tf_op jit(solution)/shard_map/ppermute | solution.py:332
  59.5 26.7 %collective-permute-start.23 = (s16[4,272,256]{2,1,0:T(8,128)(2,1)S(1)}, s16[4,272,256]{2,1,0:T(8,128)(2,1)S(1)}, u32[]{:S(2)}, u32[]{:S(2)}) collective-permute-start(s16[4,272,256]{2,1,0:T(8,128)(2,1)S(1)} %get-tuple-element.78), channel_id=1, source_target_pairs={{0,4},{1,5},{2,6},{3,7},{4,0},{5,1},{6,2},{7,3},{8,12},{9,13},{10,... | collective-permute-start | bytes 1671176 | tf_op jit(solution)/shard_map/ppermute | solution.py:335
  64.6 17.3 %collective-permute-start.20 = (s16[2,272,256]{2,1,0:T(8,128)(2,1)S(1)}, s16[2,272,256]{2,1,0:T(8,128)(2,1)S(1)}, u32[]{:S(2)}, u32[]{:S(2)}) collective-permute-start(s16[2,272,256]{2,1,0:T(8,128)(2,1)S(1)} %get-tuple-element.88), channel_id=1, source_target_pairs={{0,8},{8,0},{16,24},{24,16},{1,9},{9,1},{17,25},{25,17},{2,10},{10... | collective-permute-start | bytes 835592 | tf_op jit(solution)/shard_map/ppermute | solution.py:332
  64.7 17.2 %collective-permute-start.19 = (s16[2,272,256]{2,1,0:T(8,128)(2,1)S(1)}, s16[2,272,256]{2,1,0:T(8,128)(2,1)S(1)}, u32[]{:S(2)}, u32[]{:S(2)}) collective-permute-start(s16[2,272,256]{2,1,0:T(8,128)(2,1)S(1)} %get-tuple-element.82), channel_id=1, source_target_pairs={{0,16},{8,24},{16,0},{24,8},{1,17},{9,25},{17,1},{25,9},{2,18},{10... | collective-permute-start | bytes 835592 | tf_op jit(solution)/shard_map/ppermute | solution.py:332
  82.2 12.6 %collective-permute-start.27 = (s16[2,272,256]{2,1,0:T(8,128)(2,1)S(1)}, s16[2,272,256]{2,1,0:T(8,128)(2,1)S(1)}, u32[]{:S(2)}, u32[]{:S(2)}) collective-permute-start(s16[2,272,256]{2,1,0:T(8,128)(2,1)S(1)} %get-tuple-element.90), channel_id=1, source_target_pairs={{0,2},{1,3},{2,0},{3,1},{4,6},{5,7},{6,4},{7,5},{8,10},{9,11},{10,... | collective-permute-start | bytes 835592 | tf_op jit(solution)/shard_map/ppermute | solution.py:335
  90.0 10.5 %collective-permute-start.28 = (s16[2,272,256]{2,1,0:T(8,128)(2,1)S(1)}, s16[2,272,256]{2,1,0:T(8,128)(2,1)S(1)}, u32[]{:S(2)}, u32[]{:S(2)}) collective-permute-start(s16[2,272,256]{2,1,0:T(8,128)(2,1)S(1)} %get-tuple-element.94), channel_id=1, source_target_pairs={{0,2},{1,3},{2,0},{3,1},{4,6},{5,7},{6,4},{7,5},{8,10},{9,11},{10,... | collective-permute-start | bytes 835592 | tf_op jit(solution)/shard_map/ppermute | solution.py:335
  95.0 9.7 %collective-permute-start.29 = (s16[1,272,256]{2,1,0:T(8,128)(2,1)S(1)}, s16[1,272,256]{2,1,0:T(8,128)(2,1)S(1)}, u32[]{:S(2)}, u32[]{:S(2)}) collective-permute-start(s16[1,272,256]{2,1,0:T(8,128)(2,1)S(1)} %get-tuple-element.104), channel_id=1, source_target_pairs={{0,4},{1,5},{2,6},{3,7},{4,0},{5,1},{6,2},{7,3},{8,12},{9,13},{10,... | collective-permute-start | bytes 417800 | tf_op jit(solution)/shard_map/ppermute | solution.py:335
  97.0 11.3 %collective-permute-start.32 = (s16[272,256]{1,0:T(8,128)(2,1)S(1)}, s16[272,256]{1,0:T(8,128)(2,1)S(1)}, u32[]{:S(2)}, u32[]{:S(2)}) collective-permute-start(s16[272,256]{1,0:T(8,128)(2,1)S(1)} %finish_rows.1.refs_0_), channel_id=1, source_target_pairs={{0,24},{8,16},{16,8},{24,0},{1,25},{9,17},{17,9},{25,1},{2,26},{10... | collective-permute-start | bytes 417800 | tf_op jit(solution)/shard_map/ppermute | solution.py:332
  98.0 10.8 %collective-permute-start.31 = (s16[272,256]{1,0:T(8,128)(2,1)S(1)}, s16[272,256]{1,0:T(8,128)(2,1)S(1)}, u32[]{:S(2)}, u32[]{:S(2)}) collective-permute-start(s16[272,256]{1,0:T(8,128)(2,1)S(1)} %finish_rows.1.refs_0_), channel_id=1, source_target_pairs={{0,16},{8,24},{16,0},{24,8},{1,17},{9,25},{17,1},{25,9},{2,18},{10... | collective-permute-start | bytes 417800 | tf_op jit(solution)/shard_map/ppermute | solution.py:332
  99.5 9.5 %collective-permute-start.30 = (s16[272,256]{1,0:T(8,128)(2,1)S(1)}, s16[272,256]{1,0:T(8,128)(2,1)S(1)}, u32[]{:S(2)}, u32[]{:S(2)}) collective-permute-start(s16[272,256]{1,0:T(8,128)(2,1)S(1)} %finish_rows.1.refs_0_), channel_id=1, source_target_pairs={{0,8},{8,0},{16,24},{24,16},{1,9},{9,1},{17,25},{25,17},{2,10},{10... | collective-permute-start | bytes 417800 | tf_op jit(solution)/shard_map/ppermute | solution.py:332
  100.7 9.3 %collective-permute-start.33 = (s16[1,272,256]{2,1,0:T(8,128)(2,1)S(1)}, s16[1,272,256]{2,1,0:T(8,128)(2,1)S(1)}, u32[]{:S(2)}, u32[]{:S(2)}) collective-permute-start(s16[1,272,256]{2,1,0:T(8,128)(2,1)S(1)} %get-tuple-element.107), channel_id=1, source_target_pairs={{0,4},{1,5},{2,6},{3,7},{4,0},{5,1},{6,2},{7,3},{8,12},{9,13},{10,... | collective-permute-start | bytes 417800 | tf_op jit(solution)/shard_map/ppermute | solution.py:335
  (20 other events, 111.6 us)

commit v3 on v2

--- a/solution.py
+++ b/solution.py
@@ -120,11 +120,11 @@
 
 
 def hold_kernel(
-    order, row_ref, k_ref, sib_ref, owner_ref, own_tiles, sib_tiles,
+    order, own_ref, sib_ref, own_tiles, sib_tiles,
     count_ref, plane_ref, line_ref, label_ref, out, sems,
 ):
     tile_dev = own_tiles.shape[0]
-    sums = owner_ref.shape[0] // 2
+    sums = (own_ref.shape[0] - 2 * tile_dev) // 2
     shard, out_dev = 4, 4
     x, y, z_low, _ = here()
     g, core = lax.axis_index("grp"), lax.axis_index("wide") % 2
@@ -132,9 +132,10 @@
     def copy(tiles, which, at):
         return pltpu.make_async_copy(tiles.at[which], out.at[at], sems.at[at])
 
-    def scan(tiles, row, k, count):
+    def scan(tiles, index_ref, count):
         def one(i, count):
-            position = owner_ref[row(i)]
+            position = own_ref[2 * tile_dev + index_ref[i]]
+            k = index_ref[tile_dev + i]
             owner, local = lax.div(position, out_dev), lax.rem(position, out_dev)
             match = lax.rem(owner, 2) == core
 
@@ -151,7 +152,7 @@
                 line_ref[count] = (
                     jnp.where(odd == z_low, 0, sums // 2) + to_z * out_dev + local
                 )
-                apart, inner = lax.div(k(i), shard) ^ g, lax.rem(k(i), shard)
+                apart, inner = lax.div(k, shard) ^ g, lax.rem(k, shard)
                 half = shard // 2
                 crossed = jnp.where(lax.div(inner, half) == core, 0, half) + lax.rem(inner, half)
                 label_ref[count] = jnp.where(apart == 0, inner, apart * shard + crossed)
@@ -160,8 +161,8 @@
 
         return lax.fori_loop(0, tile_dev, one, count)
 
-    count = scan(own_tiles, lambda i: row_ref[i], lambda i: k_ref[i], 0)
-    count = scan(sib_tiles, lambda i: sib_ref[0, i], lambda i: sib_ref[1, i], count)
+    count = scan(own_tiles, own_ref, 0)
+    count = scan(sib_tiles, sib_ref, count)
     count_ref[0] = count
     for i in range(UNROLL):
         plane_ref[count + i] = sums
@@ -180,12 +181,14 @@
         out[pl.ds(i * rows, rows), :] = part[...]
 
 
-def products_kernel(fill, order, count_ref, slot_ref, label_ref, tiles, own_panel, *refs):
+def products_kernel(
+    fill, chunk, order, count_ref, slot_ref, label_ref, tiles, own_panel, *refs
+):
     parts = refs[: 1 + max(which for which, _, _ in fill)]
     *sends, sums, stack = refs[len(parts) :]
-    side = tiles.shape[1]
+    side, width = stack.shape[1:]
     for t in range(own_panel.shape[0] // side):
-        stack[t] = own_panel[pl.ds(t * side, side), :]
+        stack[t] = own_panel[pl.ds(t * side, side), pl.ds(chunk * width, width)]
     for which, t, at in fill:
         stack[at] = parts[which][pl.ds(t * side, side), :]
 
@@ -335,7 +338,8 @@
         return lax.ppermute(v, "wide", [(i, i ^ (2 << b)) for i in range(wide_count)])
 
 
-    sib_labels = to_core(jnp.stack([row_tile, contraction]))
+    own_index = jnp.concatenate([row_tile, contraction, owner_map])
+    sib_index = to_core(own_index)
     sib_tiles = to_core(tiles)
 
     def own_half(source, j):
@@ -344,7 +348,7 @@
     mines = [own_half(panel, j) for j in range(chunks)]
     ways = [None, (1, 2), (2, 1)]
     firsts = [None] + [to_grp(mines[j], ways[j][0]) for j in range(1, chunks)]
-    mine, sib_labels = lax.optimization_barrier((mines[0], sib_labels))
+    mine, sib_index = lax.optimization_barrier((mines[0], sib_index))
     near = [to_grp(mine, 1), to_grp(mine, 2), to_grp(mines[0], 3)]
 
     half, quarter = sums // 2, sums // 4
@@ -408,7 +412,7 @@
 
     def products(j, slot, sends, fill, parts):
         *sends, kept = call(
-            functools.partial(products_kernel, tuple(fill)),
+            functools.partial(products_kernel, tuple(fill), j),
             "products",
             [*sends, stack_of(sums + 1, plain)],
             counts,
@@ -417,12 +421,7 @@
             held,
             panel,
             *parts,
-            grid=(1,),
-            in_specs=in_any(1)
-            + in_smem(3)
-            + in_vmem(1)
-            + [pl.BlockSpec((rows, CHUNK), lambda i: (0, j))]
-            + in_vmem(len(parts)),
+            smem=3,
             extra=[pltpu.VMEM((4 * shard, side, CHUNK), panel.dtype)],
             mib=24,
         )
@@ -453,12 +452,10 @@
         [shape((1,), jnp.int32)]
         + [entries] * 3
         + [pltpu.VMEM((2 * tile_dev + UNROLL, side, side), tiles.dtype)],
-        row_tile,
-        contraction,
-        sib_labels,
-        owner_map,
+        own_index,
+        sib_index,
         *[pltpu.with_memory_space_constraint(v, pltpu.HBM) for v in (tiles, sib_tiles)],
-        in_specs=in_any(1) + in_smem(4) + in_any(2),
+        in_specs=in_any(1) + in_smem(2) + in_any(2),
         out_specs=in_smem(4) + in_vmem(1),
         extra=[pltpu.SemaphoreType.DMA((2 * tile_dev,))],
         mib=8,

time: 122 us -> 124 us (1.016); the launches traced: 120 us -> 124 us
  starting transfers between devices: 44.6 us -> 57 us
  Pallas kernels: 29.7 us -> 23.5 us
  local copies, waits for them, and re-layouts: 3.14 us -> 1.17 us
    ppermute x6, starting transfers between devices: 9.58 us -> 17.5 us  [to_line(): return lax.ppermute(v, 'wide', [(i, i ^ 2 << b) for i in range(wide_count)])]
    pallas_call x21, Pallas kernels: 29.7 us -> 23.5 us  [call(): pl.pallas_call(body, in_specs=more.pop('in_specs', in_any(1) + in_smem(sm...]
    ppermute x27, waiting for transfers between devices: 31 us -> 27.3 us  [to_grp(): return lax.ppermute(v, 'grp', [(i, i ^ d) for i in range(4)])]
    ppermute x6, waiting for transfers between devices: 6.43 us -> 9.83 us  [to_line(): return lax.ppermute(v, 'wide', [(i, i ^ 2 << b) for i in range(wide_count)])]
    ppermute x7, starting transfers between devices: 1.42 us -> 4.25 us  [to_core(): return lax.ppermute(v, 'wide', [(i, i ^ 1) for i in range(wide_count)])]
    unnamed x8 -> x2, local copies, waits for them, and re-layouts: 1.97 us -> 0.01 us
    ppermute x27, starting transfers between devices: 33.6 us -> 35.3 us  [to_grp(): return lax.ppermute(v, 'grp', [(i, i ^ d) for i in range(4)])]
  transfers between devices with their start and end apart: 40 -> 40, of which waited for: 21 -> 19; matrix products, arithmetic and copies ran while one was open for 2% -> 2% of each run, Pallas kernels for 24% -> 18%
where the time goes in v3:
time: 124 us
  starting transfers between devices  57 us (46%)
  waiting for transfers between devices  41 us (33%)
  Pallas kernels  23.5 us (19%)
    ppermute x27, starting transfers between devices, to_grp(): return lax.ppermute(v, 'grp', [(i, i ^ d) for i in range(4)])  35.3 us
    ppermute x27, waiting for transfers between devices, to_grp(): return lax.ppermute(v, 'grp', [(i, i ^ d) for i in range(4)])  27.3 us
    pallas_call x21, Pallas kernels, call(): pl.pallas_call(body, in_specs=more.pop('in_specs', in_any(1) + in_smem(sm...  23.5 us
    ppermute x6, starting transfers between devices, to_line(): return lax.ppermute(v, 'wide', [(i, i ^ 2 << b) for i in range(wide_count)])  17.5 us
    ppermute x6, waiting for transfers between devices, to_line(): return lax.ppermute(v, 'wide', [(i, i ^ 2 << b) for i in range(wide_count)])  9.83 us
    ppermute x7, starting transfers between devices, to_core(): return lax.ppermute(v, 'wide', [(i, i ^ 1) for i in range(wide_count)])  4.25 us
    ppermute x7, waiting for transfers between devices, to_core(): return lax.ppermute(v, 'wide', [(i, i ^ 1) for i in range(wide_count)])  3.95 us
  transfers between devices with their start and end apart: 40, of which 19 were waited for; matrix products, arithmetic and copies ran while one was open for 2% of the time, Pallas kernels for 18%

profile of v3, /device:TPU:0, one launch (start us, length us, event | category | flops | bytes accessed | tf_op | source)
XLA Modules:
  0.0 123.8 jit_solution(9523509523167368606)
XLA Ops:
  2.4 3.0 %collective-permute-start.2 = (bf16[512,256]{1,0:T(8,128)(2,1)S(1)}, bf16[512,256]{1,0:T(8,128)(2,1)S(1)}, u32[]{:S(2)}, u32[]{:S(2)}) collective-permute-start(bf16[512,256]{1,0:T(8,128)(2,1)S(1)} %get-tuple-element.116.refs_0_), channel_id=1, source_target_pairs={{0,8},{8,0},{16,24},{24,16},{1,9},{9,1},{17,25},{25,17},{2,10},{10... | collective-permute-start | bytes 786440 | tf_op jit(solution)/shard_map/ppermute | solution.py:335
  7.0 3.1 %collective-permute-done.sib_ref = s32[128]{0:T(128)S(1)} collective-permute-done((s32[128]{0:T(128)S(1)}, s32[128]{0:T(128)S(1)}, u32[]{:S(2)}, u32[]{:S(2)}) %collective-permute-start) | collective-permute-done | bytes 544 | tf_op jit(solution)/shard_map/ppermute | solution.py:332
  10.1 2.6 %collective-permute-start.5 = (bf16[512,256]{1,0:T(8,128)(2,1)S(1)}, bf16[512,256]{1,0:T(8,128)(2,1)S(1)}, u32[]{:S(2)}, u32[]{:S(2)}) collective-permute-start(bf16[512,256]{1,0:T(8,128)(2,1)S(1)} %get-tuple-element.65), channel_id=1, source_target_pairs={{0,16},{8,24},{16,0},{24,8},{1,17},{9,25},{17,1},{25,9},{2,18},{10... | collective-permute-start | bytes 786440 | tf_op jit(solution)/shard_map/ppermute | solution.py:335
  14.3 6.3 %hold.1 = (s32[1]{0:T(128)}, s32[104]{0:T(128)S(1)}, s32[104]{0:T(128)S(1)}, s32[104]{0:T(128)S(1)}, bf16[104,256,256]{2,1,0:T(8,128)(2,1)S(1)}) custom-call(s32[1]{0:T(128)} %constant.8.clone.1.order, s32[128]{0:T(128)S(1)} %pad_add_fusion.own_ref, s32[128]{0:T(128)S(1)} %collective-permute-done.sib_ref, bf16[48,256,256]{2,1,0:T(8,128)(2,1)} %own_tiles.1, ...), custom_call_target="tpu_custom_call" | custom-call | bytes 12583936 | tf_op jit(solution)/shard_map/hold/pallas_call | solution.py:369
  20.7 3.9 %collective-permute-done.5.refs_1_ = bf16[512,256]{1,0:T(8,128)(2,1)S(1)} collective-permute-done((bf16[512,256]{1,0:T(8,128)(2,1)S(1)}, bf16[512,256]{1,0:T(8,128)(2,1)S(1)}, u32[]{:S(2)}, u32[]{:S(2)}) %collective-permute-start.5) | collective-permute-done | bytes 262176 | tf_op jit(solution)/shard_map/ppermute | solution.py:335
  27.1 3.6 %products.3 = (s16[8,272,256]{2,1,0:T(8,128)(2,1)S(1)}, f32[17,256,256]{2,1,0:T(8,128)S(1)}) custom-call(s32[1]{0:T(128)} %constant.8.clone.1.order, s32[1]{0:T(128)} %get-tuple-element.67.count_ref, s32[104]{0:T(128)S(1)} %get-tuple-element.68.slot_ref, s32[104]{0:T(128)S(1)} %get-tuple-element.69.label_ref, ...), custom_call_target="tpu_custom_call" | custom-call | bytes 16778052 | tf_op jit(solution)/shard_map/products/pallas_call | solution.py:369
  32.3 3.2 %collective-permute-start.8 = (bf16[1024,256]{1,0:T(8,128)(2,1)S(1)}, bf16[1024,256]{1,0:T(8,128)(2,1)S(1)}, u32[]{:S(2)}, u32[]{:S(2)}) collective-permute-start(bf16[1024,256]{1,0:T(8,128)(2,1)S(1)} %join.3.refs_0_), channel_id=1, source_target_pairs={{0,1},{1,0},{2,3},{3,2},{4,5},{5,4},{6,7},{7,6},{8,9},{9,8},{10,11... | collective-permute-start | bytes 1572872 | tf_op jit(solution)/shard_map/ppermute | solution.py:332
  35.4 3.7 %collective-permute-done.9.refs_2_ = bf16[1024,256]{1,0:T(8,128)(2,1)S(1)} collective-permute-done((bf16[1024,256]{1,0:T(8,128)(2,1)S(1)}, bf16[1024,256]{1,0:T(8,128)(2,1)S(1)}, u32[]{:S(2)}, u32[]{:S(2)}) %collective-permute-start.9) | collective-permute-done | bytes 524320 | tf_op jit(solution)/shard_map/ppermute | solution.py:335
  41.0 3.6 %products.4 = (s16[4,272,256]{2,1,0:T(8,128)(2,1)S(1)}, s16[4,272,256]{2,1,0:T(8,128)(2,1)S(1)}, f32[17,256,256]{2,1,0:T(8,128)S(1)}) custom-call(s32[1]{0:T(128)} %constant.8.clone.1.order, s32[1]{0:T(128)} %get-tuple-element.67.count_ref, s32[104]{0:T(128)S(1)} %get-tuple-element.72.slot_ref, s32[104]{0:T(128)S(1)} %get-tuple-element.69.label_ref, ...), custom_call_target="tpu_custom_call" | custom-call | bytes 17302340 | tf_op jit(solution)/shard_map/products/pallas_call | solution.py:369
  46.7 3.6 %products.5 = (s16[4,272,256]{2,1,0:T(8,128)(2,1)S(1)}, s16[4,272,256]{2,1,0:T(8,128)(2,1)S(1)}, f32[17,256,256]{2,1,0:T(8,128)S(1)}) custom-call(s32[1]{0:T(128)} %constant.8.clone.1.order, s32[1]{0:T(128)} %get-tuple-element.67.count_ref, s32[104]{0:T(128)S(1)} %get-tuple-element.72.slot_ref, s32[104]{0:T(128)S(1)} %get-tuple-element.69.label_ref, ...), custom_call_target="tpu_custom_call" | custom-call | bytes 17302340 | tf_op jit(solution)/shard_map/products/pallas_call | solution.py:369
  52.4 3.4 %collective-permute-done.14.recv = s16[8,272,256]{2,1,0:T(8,128)(2,1)S(1)} collective-permute-done((s16[8,272,256]{2,1,0:T(8,128)(2,1)S(1)}, s16[8,272,256]{2,1,0:T(8,128)(2,1)S(1)}, u32[]{:S(2)}, u32[]{:S(2)}) %collective-permute-start.14) | collective-permute-done | bytes 1114144 | tf_op jit(solution)/shard_map/ppermute | solution.py:338
  56.3 5.6 %collective-permute-start.23 = (s16[4,272,256]{2,1,0:T(8,128)(2,1)S(1)}, s16[4,272,256]{2,1,0:T(8,128)(2,1)S(1)}, u32[]{:S(2)}, u32[]{:S(2)}) collective-permute-start(s16[4,272,256]{2,1,0:T(8,128)(2,1)S(1)} %get-tuple-element.78), channel_id=1, source_target_pairs={{0,4},{1,5},{2,6},{3,7},{4,0},{5,1},{6,2},{7,3},{8,12},{9,13},{10,... | collective-permute-start | bytes 1671176 | tf_op jit(solution)/shard_map/ppermute | solution.py:338
  64.7 5.1 %collective-permute-done.18.recv_b = s16[4,272,256]{2,1,0:T(8,128)(2,1)S(1)} collective-permute-done((s16[4,272,256]{2,1,0:T(8,128)(2,1)S(1)}, s16[4,272,256]{2,1,0:T(8,128)(2,1)S(1)}, u32[]{:S(2)}, u32[]{:S(2)}) %collective-permute-start.18) | collective-permute-done | bytes 557088 | tf_op jit(solution)/shard_map/ppermute | solution.py:335
  73.4 2.3 %collective-permute-start.21 = (s16[2,272,256]{2,1,0:T(8,128)(2,1)S(1)}, s16[2,272,256]{2,1,0:T(8,128)(2,1)S(1)}, u32[]{:S(2)}, u32[]{:S(2)}) collective-permute-start(s16[2,272,256]{2,1,0:T(8,128)(2,1)S(1)} %get-tuple-element.86), channel_id=1, source_target_pairs={{0,16},{8,24},{16,0},{24,8},{1,17},{9,25},{17,1},{25,9},{2,18},{10... | collective-permute-start | bytes 835592 | tf_op jit(solution)/shard_map/ppermute | solution.py:335
  77.6 5.8 %collective-permute-start.27 = (s16[2,272,256]{2,1,0:T(8,128)(2,1)S(1)}, s16[2,272,256]{2,1,0:T(8,128)(2,1)S(1)}, u32[]{:S(2)}, u32[]{:S(2)}) collective-permute-start(s16[2,272,256]{2,1,0:T(8,128)(2,1)S(1)} %get-tuple-element.90), channel_id=1, source_target_pairs={{0,2},{1,3},{2,0},{3,1},{4,6},{5,7},{6,4},{7,5},{8,10},{9,11},{10,... | collective-permute-start | bytes 835592 | tf_op jit(solution)/shard_map/ppermute | solution.py:338
  83.7 2.7 %collective-permute-done.23.recv = s16[4,272,256]{2,1,0:T(8,128)(2,1)S(1)} collective-permute-done((s16[4,272,256]{2,1,0:T(8,128)(2,1)S(1)}, s16[4,272,256]{2,1,0:T(8,128)(2,1)S(1)}, u32[]{:S(2)}, u32[]{:S(2)}) %collective-permute-start.23) | collective-permute-done | bytes 557088 | tf_op jit(solution)/shard_map/ppermute | solution.py:338
  86.7 2.6 %collective-permute-start.25 = (s16[272,256]{1,0:T(8,128)(2,1)S(1)}, s16[272,256]{1,0:T(8,128)(2,1)S(1)}, u32[]{:S(2)}, u32[]{:S(2)}) collective-permute-start(s16[272,256]{1,0:T(8,128)(2,1)S(1)} %get-tuple-element.99), channel_id=1, source_target_pairs={{0,16},{8,24},{16,0},{24,8},{1,17},{9,25},{17,1},{25,9},{2,18},{10... | collective-permute-start | bytes 417800 | tf_op jit(solution)/shard_map/ppermute | solution.py:335
  92.3 3.3 %collective-permute-done.25.refs_1_ = s16[272,256]{1,0:T(8,128)(2,1)S(1)} collective-permute-done((s16[272,256]{1,0:T(8,128)(2,1)S(1)}, s16[272,256]{1,0:T(8,128)(2,1)S(1)}, u32[]{:S(2)}, u32[]{:S(2)}) %collective-permute-start.25) | collective-permute-done | bytes 139296 | tf_op jit(solution)/shard_map/ppermute | solution.py:335
  97.9 2.3 %collective-permute-start.29 = (s16[1,272,256]{2,1,0:T(8,128)(2,1)S(1)}, s16[1,272,256]{2,1,0:T(8,128)(2,1)S(1)}, u32[]{:S(2)}, u32[]{:S(2)}) collective-permute-start(s16[1,272,256]{2,1,0:T(8,128)(2,1)S(1)} %get-tuple-element.104), channel_id=1, source_target_pairs={{0,4},{1,5},{2,6},{3,7},{4,0},{5,1},{6,2},{7,3},{8,12},{9,13},{10,... | collective-permute-start | bytes 417800 | tf_op jit(solution)/shard_map/ppermute | solution.py:338
  104.6 3.8 %collective-permute-done.29.recv = s16[1,272,256]{2,1,0:T(8,128)(2,1)S(1)} collective-permute-done((s16[1,272,256]{2,1,0:T(8,128)(2,1)S(1)}, s16[1,272,256]{2,1,0:T(8,128)(2,1)S(1)}, u32[]{:S(2)}, u32[]{:S(2)}) %collective-permute-start.29) | collective-permute-done | bytes 139296 | tf_op jit(solution)/shard_map/ppermute | solution.py:338
  108.5 2.0 %collective-permute-start.36 = (s16[272,256]{1,0:T(8,128)(2,1)S(1)}, s16[272,256]{1,0:T(8,128)(2,1)S(1)}, u32[]{:S(2)}, u32[]{:S(2)}) collective-permute-start(s16[272,256]{1,0:T(8,128)(2,1)S(1)} %finish.2.refs_0_), channel_id=1, source_target_pairs={{0,24},{8,16},{16,8},{24,0},{1,25},{9,17},{17,9},{25,1},{2,26},{10... | collective-permute-start | bytes 417800 | tf_op jit(solution)/shard_map/ppermute | solution.py:335
  113.2 2.0 %collective-permute-start.39 = (s16[272,256]{1,0:T(8,128)(2,1)S(1)}, s16[272,256]{1,0:T(8,128)(2,1)S(1)}, u32[]{:S(2)}, u32[]{:S(2)}) collective-permute-start(s16[272,256]{1,0:T(8,128)(2,1)S(1)} %finish.3.refs_0_), channel_id=1, source_target_pairs={{0,24},{8,16},{16,8},{24,0},{1,25},{9,17},{17,9},{25,1},{2,26},{10... | collective-permute-start | bytes 417800 | tf_op jit(solution)/shard_map/ppermute | solution.py:335
  116.8 2.1 %collective-permute-done.35.refs_2_ = s16[272,256]{1,0:T(8,128)(2,1)S(1)} collective-permute-done((s16[272,256]{1,0:T(8,128)(2,1)S(1)}, s16[272,256]{1,0:T(8,128)(2,1)S(1)}, u32[]{:S(2)}, u32[]{:S(2)}) %collective-permute-start.35) | collective-permute-done | bytes 139296 | tf_op jit(solution)/shard_map/ppermute | solution.py:335
  120.0 2.0 %collective-permute-done.39.refs_3_ = s16[272,256]{1,0:T(8,128)(2,1)S(1)} collective-permute-done((s16[272,256]{1,0:T(8,128)(2,1)S(1)}, s16[272,256]{1,0:T(8,128)(2,1)S(1)}, u32[]{:S(2)}, u32[]{:S(2)}) %collective-permute-start.39) | collective-permute-done | bytes 139296 | tf_op jit(solution)/shard_map/ppermute | solution.py:335
  (81 shorter events, 42.2 us)
Async XLA Ops:
  0.0 12.8 %collective-permute-start.1 = (bf16[48,256,256]{2,1,0:T(8,128)(2,1)}, bf16[48,256,256]{2,1,0:T(8,128)(2,1)}, u32[]{:S(2)}, u32[]{:S(2)}) collective-permute-start(bf16[48,256,256]{2,1,0:T(8,128)(2,1)} %own_tiles.1), channel_id=1, source_target_pairs={{0,1},{1,0},{2,3},{3,2},{4,5},{5,4},{6,7},{7,6},{8,9},{9,8},{10,11... | collective-permute-start | bytes 18874376 | tf_op jit(solution)/shard_map/ppermute | solution.py:332
  2.4 18.2 %collective-permute-start.2 = (bf16[512,256]{1,0:T(8,128)(2,1)S(1)}, bf16[512,256]{1,0:T(8,128)(2,1)S(1)}, u32[]{:S(2)}, u32[]{:S(2)}) collective-permute-start(bf16[512,256]{1,0:T(8,128)(2,1)S(1)} %get-tuple-element.116.refs_0_), channel_id=1, source_target_pairs={{0,8},{8,0},{16,24},{24,16},{1,9},{9,1},{17,25},{25,17},{2,10},{10... | collective-permute-start | bytes 786440 | tf_op jit(solution)/shard_map/ppermute | solution.py:335
  5.5 15.2 %collective-permute-start.3 = (bf16[512,256]{1,0:T(8,128)(2,1)S(1)}, bf16[512,256]{1,0:T(8,128)(2,1)S(1)}, u32[]{:S(2)}, u32[]{:S(2)}) collective-permute-start(bf16[512,256]{1,0:T(8,128)(2,1)S(1)} %get-tuple-element.115.refs_0_), channel_id=1, source_target_pairs={{0,16},{8,24},{16,0},{24,8},{1,17},{9,25},{17,1},{25,9},{2,18},{10... | collective-permute-start | bytes 786440 | tf_op jit(solution)/shard_map/ppermute | solution.py:335
  7.0 13.8 %collective-permute-start.6 = (bf16[512,256]{1,0:T(8,128)(2,1)S(1)}, bf16[512,256]{1,0:T(8,128)(2,1)S(1)}, u32[]{:S(2)}, u32[]{:S(2)}) collective-permute-start(bf16[512,256]{1,0:T(8,128)(2,1)S(1)} %get-tuple-element.65), channel_id=1, source_target_pairs={{0,24},{8,16},{16,8},{24,0},{1,25},{9,17},{17,9},{25,1},{2,26},{10... | collective-permute-start | bytes 786440 | tf_op jit(solution)/shard_map/ppermute | solution.py:335
  10.1 14.5 %collective-permute-start.5 = (bf16[512,256]{1,0:T(8,128)(2,1)S(1)}, bf16[512,256]{1,0:T(8,128)(2,1)S(1)}, u32[]{:S(2)}, u32[]{:S(2)}) collective-permute-start(bf16[512,256]{1,0:T(8,128)(2,1)S(1)} %get-tuple-element.65), channel_id=1, source_target_pairs={{0,16},{8,24},{16,0},{24,8},{1,17},{9,25},{17,1},{25,9},{2,18},{10... | collective-permute-start | bytes 786440 | tf_op jit(solution)/shard_map/ppermute | solution.py:335
  12.8 11.9 %collective-permute-start.4 = (bf16[512,256]{1,0:T(8,128)(2,1)S(1)}, bf16[512,256]{1,0:T(8,128)(2,1)S(1)}, u32[]{:S(2)}, u32[]{:S(2)}) collective-permute-start(bf16[512,256]{1,0:T(8,128)(2,1)S(1)} %get-tuple-element.65), channel_id=1, source_target_pairs={{0,8},{8,0},{16,24},{24,16},{1,9},{9,1},{17,25},{25,17},{2,10},{10... | collective-permute-start | bytes 786440 | tf_op jit(solution)/shard_map/ppermute | solution.py:335
  24.8 14.3 %collective-permute-start.9 = (bf16[1024,256]{1,0:T(8,128)(2,1)S(1)}, bf16[1024,256]{1,0:T(8,128)(2,1)S(1)}, u32[]{:S(2)}, u32[]{:S(2)}) collective-permute-start(bf16[1024,256]{1,0:T(8,128)(2,1)S(1)} %join.3.refs_0_), channel_id=1, source_target_pairs={{0,16},{8,24},{16,0},{24,8},{1,17},{9,25},{17,1},{25,9},{2,18},{10... | collective-permute-start | bytes 1572872 | tf_op jit(solution)/shard_map/ppermute | solution.py:335
  26.4 14.0 %collective-permute-start.12 = (bf16[1024,256]{1,0:T(8,128)(2,1)S(1)}, bf16[1024,256]{1,0:T(8,128)(2,1)S(1)}, u32[]{:S(2)}, u32[]{:S(2)}) collective-permute-start(bf16[1024,256]{1,0:T(8,128)(2,1)S(1)} %join.4.refs_0_), channel_id=1, source_target_pairs={{0,8},{8,0},{16,24},{24,16},{1,9},{9,1},{17,25},{25,17},{2,10},{10... | collective-permute-start | bytes 1572872 | tf_op jit(solution)/shard_map/ppermute | solution.py:335
  30.6 25.1 %collective-permute-start.14 = (s16[8,272,256]{2,1,0:T(8,128)(2,1)S(1)}, s16[8,272,256]{2,1,0:T(8,128)(2,1)S(1)}, u32[]{:S(2)}, u32[]{:S(2)}) collective-permute-start(s16[8,272,256]{2,1,0:T(8,128)(2,1)S(1)} %get-tuple-element.70), channel_id=1, source_target_pairs={{0,2},{1,3},{2,0},{3,1},{4,6},{5,7},{6,4},{7,5},{8,10},{9,11},{10,... | collective-permute-start | bytes 3342344 | tf_op jit(solution)/shard_map/ppermute | solution.py:338
  44.6 17.3 %collective-permute-start.16 = (s16[4,272,256]{2,1,0:T(8,128)(2,1)S(1)}, s16[4,272,256]{2,1,0:T(8,128)(2,1)S(1)}, u32[]{:S(2)}, u32[]{:S(2)}) collective-permute-start(s16[4,272,256]{2,1,0:T(8,128)(2,1)S(1)} %get-tuple-element.80), channel_id=1, source_target_pairs={{0,16},{8,24},{16,0},{24,8},{1,17},{9,25},{17,1},{25,9},{2,18},{10... | collective-permute-start | bytes 1671176 | tf_op jit(solution)/shard_map/ppermute | solution.py:335
  46.2 15.7 %collective-permute-start.15 = (s16[4,272,256]{2,1,0:T(8,128)(2,1)S(1)}, s16[4,272,256]{2,1,0:T(8,128)(2,1)S(1)}, u32[]{:S(2)}, u32[]{:S(2)}) collective-permute-start(s16[4,272,256]{2,1,0:T(8,128)(2,1)S(1)} %get-tuple-element.73), channel_id=1, source_target_pairs={{0,8},{8,0},{16,24},{24,16},{1,9},{9,1},{17,25},{25,17},{2,10},{10... | collective-permute-start | bytes 1671176 | tf_op jit(solution)/shard_map/ppermute | solution.py:335
  50.3 19.5 %collective-permute-start.18 = (s16[4,272,256]{2,1,0:T(8,128)(2,1)S(1)}, s16[4,272,256]{2,1,0:T(8,128)(2,1)S(1)}, u32[]{:S(2)}, u32[]{:S(2)}) collective-permute-start(s16[4,272,256]{2,1,0:T(8,128)(2,1)S(1)} %get-tuple-element.84), channel_id=1, source_target_pairs={{0,16},{8,24},{16,0},{24,8},{1,17},{9,25},{17,1},{25,9},{2,18},{10... | collective-permute-start | bytes 1671176 | tf_op jit(solution)/shard_map/ppermute | solution.py:335
  52.0 19.3 %collective-permute-start.17 = (s16[4,272,256]{2,1,0:T(8,128)(2,1)S(1)}, s16[4,272,256]{2,1,0:T(8,128)(2,1)S(1)}, u32[]{:S(2)}, u32[]{:S(2)}) collective-permute-start(s16[4,272,256]{2,1,0:T(8,128)(2,1)S(1)} %get-tuple-element.75), channel_id=1, source_target_pairs={{0,8},{8,0},{16,24},{24,16},{1,9},{9,1},{17,25},{25,17},{2,10},{10... | collective-permute-start | bytes 1671176 | tf_op jit(solution)/shard_map/ppermute | solution.py:335
  56.3 30.0 %collective-permute-start.23 = (s16[4,272,256]{2,1,0:T(8,128)(2,1)S(1)}, s16[4,272,256]{2,1,0:T(8,128)(2,1)S(1)}, u32[]{:S(2)}, u32[]{:S(2)}) collective-permute-start(s16[4,272,256]{2,1,0:T(8,128)(2,1)S(1)} %get-tuple-element.78), channel_id=1, source_target_pairs={{0,4},{1,5},{2,6},{3,7},{4,0},{5,1},{6,2},{7,3},{8,12},{9,13},{10,... | collective-permute-start | bytes 1671176 | tf_op jit(solution)/shard_map/ppermute | solution.py:338
  62.5 14.8 %collective-permute-start.20 = (s16[2,272,256]{2,1,0:T(8,128)(2,1)S(1)}, s16[2,272,256]{2,1,0:T(8,128)(2,1)S(1)}, u32[]{:S(2)}, u32[]{:S(2)}) collective-permute-start(s16[2,272,256]{2,1,0:T(8,128)(2,1)S(1)} %get-tuple-element.88), channel_id=1, source_target_pairs={{0,8},{8,0},{16,24},{24,16},{1,9},{9,1},{17,25},{25,17},{2,10},{10... | collective-permute-start | bytes 835592 | tf_op jit(solution)/shard_map/ppermute | solution.py:335
  64.5 12.9 %collective-permute-start.19 = (s16[2,272,256]{2,1,0:T(8,128)(2,1)S(1)}, s16[2,272,256]{2,1,0:T(8,128)(2,1)S(1)}, u32[]{:S(2)}, u32[]{:S(2)}) collective-permute-start(s16[2,272,256]{2,1,0:T(8,128)(2,1)S(1)} %get-tuple-element.82), channel_id=1, source_target_pairs={{0,16},{8,24},{16,0},{24,8},{1,17},{9,25},{17,1},{25,9},{2,18},{10... | collective-permute-start | bytes 835592 | tf_op jit(solution)/shard_map/ppermute | solution.py:335
  72.0 11.4 %collective-permute-start.22 = (s16[2,272,256]{2,1,0:T(8,128)(2,1)S(1)}, s16[2,272,256]{2,1,0:T(8,128)(2,1)S(1)}, u32[]{:S(2)}, u32[]{:S(2)}) collective-permute-start(s16[2,272,256]{2,1,0:T(8,128)(2,1)S(1)} %get-tuple-element.92), channel_id=1, source_target_pairs={{0,8},{8,0},{16,24},{24,16},{1,9},{9,1},{17,25},{25,17},{2,10},{10... | collective-permute-start | bytes 835592 | tf_op jit(solution)/shard_map/ppermute | solution.py:335
  73.4 10.0 %collective-permute-start.21 = (s16[2,272,256]{2,1,0:T(8,128)(2,1)S(1)}, s16[2,272,256]{2,1,0:T(8,128)(2,1)S(1)}, u32[]{:S(2)}, u32[]{:S(2)}) collective-permute-start(s16[2,272,256]{2,1,0:T(8,128)(2,1)S(1)} %get-tuple-element.86), channel_id=1, source_target_pairs={{0,16},{8,24},{16,0},{24,8},{1,17},{9,25},{17,1},{25,9},{2,18},{10... | collective-permute-start | bytes 835592 | tf_op jit(solution)/shard_map/ppermute | solution.py:335
  77.6 20.1 %collective-permute-start.27 = (s16[2,272,256]{2,1,0:T(8,128)(2,1)S(1)}, s16[2,272,256]{2,1,0:T(8,128)(2,1)S(1)}, u32[]{:S(2)}, u32[]{:S(2)}) collective-permute-start(s16[2,272,256]{2,1,0:T(8,128)(2,1)S(1)} %get-tuple-element.90), channel_id=1, source_target_pairs={{0,2},{1,3},{2,0},{3,1},{4,6},{5,7},{6,4},{7,5},{8,10},{9,11},{10,... | collective-permute-start | bytes 835592 | tf_op jit(solution)/shard_map/ppermute | solution.py:338
  90.9 12.7 %collective-permute-start.28 = (s16[2,272,256]{2,1,0:T(8,128)(2,1)S(1)}, s16[2,272,256]{2,1,0:T(8,128)(2,1)S(1)}, u32[]{:S(2)}, u32[]{:S(2)}) collective-permute-start(s16[2,272,256]{2,1,0:T(8,128)(2,1)S(1)} %get-tuple-element.94), channel_id=1, source_target_pairs={{0,2},{1,3},{2,0},{3,1},{4,6},{5,7},{6,4},{7,5},{8,10},{9,11},{10,... | collective-permute-start | bytes 835592 | tf_op jit(solution)/shard_map/ppermute | solution.py:338
  97.9 10.5 %collective-permute-start.29 = (s16[1,272,256]{2,1,0:T(8,128)(2,1)S(1)}, s16[1,272,256]{2,1,0:T(8,128)(2,1)S(1)}, u32[]{:S(2)}, u32[]{:S(2)}) collective-permute-start(s16[1,272,256]{2,1,0:T(8,128)(2,1)S(1)} %get-tuple-element.104), channel_id=1, source_target_pairs={{0,4},{1,5},{2,6},{3,7},{4,0},{5,1},{6,2},{7,3},{8,12},{9,13},{10,... | collective-permute-start | bytes 417800 | tf_op jit(solution)/shard_map/ppermute | solution.py:338
  100.1 10.3 %collective-permute-start.32 = (s16[272,256]{1,0:T(8,128)(2,1)S(1)}, s16[272,256]{1,0:T(8,128)(2,1)S(1)}, u32[]{:S(2)}, u32[]{:S(2)}) collective-permute-start(s16[272,256]{1,0:T(8,128)(2,1)S(1)} %finish_rows.1.refs_0_), channel_id=1, source_target_pairs={{0,24},{8,16},{16,8},{24,0},{1,25},{9,17},{17,9},{25,1},{2,26},{10... | collective-permute-start | bytes 417800 | tf_op jit(solution)/shard_map/ppermute | solution.py:335
  100.8 10.0 %collective-permute-start.31 = (s16[272,256]{1,0:T(8,128)(2,1)S(1)}, s16[272,256]{1,0:T(8,128)(2,1)S(1)}, u32[]{:S(2)}, u32[]{:S(2)}) collective-permute-start(s16[272,256]{1,0:T(8,128)(2,1)S(1)} %finish_rows.1.refs_0_), channel_id=1, source_target_pairs={{0,16},{8,24},{16,0},{24,8},{1,17},{9,25},{17,1},{25,9},{2,18},{10... | collective-permute-start | bytes 417800 | tf_op jit(solution)/shard_map/ppermute | solution.py:335
  102.1 9.9 %collective-permute-start.30 = (s16[272,256]{1,0:T(8,128)(2,1)S(1)}, s16[272,256]{1,0:T(8,128)(2,1)S(1)}, u32[]{:S(2)}, u32[]{:S(2)}) collective-permute-start(s16[272,256]{1,0:T(8,128)(2,1)S(1)} %finish_rows.1.refs_0_), channel_id=1, source_target_pairs={{0,8},{8,0},{16,24},{24,16},{1,9},{9,1},{17,25},{25,17},{2,10},{10... | collective-permute-start | bytes 417800 | tf_op jit(solution)/shard_map/ppermute | solution.py:335
  (17 other events, 122.4 us)

commit v4 on v3

--- a/solution.py
+++ b/solution.py
@@ -244,21 +244,19 @@
         keep[i] = jnp.where(odd == 1, value_b, value_a)
 
 
-def rows_kernel(order, recv, kept, send_1, send_2, send_3, keep):
-    side = kept.shape[1]
-    x, y, _, _ = here()
-    row = 2 * y + x
-    for d, send in enumerate((send_1, send_2, send_3), 1):
-        put_encoded(send, kept[row ^ d] + get_decoded(recv.at[row ^ d], side))
-    keep[...] = kept[row] + get_decoded(recv.at[row], side)
-
-
-def finish_rows_kernel(order, *refs):
-    *recvs, kept, out = refs
-    value = kept[...]
-    for recv in recvs:
-        value += get_decoded(recv, kept.shape[0])
-    put_encoded(out, value)
+def rows_kernel(order, recv, kept, send_a, send_b):
+    side, half = kept.shape[1], send_a.shape[0]
+    for i in range(2 * half):
+        put_encoded(
+            (send_a, send_b)[i // half].at[i % half], kept[i] + get_decoded(recv.at[i], side)
+        )
+
+
+def swap_kernel(order, own_a, own_b, recv_a, recv_b, send_a, send_b):
+    side = own_a.shape[1] - CODE_ROWS
+    for own, recv, send in ((own_a, recv_a, send_a), (own_b, recv_b, send_b)):
+        for i in range(own.shape[0]):
+            put_encoded(send.at[i], get_decoded(own.at[i], side) + get_decoded(recv.at[i], side))
 
 
 def line_kernel(order, recv, kept, send, keep):
@@ -280,13 +278,19 @@
     blocks, (out, rows, sems) = refs[:4], refs[-3:]
     side, width = rows.shape[1:]
     x, y, _, _ = here()
+    halves = len(blocks[0].shape) == 3
     copies = []
-    for d, block in enumerate(blocks):
-        rows[d] = get_decoded(block, side)
-        at = pl.multiple_of(((2 * y + x) ^ d) * side, side)
+    for i in range(4):
+        if halves:
+            own, recv = blocks[i // 2].at[i % 2], blocks[2 + i // 2].at[i % 2]
+            rows[i] = get_decoded(own, side) + get_decoded(recv, side)
+            at = i * side
+        else:
+            rows[i] = get_decoded(blocks[i], side)
+            at = pl.multiple_of(((2 * y + x) ^ i) * side, side)
         copies.append(
             pltpu.make_async_copy(
-                rows.at[d], out.at[pl.ds(at, side), pl.ds(chunk * width, width)], sems.at[d]
+                rows.at[i], out.at[pl.ds(at, side), pl.ds(chunk * width, width)], sems.at[i]
             )
         )
         copies[-1].start()
@@ -502,28 +506,26 @@
     *sent[2], keep[2] = plane(2)
     sent[1], keep[1] = owner(1)
     sent[2], keep[2] = owner(2)
-    *sends, keep_0 = call(
-        rows_kernel, "rows", [coded] * 3 + [plain], to_line(sent_0, 1), keep_0
-    )
-    (done_0,) = call(
-        finish_rows_kernel,
-        "finish_rows",
-        [coded],
-        *[to_grp(v, d) for d, v in enumerate(sends, 1)],
-        keep_0,
-    )
-
-    for j in (1, 2):
-        sent[j], keep[j] = call(
+    pair_of = [stack_of(2, coded)] * 2
+    own_a, own_b = call(rows_kernel, "rows", pair_of, to_line(sent_0, 1), keep_0)
+
+    def line(j):
+        return call(
             line_kernel,
             "line",
             [stack_of(1, coded), stack_of(1, plain)],
             to_line(sent[j], 0),
             keep[j],
         )
+
+    sent[1], keep[1] = line(1)
+    sent[2], keep[2] = line(2)
+    own_a, own_b = call(
+        swap_kernel, "swap", pair_of, own_a, own_b, to_grp(own_a, 1), to_grp(own_b, 2)
+    )
     (done_1,) = call(finish_kernel, "finish", [coded], to_line(sent[1], 1), keep[1])
-    result = spread(0, gathered(done_0), None)
     (done_2,) = call(finish_kernel, "finish", [coded], to_line(sent[2], 1), keep[2])
+    result = spread(0, [own_a, own_b, to_grp(own_a, 2), to_grp(own_b, 1)], None)
     result = spread(1, gathered(done_1), result)
     return spread(2, gathered(done_2), result)
 

time: 124 us -> 123 us (level)
  starting transfers between devices: 57 us -> 38.8 us
  waiting for transfers between devices: 41 us -> 54 us
  Pallas kernels: 23.5 us -> 28.1 us
    ppermute x6, starting transfers between devices: 17.5 us -> 8.49 us  [to_line(): return lax.ppermute(v, 'wide', [(i, i ^ 2 << b) for i in range(wide_count)])]
    ppermute x6, waiting for transfers between devices: 9.83 us -> 18.1 us  [to_line(): return lax.ppermute(v, 'wide', [(i, i ^ 2 << b) for i in range(wide_count)])]
    ppermute x27 -> x25, starting transfers between devices: 35.3 us -> 29.2 us  [to_grp(): return lax.ppermute(v, 'grp', [(i, i ^ d) for i in range(4)])]
    ppermute x27 -> x25, waiting for transfers between devices: 27.3 us -> 31.9 us  [to_grp(): return lax.ppermute(v, 'grp', [(i, i ^ d) for i in range(4)])]
    pallas_call x21, Pallas kernels: 23.5 us -> 28.1 us  [call(): pl.pallas_call(body, in_specs=more.pop('in_specs', in_any(1) + in_smem(sm...]
    ppermute x7, starting transfers between devices: 4.25 us -> 1.1 us  [to_core(): return lax.ppermute(v, 'wide', [(i, i ^ 1) for i in range(wide_count)])]
  transfers between devices with their start and end apart: 40 -> 38, of which waited for: 19 -> 20; matrix products, arithmetic and copies ran while one was open for 2% -> 2% of each run, Pallas kernels for 18% -> 22%
where the time goes in v4:
time: 123 us
  waiting for transfers between devices  54 us (44%)
  starting transfers between devices  38.8 us (32%)
  Pallas kernels  28.1 us (23%)
    ppermute x25, waiting for transfers between devices, to_grp(): return lax.ppermute(v, 'grp', [(i, i ^ d) for i in range(4)])  31.9 us
    ppermute x25, starting transfers between devices, to_grp(): return lax.ppermute(v, 'grp', [(i, i ^ d) for i in range(4)])  29.2 us
    pallas_call x21, Pallas kernels, call(): pl.pallas_call(body, in_specs=more.pop('in_specs', in_any(1) + in_smem(sm...  28.1 us
    ppermute x6, waiting for transfers between devices, to_line(): return lax.ppermute(v, 'wide', [(i, i ^ 2 << b) for i in range(wide_count)])  18.1 us
    ppermute x6, starting transfers between devices, to_line(): return lax.ppermute(v, 'wide', [(i, i ^ 2 << b) for i in range(wide_count)])  8.49 us
    ppermute x7, waiting for transfers between devices, to_core(): return lax.ppermute(v, 'wide', [(i, i ^ 1) for i in range(wide_count)])  3.95 us
  transfers between devices with their start and end apart: 38, of which 20 were waited for; matrix products, arithmetic and copies ran while one was open for 2% of the time, Pallas kernels for 22%

profile of v4, /device:TPU:0, one launch (start us, length us, event | category | flops | bytes accessed | tf_op | source)
XLA Modules:
  0.0 123.0 jit_solution(10451190235119976104)
XLA Ops:
  2.4 3.0 %collective-permute-start.2 = (bf16[512,256]{1,0:T(8,128)(2,1)S(1)}, bf16[512,256]{1,0:T(8,128)(2,1)S(1)}, u32[]{:S(2)}, u32[]{:S(2)}) collective-permute-start(bf16[512,256]{1,0:T(8,128)(2,1)S(1)} %get-tuple-element.116.refs_0_), channel_id=1, source_target_pairs={{0,8},{8,0},{16,24},{24,16},{1,9},{9,1},{17,25},{25,17},{2,10},{10... | collective-permute-start | bytes 786440 | tf_op jit(solution)/shard_map/ppermute | solution.py:339
  7.0 3.1 %collective-permute-done.sib_ref = s32[128]{0:T(128)S(1)} collective-permute-done((s32[128]{0:T(128)S(1)}, s32[128]{0:T(128)S(1)}, u32[]{:S(2)}, u32[]{:S(2)}) %collective-permute-start) | collective-permute-done | bytes 544 | tf_op jit(solution)/shard_map/ppermute | solution.py:336
  10.1 2.6 %collective-permute-start.5 = (bf16[512,256]{1,0:T(8,128)(2,1)S(1)}, bf16[512,256]{1,0:T(8,128)(2,1)S(1)}, u32[]{:S(2)}, u32[]{:S(2)}) collective-permute-start(bf16[512,256]{1,0:T(8,128)(2,1)S(1)} %get-tuple-element.65), channel_id=1, source_target_pairs={{0,16},{8,24},{16,0},{24,8},{1,17},{9,25},{17,1},{25,9},{2,18},{10... | collective-permute-start | bytes 786440 | tf_op jit(solution)/shard_map/ppermute | solution.py:339
  14.3 6.4 %hold.1 = (s32[1]{0:T(128)}, s32[104]{0:T(128)S(1)}, s32[104]{0:T(128)S(1)}, s32[104]{0:T(128)S(1)}, bf16[104,256,256]{2,1,0:T(8,128)(2,1)S(1)}) custom-call(s32[1]{0:T(128)} %constant.8.clone.1.order, s32[128]{0:T(128)S(1)} %pad_add_fusion.own_ref, s32[128]{0:T(128)S(1)} %collective-permute-done.sib_ref, bf16[48,256,256]{2,1,0:T(8,128)(2,1)} %own_tiles.1, ...), custom_call_target="tpu_custom_call" | custom-call | bytes 12583936 | tf_op jit(solution)/shard_map/hold/pallas_call | solution.py:373
  20.8 3.9 %collective-permute-done.5.refs_1_ = bf16[512,256]{1,0:T(8,128)(2,1)S(1)} collective-permute-done((bf16[512,256]{1,0:T(8,128)(2,1)S(1)}, bf16[512,256]{1,0:T(8,128)(2,1)S(1)}, u32[]{:S(2)}, u32[]{:S(2)}) %collective-permute-start.5) | collective-permute-done | bytes 262176 | tf_op jit(solution)/shard_map/ppermute | solution.py:339
  27.1 5.0 %products.3 = (s16[8,272,256]{2,1,0:T(8,128)(2,1)S(1)}, f32[17,256,256]{2,1,0:T(8,128)S(1)}) custom-call(s32[1]{0:T(128)} %constant.8.clone.1.order, s32[1]{0:T(128)} %get-tuple-element.67.count_ref, s32[104]{0:T(128)S(1)} %get-tuple-element.68.slot_ref, s32[104]{0:T(128)S(1)} %get-tuple-element.69.label_ref, ...), custom_call_target="tpu_custom_call" | custom-call | bytes 16778052 | tf_op jit(solution)/shard_map/products/pallas_call | solution.py:373
  32.0 2.1 %collective-permute-start.14 = (s16[8,272,256]{2,1,0:T(8,128)(2,1)S(1)}, s16[8,272,256]{2,1,0:T(8,128)(2,1)S(1)}, u32[]{:S(2)}, u32[]{:S(2)}) collective-permute-start(s16[8,272,256]{2,1,0:T(8,128)(2,1)S(1)} %get-tuple-element.70), channel_id=1, source_target_pairs={{0,2},{1,3},{2,0},{3,1},{4,6},{5,7},{6,4},{7,5},{8,10},{9,11},{10,... | collective-permute-start | bytes 3342344 | tf_op jit(solution)/shard_map/ppermute | solution.py:342
  34.2 5.0 %collective-permute-done.9.refs_2_ = bf16[1024,256]{1,0:T(8,128)(2,1)S(1)} collective-permute-done((bf16[1024,256]{1,0:T(8,128)(2,1)S(1)}, bf16[1024,256]{1,0:T(8,128)(2,1)S(1)}, u32[]{:S(2)}, u32[]{:S(2)}) %collective-permute-start.9) | collective-permute-done | bytes 524320 | tf_op jit(solution)/shard_map/ppermute | solution.py:339
  41.0 5.0 %products.4 = (s16[4,272,256]{2,1,0:T(8,128)(2,1)S(1)}, s16[4,272,256]{2,1,0:T(8,128)(2,1)S(1)}, f32[17,256,256]{2,1,0:T(8,128)S(1)}) custom-call(s32[1]{0:T(128)} %constant.8.clone.1.order, s32[1]{0:T(128)} %get-tuple-element.67.count_ref, s32[104]{0:T(128)S(1)} %get-tuple-element.72.slot_ref, s32[104]{0:T(128)S(1)} %get-tuple-element.69.label_ref, ...), custom_call_target="tpu_custom_call" | custom-call | bytes 17302340 | tf_op jit(solution)/shard_map/products/pallas_call | solution.py:373
  46.0 2.1 %collective-permute-start.16 = (s16[4,272,256]{2,1,0:T(8,128)(2,1)S(1)}, s16[4,272,256]{2,1,0:T(8,128)(2,1)S(1)}, u32[]{:S(2)}, u32[]{:S(2)}) collective-permute-start(s16[4,272,256]{2,1,0:T(8,128)(2,1)S(1)} %get-tuple-element.80), channel_id=1, source_target_pairs={{0,16},{8,24},{16,0},{24,8},{1,17},{9,25},{17,1},{25,9},{2,18},{10... | collective-permute-start | bytes 1671176 | tf_op jit(solution)/shard_map/ppermute | solution.py:339
  48.1 5.0 %products.5 = (s16[4,272,256]{2,1,0:T(8,128)(2,1)S(1)}, s16[4,272,256]{2,1,0:T(8,128)(2,1)S(1)}, f32[17,256,256]{2,1,0:T(8,128)S(1)}) custom-call(s32[1]{0:T(128)} %constant.8.clone.1.order, s32[1]{0:T(128)} %get-tuple-element.67.count_ref, s32[104]{0:T(128)S(1)} %get-tuple-element.72.slot_ref, s32[104]{0:T(128)S(1)} %get-tuple-element.69.label_ref, ...), custom_call_target="tpu_custom_call" | custom-call | bytes 17302340 | tf_op jit(solution)/shard_map/products/pallas_call | solution.py:373
  53.1 2.2 %collective-permute-start.18 = (s16[4,272,256]{2,1,0:T(8,128)(2,1)S(1)}, s16[4,272,256]{2,1,0:T(8,128)(2,1)S(1)}, u32[]{:S(2)}, u32[]{:S(2)}) collective-permute-start(s16[4,272,256]{2,1,0:T(8,128)(2,1)S(1)} %get-tuple-element.84), channel_id=1, source_target_pairs={{0,16},{8,24},{16,0},{24,8},{1,17},{9,25},{17,1},{25,9},{2,18},{10... | collective-permute-start | bytes 1671176 | tf_op jit(solution)/shard_map/ppermute | solution.py:339
  55.7 3.5 %collective-permute-done.14.recv = s16[8,272,256]{2,1,0:T(8,128)(2,1)S(1)} collective-permute-done((s16[8,272,256]{2,1,0:T(8,128)(2,1)S(1)}, s16[8,272,256]{2,1,0:T(8,128)(2,1)S(1)}, u32[]{:S(2)}, u32[]{:S(2)}) %collective-permute-start.14) | collective-permute-done | bytes 1114144 | tf_op jit(solution)/shard_map/ppermute | solution.py:342
  59.8 2.5 %collective-permute-start.23 = (s16[4,272,256]{2,1,0:T(8,128)(2,1)S(1)}, s16[4,272,256]{2,1,0:T(8,128)(2,1)S(1)}, u32[]{:S(2)}, u32[]{:S(2)}) collective-permute-start(s16[4,272,256]{2,1,0:T(8,128)(2,1)S(1)} %get-tuple-element.78), channel_id=1, source_target_pairs={{0,4},{1,5},{2,6},{3,7},{4,0},{5,1},{6,2},{7,3},{8,12},{9,13},{10,... | collective-permute-start | bytes 1671176 | tf_op jit(solution)/shard_map/ppermute | solution.py:342
  66.0 7.4 %collective-permute-done.18.recv_b = s16[4,272,256]{2,1,0:T(8,128)(2,1)S(1)} collective-permute-done((s16[4,272,256]{2,1,0:T(8,128)(2,1)S(1)}, s16[4,272,256]{2,1,0:T(8,128)(2,1)S(1)}, u32[]{:S(2)}, u32[]{:S(2)}) %collective-permute-start.18) | collective-permute-done | bytes 557088 | tf_op jit(solution)/shard_map/ppermute | solution.py:339
  73.4 2.2 %collective-permute-done.17.recv_a = s16[4,272,256]{2,1,0:T(8,128)(2,1)S(1)} collective-permute-done((s16[4,272,256]{2,1,0:T(8,128)(2,1)S(1)}, s16[4,272,256]{2,1,0:T(8,128)(2,1)S(1)}, u32[]{:S(2)}, u32[]{:S(2)}) %collective-permute-start.17) | collective-permute-done | bytes 557088 | tf_op jit(solution)/shard_map/ppermute | solution.py:339
  78.0 3.6 %collective-permute-done.20.recv_b = s16[2,272,256]{2,1,0:T(8,128)(2,1)S(1)} collective-permute-done((s16[2,272,256]{2,1,0:T(8,128)(2,1)S(1)}, s16[2,272,256]{2,1,0:T(8,128)(2,1)S(1)}, u32[]{:S(2)}, u32[]{:S(2)}) %collective-permute-start.20) | collective-permute-done | bytes 278560 | tf_op jit(solution)/shard_map/ppermute | solution.py:339
  82.5 3.4 %collective-permute-done.22.recv_b = s16[2,272,256]{2,1,0:T(8,128)(2,1)S(1)} collective-permute-done((s16[2,272,256]{2,1,0:T(8,128)(2,1)S(1)}, s16[2,272,256]{2,1,0:T(8,128)(2,1)S(1)}, u32[]{:S(2)}, u32[]{:S(2)}) %collective-permute-start.22) | collective-permute-done | bytes 278560 | tf_op jit(solution)/shard_map/ppermute | solution.py:339
  86.2 2.1 %collective-permute-start.25 = (s16[2,272,256]{2,1,0:T(8,128)(2,1)S(1)}, s16[2,272,256]{2,1,0:T(8,128)(2,1)S(1)}, u32[]{:S(2)}, u32[]{:S(2)}) collective-permute-start(s16[2,272,256]{2,1,0:T(8,128)(2,1)S(1)} %get-tuple-element.94), channel_id=1, source_target_pairs={{0,2},{1,3},{2,0},{3,1},{4,6},{5,7},{6,4},{7,5},{8,10},{9,11},{10,... | collective-permute-start | bytes 835592 | tf_op jit(solution)/shard_map/ppermute | solution.py:342
  89.6 3.5 %collective-permute-done.24.recv = s16[2,272,256]{2,1,0:T(8,128)(2,1)S(1)} collective-permute-done((s16[2,272,256]{2,1,0:T(8,128)(2,1)S(1)}, s16[2,272,256]{2,1,0:T(8,128)(2,1)S(1)}, u32[]{:S(2)}, u32[]{:S(2)}) %collective-permute-start.24) | collective-permute-done | bytes 278560 | tf_op jit(solution)/shard_map/ppermute | solution.py:342
  94.0 5.3 %collective-permute-done.25.recv = s16[2,272,256]{2,1,0:T(8,128)(2,1)S(1)} collective-permute-done((s16[2,272,256]{2,1,0:T(8,128)(2,1)S(1)}, s16[2,272,256]{2,1,0:T(8,128)(2,1)S(1)}, u32[]{:S(2)}, u32[]{:S(2)}) %collective-permute-start.25) | collective-permute-done | bytes 278560 | tf_op jit(solution)/shard_map/ppermute | solution.py:342
  105.4 5.6 %collective-permute-done.29.recv = s16[1,272,256]{2,1,0:T(8,128)(2,1)S(1)} collective-permute-done((s16[1,272,256]{2,1,0:T(8,128)(2,1)S(1)}, s16[1,272,256]{2,1,0:T(8,128)(2,1)S(1)}, u32[]{:S(2)}, u32[]{:S(2)}) %collective-permute-start.29) | collective-permute-done | bytes 139296 | tf_op jit(solution)/shard_map/ppermute | solution.py:342
  112.8 2.4 %collective-permute-start.37 = (s16[272,256]{1,0:T(8,128)(2,1)S(1)}, s16[272,256]{1,0:T(8,128)(2,1)S(1)}, u32[]{:S(2)}, u32[]{:S(2)}) collective-permute-start(s16[272,256]{1,0:T(8,128)(2,1)S(1)} %finish.3.refs_0_), channel_id=1, source_target_pairs={{0,24},{8,16},{16,8},{24,0},{1,25},{9,17},{17,9},{25,1},{2,26},{10... | collective-permute-start | bytes 417800 | tf_op jit(solution)/shard_map/ppermute | solution.py:339
  117.4 1.9 %collective-permute-done.33.refs_2_ = s16[272,256]{1,0:T(8,128)(2,1)S(1)} collective-permute-done((s16[272,256]{1,0:T(8,128)(2,1)S(1)}, s16[272,256]{1,0:T(8,128)(2,1)S(1)}, u32[]{:S(2)}, u32[]{:S(2)}) %collective-permute-start.33) | collective-permute-done | bytes 139296 | tf_op jit(solution)/shard_map/ppermute | solution.py:339
  (77 shorter events, 34.3 us)
Async XLA Ops:
  0.0 12.8 %collective-permute-start.1 = (bf16[48,256,256]{2,1,0:T(8,128)(2,1)}, bf16[48,256,256]{2,1,0:T(8,128)(2,1)}, u32[]{:S(2)}, u32[]{:S(2)}) collective-permute-start(bf16[48,256,256]{2,1,0:T(8,128)(2,1)} %own_tiles.1), channel_id=1, source_target_pairs={{0,1},{1,0},{2,3},{3,2},{4,5},{5,4},{6,7},{7,6},{8,9},{9,8},{10,11... | collective-permute-start | bytes 18874376 | tf_op jit(solution)/shard_map/ppermute | solution.py:336
  2.4 18.2 %collective-permute-start.2 = (bf16[512,256]{1,0:T(8,128)(2,1)S(1)}, bf16[512,256]{1,0:T(8,128)(2,1)S(1)}, u32[]{:S(2)}, u32[]{:S(2)}) collective-permute-start(bf16[512,256]{1,0:T(8,128)(2,1)S(1)} %get-tuple-element.116.refs_0_), channel_id=1, source_target_pairs={{0,8},{8,0},{16,24},{24,16},{1,9},{9,1},{17,25},{25,17},{2,10},{10... | collective-permute-start | bytes 786440 | tf_op jit(solution)/shard_map/ppermute | solution.py:339
  5.5 15.3 %collective-permute-start.3 = (bf16[512,256]{1,0:T(8,128)(2,1)S(1)}, bf16[512,256]{1,0:T(8,128)(2,1)S(1)}, u32[]{:S(2)}, u32[]{:S(2)}) collective-permute-start(bf16[512,256]{1,0:T(8,128)(2,1)S(1)} %get-tuple-element.115.refs_0_), channel_id=1, source_target_pairs={{0,16},{8,24},{16,0},{24,8},{1,17},{9,25},{17,1},{25,9},{2,18},{10... | collective-permute-start | bytes 786440 | tf_op jit(solution)/shard_map/ppermute | solution.py:339
  7.0 13.8 %collective-permute-start.6 = (bf16[512,256]{1,0:T(8,128)(2,1)S(1)}, bf16[512,256]{1,0:T(8,128)(2,1)S(1)}, u32[]{:S(2)}, u32[]{:S(2)}) collective-permute-start(bf16[512,256]{1,0:T(8,128)(2,1)S(1)} %get-tuple-element.65), channel_id=1, source_target_pairs={{0,24},{8,16},{16,8},{24,0},{1,25},{9,17},{17,9},{25,1},{2,26},{10... | collective-permute-start | bytes 786440 | tf_op jit(solution)/shard_map/ppermute | solution.py:339
  10.1 14.5 %collective-permute-start.5 = (bf16[512,256]{1,0:T(8,128)(2,1)S(1)}, bf16[512,256]{1,0:T(8,128)(2,1)S(1)}, u32[]{:S(2)}, u32[]{:S(2)}) collective-permute-start(bf16[512,256]{1,0:T(8,128)(2,1)S(1)} %get-tuple-element.65), channel_id=1, source_target_pairs={{0,16},{8,24},{16,0},{24,8},{1,17},{9,25},{17,1},{25,9},{2,18},{10... | collective-permute-start | bytes 786440 | tf_op jit(solution)/shard_map/ppermute | solution.py:339
  12.8 11.9 %collective-permute-start.4 = (bf16[512,256]{1,0:T(8,128)(2,1)S(1)}, bf16[512,256]{1,0:T(8,128)(2,1)S(1)}, u32[]{:S(2)}, u32[]{:S(2)}) collective-permute-start(bf16[512,256]{1,0:T(8,128)(2,1)S(1)} %get-tuple-element.65), channel_id=1, source_target_pairs={{0,8},{8,0},{16,24},{24,16},{1,9},{9,1},{17,25},{25,17},{2,10},{10... | collective-permute-start | bytes 786440 | tf_op jit(solution)/shard_map/ppermute | solution.py:339
  24.8 14.3 %collective-permute-start.9 = (bf16[1024,256]{1,0:T(8,128)(2,1)S(1)}, bf16[1024,256]{1,0:T(8,128)(2,1)S(1)}, u32[]{:S(2)}, u32[]{:S(2)}) collective-permute-start(bf16[1024,256]{1,0:T(8,128)(2,1)S(1)} %join.3.refs_0_), channel_id=1, source_target_pairs={{0,16},{8,24},{16,0},{24,8},{1,17},{9,25},{17,1},{25,9},{2,18},{10... | collective-permute-start | bytes 1572872 | tf_op jit(solution)/shard_map/ppermute | solution.py:339
  26.4 14.0 %collective-permute-start.12 = (bf16[1024,256]{1,0:T(8,128)(2,1)S(1)}, bf16[1024,256]{1,0:T(8,128)(2,1)S(1)}, u32[]{:S(2)}, u32[]{:S(2)}) collective-permute-start(bf16[1024,256]{1,0:T(8,128)(2,1)S(1)} %join.4.refs_0_), channel_id=1, source_target_pairs={{0,8},{8,0},{16,24},{24,16},{1,9},{9,1},{17,25},{25,17},{2,10},{10... | collective-permute-start | bytes 1572872 | tf_op jit(solution)/shard_map/ppermute | solution.py:339
  32.0 27.1 %collective-permute-start.14 = (s16[8,272,256]{2,1,0:T(8,128)(2,1)S(1)}, s16[8,272,256]{2,1,0:T(8,128)(2,1)S(1)}, u32[]{:S(2)}, u32[]{:S(2)}) collective-permute-start(s16[8,272,256]{2,1,0:T(8,128)(2,1)S(1)} %get-tuple-element.70), channel_id=1, source_target_pairs={{0,2},{1,3},{2,0},{3,1},{4,6},{5,7},{6,4},{7,5},{8,10},{9,11},{10,... | collective-permute-start | bytes 3342344 | tf_op jit(solution)/shard_map/ppermute | solution.py:342
  46.0 16.2 %collective-permute-start.16 = (s16[4,272,256]{2,1,0:T(8,128)(2,1)S(1)}, s16[4,272,256]{2,1,0:T(8,128)(2,1)S(1)}, u32[]{:S(2)}, u32[]{:S(2)}) collective-permute-start(s16[4,272,256]{2,1,0:T(8,128)(2,1)S(1)} %get-tuple-element.80), channel_id=1, source_target_pairs={{0,16},{8,24},{16,0},{24,8},{1,17},{9,25},{17,1},{25,9},{2,18},{10... | collective-permute-start | bytes 1671176 | tf_op jit(solution)/shard_map/ppermute | solution.py:339
  48.1 15.6 %collective-permute-start.15 = (s16[4,272,256]{2,1,0:T(8,128)(2,1)S(1)}, s16[4,272,256]{2,1,0:T(8,128)(2,1)S(1)}, u32[]{:S(2)}, u32[]{:S(2)}) collective-permute-start(s16[4,272,256]{2,1,0:T(8,128)(2,1)S(1)} %get-tuple-element.73), channel_id=1, source_target_pairs={{0,8},{8,0},{16,24},{24,16},{1,9},{9,1},{17,25},{25,17},{2,10},{10... | collective-permute-start | bytes 1671176 | tf_op jit(solution)/shard_map/ppermute | solution.py:339
  53.1 20.3 %collective-permute-start.18 = (s16[4,272,256]{2,1,0:T(8,128)(2,1)S(1)}, s16[4,272,256]{2,1,0:T(8,128)(2,1)S(1)}, u32[]{:S(2)}, u32[]{:S(2)}) collective-permute-start(s16[4,272,256]{2,1,0:T(8,128)(2,1)S(1)} %get-tuple-element.84), channel_id=1, source_target_pairs={{0,16},{8,24},{16,0},{24,8},{1,17},{9,25},{17,1},{25,9},{2,18},{10... | collective-permute-start | bytes 1671176 | tf_op jit(solution)/shard_map/ppermute | solution.py:339
  55.3 20.2 %collective-permute-start.17 = (s16[4,272,256]{2,1,0:T(8,128)(2,1)S(1)}, s16[4,272,256]{2,1,0:T(8,128)(2,1)S(1)}, u32[]{:S(2)}, u32[]{:S(2)}) collective-permute-start(s16[4,272,256]{2,1,0:T(8,128)(2,1)S(1)} %get-tuple-element.75), channel_id=1, source_target_pairs={{0,8},{8,0},{16,24},{24,16},{1,9},{9,1},{17,25},{25,17},{2,10},{10... | collective-permute-start | bytes 1671176 | tf_op jit(solution)/shard_map/ppermute | solution.py:339
  59.8 28.5 %collective-permute-start.23 = (s16[4,272,256]{2,1,0:T(8,128)(2,1)S(1)}, s16[4,272,256]{2,1,0:T(8,128)(2,1)S(1)}, u32[]{:S(2)}, u32[]{:S(2)}) collective-permute-start(s16[4,272,256]{2,1,0:T(8,128)(2,1)S(1)} %get-tuple-element.78), channel_id=1, source_target_pairs={{0,4},{1,5},{2,6},{3,7},{4,0},{5,1},{6,2},{7,3},{8,12},{9,13},{10,... | collective-permute-start | bytes 1671176 | tf_op jit(solution)/shard_map/ppermute | solution.py:342
  64.2 17.3 %collective-permute-start.19 = (s16[2,272,256]{2,1,0:T(8,128)(2,1)S(1)}, s16[2,272,256]{2,1,0:T(8,128)(2,1)S(1)}, u32[]{:S(2)}, u32[]{:S(2)}) collective-permute-start(s16[2,272,256]{2,1,0:T(8,128)(2,1)S(1)} %get-tuple-element.82), channel_id=1, source_target_pairs={{0,16},{8,24},{16,0},{24,8},{1,17},{9,25},{17,1},{25,9},{2,18},{10... | collective-permute-start | bytes 835592 | tf_op jit(solution)/shard_map/ppermute | solution.py:339
  64.3 17.2 %collective-permute-start.20 = (s16[2,272,256]{2,1,0:T(8,128)(2,1)S(1)}, s16[2,272,256]{2,1,0:T(8,128)(2,1)S(1)}, u32[]{:S(2)}, u32[]{:S(2)}) collective-permute-start(s16[2,272,256]{2,1,0:T(8,128)(2,1)S(1)} %get-tuple-element.88), channel_id=1, source_target_pairs={{0,8},{8,0},{16,24},{24,16},{1,9},{9,1},{17,25},{25,17},{2,10},{10... | collective-permute-start | bytes 835592 | tf_op jit(solution)/shard_map/ppermute | solution.py:339
  81.8 11.2 %collective-permute-start.24 = (s16[2,272,256]{2,1,0:T(8,128)(2,1)S(1)}, s16[2,272,256]{2,1,0:T(8,128)(2,1)S(1)}, u32[]{:S(2)}, u32[]{:S(2)}) collective-permute-start(s16[2,272,256]{2,1,0:T(8,128)(2,1)S(1)} %get-tuple-element.90), channel_id=1, source_target_pairs={{0,2},{1,3},{2,0},{3,1},{4,6},{5,7},{6,4},{7,5},{8,10},{9,11},{10,... | collective-permute-start | bytes 835592 | tf_op jit(solution)/shard_map/ppermute | solution.py:342
  86.2 13.1 %collective-permute-start.25 = (s16[2,272,256]{2,1,0:T(8,128)(2,1)S(1)}, s16[2,272,256]{2,1,0:T(8,128)(2,1)S(1)}, u32[]{:S(2)}, u32[]{:S(2)}) collective-permute-start(s16[2,272,256]{2,1,0:T(8,128)(2,1)S(1)} %get-tuple-element.94), channel_id=1, source_target_pairs={{0,2},{1,3},{2,0},{3,1},{4,6},{5,7},{6,4},{7,5},{8,10},{9,11},{10,... | collective-permute-start | bytes 835592 | tf_op jit(solution)/shard_map/ppermute | solution.py:342
  88.6 10.8 %collective-permute-start.27 = (s16[2,272,256]{2,1,0:T(8,128)(2,1)S(1)}, s16[2,272,256]{2,1,0:T(8,128)(2,1)S(1)}, u32[]{:S(2)}, u32[]{:S(2)}) collective-permute-start(s16[2,272,256]{2,1,0:T(8,128)(2,1)S(1)} %get-tuple-element.105.own_b), channel_id=1, source_target_pairs={{0,16},{8,24},{16,0},{24,8},{1,17},{9,25},{17,1},{25,9},{2,18},{10... | collective-permute-start | bytes 835592 | tf_op jit(solution)/shard_map/ppermute | solution.py:339
  89.0 10.4 %collective-permute-start.26 = (s16[2,272,256]{2,1,0:T(8,128)(2,1)S(1)}, s16[2,272,256]{2,1,0:T(8,128)(2,1)S(1)}, u32[]{:S(2)}, u32[]{:S(2)}) collective-permute-start(s16[2,272,256]{2,1,0:T(8,128)(2,1)S(1)} %get-tuple-element.97.own_a), channel_id=1, source_target_pairs={{0,8},{8,0},{16,24},{24,16},{1,9},{9,1},{17,25},{25,17},{2,10},{10... | collective-permute-start | bytes 835592 | tf_op jit(solution)/shard_map/ppermute | solution.py:339
  99.9 15.3 %collective-permute-start.31 = (s16[2,272,256]{2,1,0:T(8,128)(2,1)S(1)}, s16[2,272,256]{2,1,0:T(8,128)(2,1)S(1)}, u32[]{:S(2)}, u32[]{:S(2)}) collective-permute-start(s16[2,272,256]{2,1,0:T(8,128)(2,1)S(1)} %get-tuple-element.112.refs_1_), channel_id=1, source_target_pairs={{0,8},{8,0},{16,24},{24,16},{1,9},{9,1},{17,25},{25,17},{2,10},{10... | collective-permute-start | bytes 835592 | tf_op jit(solution)/shard_map/ppermute | solution.py:339
  101.7 13.8 %collective-permute-start.30 = (s16[2,272,256]{2,1,0:T(8,128)(2,1)S(1)}, s16[2,272,256]{2,1,0:T(8,128)(2,1)S(1)}, u32[]{:S(2)}, u32[]{:S(2)}) collective-permute-start(s16[2,272,256]{2,1,0:T(8,128)(2,1)S(1)} %get-tuple-element.106.refs_0_), channel_id=1, source_target_pairs={{0,16},{8,24},{16,0},{24,8},{1,17},{9,25},{17,1},{25,9},{2,18},{10... | collective-permute-start | bytes 835592 | tf_op jit(solution)/shard_map/ppermute | solution.py:339
  102.8 10.0 %collective-permute-start.34 = (s16[272,256]{1,0:T(8,128)(2,1)S(1)}, s16[272,256]{1,0:T(8,128)(2,1)S(1)}, u32[]{:S(2)}, u32[]{:S(2)}) collective-permute-start(s16[272,256]{1,0:T(8,128)(2,1)S(1)} %finish.2.refs_0_), channel_id=1, source_target_pairs={{0,24},{8,16},{16,8},{24,0},{1,25},{9,17},{17,9},{25,1},{2,26},{10... | collective-permute-start | bytes 417800 | tf_op jit(solution)/shard_map/ppermute | solution.py:339
  104.2 15.1 %collective-permute-start.33 = (s16[272,256]{1,0:T(8,128)(2,1)S(1)}, s16[272,256]{1,0:T(8,128)(2,1)S(1)}, u32[]{:S(2)}, u32[]{:S(2)}) collective-permute-start(s16[272,256]{1,0:T(8,128)(2,1)S(1)} %finish.2.refs_0_), channel_id=1, source_target_pairs={{0,16},{8,24},{16,0},{24,8},{1,17},{9,25},{17,1},{25,9},{2,18},{10... | collective-permute-start | bytes 417800 | tf_op jit(solution)/shard_map/ppermute | solution.py:339
  (15 other events, 109.6 us)
